TPU v7x, 256 devices: a whole 4x4x8 slice. The times are simulated.
256 devices in a mesh: section: 8 (over x, core), ep: 32 (over z, y).
Axes of the slice: x: 4, y: 4, z: 8, core: 2. Of those that a mesh axis runs over, the one named last changes fastest.
Arguments:
- spans: bfloat16 [8, 256, 3584], P(None, 'ep'), may hold values from -6 to 6
- attn_gain: float32 [8, 3584], P('section'), may hold values from 0.25 to 1.75
- kv_gain: float32 [8, 512], P('section'), may hold values from 0.25 to 1.75
- moe_gain: float32 [8, 3584], P('section'), may hold values from 0.25 to 1.75
- w_latent: bfloat16 [8, 3584, 576], P('section', 'ep'), may hold values from -0.09375 to 0.09375
- w_gate: bfloat16 [8, 3584, 16384], P('section', None, 'ep'), may hold values from -0.09375 to 0.09375
- w_up: bfloat16 [8, 3584, 16384], P('section', None, 'ep'), may hold values from -0.09375 to 0.09375
- w_down: bfloat16 [8, 16384, 3584], P('section', 'ep'), may hold values from -0.125 to 0.125
- expert_ids: int32 [8, 8, 256, 2], P('section'), may hold values from 0 to 7, all different within a row; in each aligned block of 8 rows (0 to 7, 8 to 15, ..., all dimensions but the last counted through in order) at most 4 rows name the same one
- gate_vals: float32 [8, 8, 256, 2], P('section', None, 'ep'), may hold values from 0.2 to 1
- owner_map: int32 [8, 8, 64], P('section'), may hold values from 0 to 63, each once within a row
- offsets: int32 [8], replicated, may hold values from 0 to 130816
Outputs:
- states: bfloat16 [8, 256, 3584], P('section', 'ep')
- kv_cache: bfloat16 [8, 8, 256, 576], P('section', None, 'ep')
Inputs may be any that keep to these rules, and one draw needn't show every extreme that they name: `expert_ids`: each token's 2 ids are different. In each aligned block of 8 tokens of one span and layer (the rows of one device), no expert is picked by more than 4 tokens, a bound that some block reaches. `owner_map`: each row of 64 entries is a permutation.
All inputs are finite; a program needn't handle non-finite values.
Results may differ from a plain program's by a relative error of at most 0.029.
Values may be sent and summed in bfloat16 or wider, within the bound.
No kernel may reach another device: no remote copies, remote signals or barrier semaphores. Data moves between devices by JAX's collectives and lax.ppermute only.
A program may use at most 64 MiB of HBM per device.

v0:
```python
import jax
import jax.numpy as jnp
from jax import lax
from jax.sharding import PartitionSpec as P

LAT = 512
EXP_SPLIT = 4
TOPK = 2
KVBLK = 4


eps = 1e-06


def shifted(block, axis, distance):
    devices = range(lax.axis_size(axis))
    route = [(i - distance, i) for i in devices if i - distance in devices]
    return lax.ppermute(block, axis, route)


def rms_scale(values, gain_vec):
    values = values.astype(jnp.float32)
    return values * lax.rsqrt(jnp.mean(values * values, axis=-1, keepdims=True) + eps) * gain_vec


def rotate_pairs(rope_part, positions):
    half_dim = rope_part.shape[-1] // 2
    frequency = 10000.0 ** (-jnp.arange(half_dim, dtype=jnp.float32) / half_dim)
    angles = positions.astype(jnp.float32)[:, None] * frequency[None, :]
    cosine = jnp.cos(angles)
    sine_part = jnp.sin(angles)
    first_half = rope_part[:, :half_dim]
    second = rope_part[:, half_dim:]
    return jnp.concatenate(
        [first_half * cosine - second * sine_part, second * cosine + first_half * sine_part], axis=1
    )


def latent_rows(latent, gain_vec, positions):
    compressed = rms_scale(latent[:, :LAT], gain_vec)
    rotated = rotate_pairs(latent[:, LAT:], positions)
    return jnp.concatenate([compressed, rotated], axis=1).astype(jnp.bfloat16)


def packing(route_ids, expert_list, capacity):
    matches = route_ids[:, :, None, :] == expert_list[None, None, :, None]
    picked = jnp.any(matches, axis=3).astype(jnp.int32)
    slot_rank = jnp.cumsum(picked, axis=1) - 1
    slot_ids = jnp.arange(capacity, dtype=jnp.int32)
    slot_table = (slot_rank[..., None] == slot_ids) & (picked[..., None] > 0)
    return jnp.transpose(slot_table, (0, 2, 3, 1))


def expert_slice(token_rows, local_gate, local_up, local_down):
    gate_proj = jnp.einsum(
        "smd,dh->smh", token_rows, local_gate, preferred_element_type=jnp.float32
    )
    up_proj = jnp.einsum("smd,dh->smh", token_rows, local_up, preferred_element_type=jnp.float32)
    hidden = (jax.nn.silu(gate_proj) * up_proj).astype(jnp.bfloat16)
    return jnp.einsum("smh,hd->smd", hidden, local_down, preferred_element_type=jnp.float32).astype(
        jnp.bfloat16
    )


def body(
    spans,
    attn_gain,
    kv_gain,
    moe_gain,
    w_latent,
    w_gate,
    w_up,
    w_down,
    expert_ids,
    gate_vals,
    owner_map,
    offsets,
):
    section_id = lax.axis_index("section")
    member = lax.axis_index("ep")
    n_members = lax.axis_size("ep")
    n_sections = lax.axis_size("section")
    n_spans = spans.shape[0]
    span_dev = spans.shape[1]
    model_width = spans.shape[2]
    kv_width = w_latent.shape[2]
    experts = n_members // EXP_SPLIT
    capacity = min(span_dev, 2 * span_dev * TOPK // experts)
    per_owner = span_dev // KVBLK
    all_experts = jnp.arange(experts, dtype=jnp.int32)
    my_expert = member // EXP_SPLIT
    local_gate = w_gate[0]
    local_up = w_up[0]
    local_down = w_down[0]
    latent_full = lax.all_gather(w_latent[0], "ep", axis=0, tiled=True)

    def project(normed):
        return jnp.dot(normed, latent_full, preferred_element_type=jnp.float32)

    def send_back(partial_value):
        return lax.all_to_all(partial_value, "ep", split_axis=0, concat_axis=0, tiled=True)

    def expert_work(token_rows):
        return send_back(expert_slice(token_rows, local_gate, local_up, local_down))

    def layer_tick(tick_step, layer_in, kv_store):
        span_id = tick_step - section_id
        is_live = span_id >= 0
        span_slot = jnp.clip(span_id, 0, n_spans - 1)
        entering = lax.dynamic_index_in_dim(
            spans, jnp.minimum(tick_step, n_spans - 1), 0, keepdims=False
        )
        tokens = jnp.where(section_id == 0, entering, layer_in)
        normed_kv = rms_scale(tokens, attn_gain[0]).astype(jnp.bfloat16)
        latent = project(normed_kv)
        positions = offsets[span_slot] + member * span_dev + jnp.arange(span_dev, dtype=jnp.int32)
        kv_rows = jnp.where(
            is_live,
            latent_rows(latent, kv_gain[0], positions),
            jnp.zeros((span_dev, kv_width), jnp.bfloat16),
        )
        current = lax.dynamic_index_in_dim(kv_store, span_slot, 0, keepdims=False)
        gathered = lax.all_gather(kv_rows, "ep", axis=0, tiled=True)
        block_order = lax.dynamic_index_in_dim(owner_map[0], span_slot, 0, keepdims=False)
        owned_ids = lax.dynamic_slice_in_dim(block_order, member * per_owner, per_owner, 0)
        blocks = gathered.reshape(-1, KVBLK, kv_width)
        my_blocks = jnp.take(blocks, owned_ids, axis=0).reshape(span_dev, kv_width)
        kv_store = lax.dynamic_update_index_in_dim(
            kv_store, jnp.where(is_live, my_blocks, current), span_slot, 0
        )
        normed_moe = rms_scale(tokens, moe_gain[0]).astype(jnp.bfloat16)
        span_ids = lax.dynamic_index_in_dim(expert_ids[0], span_slot, 0, keepdims=False)
        own_ids = lax.dynamic_slice_in_dim(span_ids, member * span_dev, span_dev, 0)
        own_table = packing(own_ids[None], all_experts, capacity)[0]
        everything = lax.all_gather(normed_moe, "ep", axis=0, tiled=True)
        mine_table = packing(span_ids.reshape(n_members, span_dev, -1), my_expert[None], capacity)[
            :, 0
        ]
        selected = jnp.einsum(
            "scr,srd->scd",
            mine_table.astype(jnp.bfloat16),
            everything.reshape(n_members, span_dev, model_width),
            preferred_element_type=jnp.float32,
        ).astype(jnp.bfloat16)
        returned = expert_work(selected)
        gate_rows = lax.dynamic_index_in_dim(gate_vals[0], span_slot, 0, keepdims=False)
        gate_for = jnp.sum(
            jnp.where(
                own_ids[:, :, None] == all_experts[None, None, :], gate_rows[:, :, None], 0.0
            ),
            axis=1,
        )
        weighting = own_table.astype(jnp.float32) * jnp.transpose(gate_for)[:, None, :]
        grouped = returned.reshape(experts, EXP_SPLIT, capacity, model_width).astype(jnp.float32)
        moe_sum = jnp.einsum("ecr,ejcd->rd", weighting, grouped, precision=lax.Precision.HIGHEST)
        layer_out = (tokens.astype(jnp.float32) + moe_sum).astype(jnp.bfloat16)
        return (layer_out, kv_store)

    def advance(tick_step, state_pair):
        layer_out, kv_store = layer_tick(tick_step, state_pair[0], state_pair[1])
        return (shifted(layer_out, "section", 1), kv_store)

    initial = (
        jnp.zeros((span_dev, model_width), jnp.bfloat16),
        jnp.zeros((n_spans, span_dev, kv_width), jnp.bfloat16),
    )
    layer_in, kv_store = lax.fori_loop(0, n_sections - 1, advance, initial)
    layer_out, kv_store = layer_tick(n_sections - 1, layer_in, kv_store)
    return (layer_out[None], kv_store[None])


def solution(mesh):
    in_specs = (
        P(None, "ep", None),
        P("section", None),
        P("section", None),
        P("section", None),
        P("section", "ep", None),
        P("section", None, "ep"),
        P("section", None, "ep"),
        P("section", "ep", None),
        P("section", None, None, None),
        P("section", None, "ep", None),
        P("section", None, None),
        P(),
    )
    out_specs = (P("section", "ep", None), P("section", None, "ep", None))
    return jax.shard_map(body, mesh=mesh, in_specs=in_specs, out_specs=out_specs, check_vma=False)
```

profile of v0, /device:TPU:8, one launch (start us, length us, event | category | flops | bytes accessed | tf_op | source)
XLA Modules:
  0.0 1431.0 jit_solution(18439594347173057534)
XLA Ops:
  8.7 86.7 %all-gather.7.cloned.1.call-done = bf16[1,3584,576]{2,1,0:T(8,128)(2,1)} async-done(((bf16[1,112,576]{2,1,0:T(8,128)(2,1)}), bf16[1,3584,576]{2,1,0:T(8,128)(2,1)}) %all-gather.7.cloned.1.call-update) | async-done | bytes 4128784 | tf_op jit(solution)/shard_map/all_gather | solution.py:95
  95.4 1164.7 %while.20 = (s32[]{:T(128)}, bf16[8,3584]{1,0:T(8,128)(2,1)S(1)}, bf16[8,8,576]{2,1,0:T(8,128)(2,1)S(1)}, pred[]{:T(512)}, bf16[8,8,3584]{2,1,0:T(8,128)(2,1)}, ...) while((s32[]{:T(128)}, bf16[8,3584]{1,0:T(8,128)(2,1)S(1)}, ...), condition=%wide.region_9.11_spmd.clone.clone, body=%wide.region_0.10_spmd.clone.clone.sunk | while | flops 1463282432 | bytes 35133292 | solution.py:167
  105.8 68.5 %all-gather.9.cloned.1.call-done = bf16[256,3584]{1,0:T(8,128)(2,1)} async-done(((bf16[8,3584]{1,0:T(8,128)(2,1)}), bf16[256,3584]{1,0:T(8,128)(2,1)}) %all-gather.9.cloned.1.call-update) | async-done | bytes 1835024 | tf_op jit(solution)/shard_map/while/body/eval_jaxpr/all_gather | solution.py:135
  179.1 4.4 convolution_convert_fusion.7
  185.2 7.4 all-to-all-start
  193.0 58.9 %all_gather.41 = bf16[256,576]{1,0:T(8,128)(2,1)S(1)} all-gather(bf16[8,576]{1,0:T(8,128)(2,1)S(1)} %maximum_select_fusion.3), channel_id=1, replica_groups=mesh['section'=8,'ep'=32] {'ep'}, dimensions={0}, use_global_device_ids=true | all-gather | bytes 304128 | tf_op jit(solution)/shard_map/while/body/eval_jaxpr/all_gather | solution.py:123
  268.0 73.5 %all-gather.9.cloned.1.call-done = bf16[256,3584]{1,0:T(8,128)(2,1)} async-done(((bf16[8,3584]{1,0:T(8,128)(2,1)}), bf16[256,3584]{1,0:T(8,128)(2,1)}) %all-gather.9.cloned.1.call-update) | async-done | bytes 1835024 | tf_op jit(solution)/shard_map/while/body/eval_jaxpr/all_gather | solution.py:135
  346.4 4.4 convolution_convert_fusion.7
  352.4 7.4 all-to-all-start
  360.2 58.9 %all_gather.41 = bf16[256,576]{1,0:T(8,128)(2,1)S(1)} all-gather(bf16[8,576]{1,0:T(8,128)(2,1)S(1)} %maximum_select_fusion.3), channel_id=1, replica_groups=mesh['section'=8,'ep'=32] {'ep'}, dimensions={0}, use_global_device_ids=true | all-gather | bytes 304128 | tf_op jit(solution)/shard_map/while/body/eval_jaxpr/all_gather | solution.py:123
  435.2 73.2 %all-gather.9.cloned.1.call-done = bf16[256,3584]{1,0:T(8,128)(2,1)} async-done(((bf16[8,3584]{1,0:T(8,128)(2,1)}), bf16[256,3584]{1,0:T(8,128)(2,1)}) %all-gather.9.cloned.1.call-update) | async-done | bytes 1835024 | tf_op jit(solution)/shard_map/while/body/eval_jaxpr/all_gather | solution.py:135
  513.3 4.4 convolution_convert_fusion.7
  519.3 7.4 all-to-all-start
  527.1 58.9 %all_gather.41 = bf16[256,576]{1,0:T(8,128)(2,1)S(1)} all-gather(bf16[8,576]{1,0:T(8,128)(2,1)S(1)} %maximum_select_fusion.3), channel_id=1, replica_groups=mesh['section'=8,'ep'=32] {'ep'}, dimensions={0}, use_global_device_ids=true | all-gather | bytes 304128 | tf_op jit(solution)/shard_map/while/body/eval_jaxpr/all_gather | solution.py:123
  602.1 73.2 %all-gather.9.cloned.1.call-done = bf16[256,3584]{1,0:T(8,128)(2,1)} async-done(((bf16[8,3584]{1,0:T(8,128)(2,1)}), bf16[256,3584]{1,0:T(8,128)(2,1)}) %all-gather.9.cloned.1.call-update) | async-done | bytes 1835024 | tf_op jit(solution)/shard_map/while/body/eval_jaxpr/all_gather | solution.py:135
  680.1 4.4 convolution_convert_fusion.7
  686.2 7.4 all-to-all-start
  694.0 58.9 %all_gather.41 = bf16[256,576]{1,0:T(8,128)(2,1)S(1)} all-gather(bf16[8,576]{1,0:T(8,128)(2,1)S(1)} %maximum_select_fusion.3), channel_id=1, replica_groups=mesh['section'=8,'ep'=32] {'ep'}, dimensions={0}, use_global_device_ids=true | all-gather | bytes 304128 | tf_op jit(solution)/shard_map/while/body/eval_jaxpr/all_gather | solution.py:123
  769.0 73.2 %all-gather.9.cloned.1.call-done = bf16[256,3584]{1,0:T(8,128)(2,1)} async-done(((bf16[8,3584]{1,0:T(8,128)(2,1)}), bf16[256,3584]{1,0:T(8,128)(2,1)}) %all-gather.9.cloned.1.call-update) | async-done | bytes 1835024 | tf_op jit(solution)/shard_map/while/body/eval_jaxpr/all_gather | solution.py:135
  853.1 7.4 all-to-all-start
  860.9 58.9 %all_gather.41 = bf16[256,576]{1,0:T(8,128)(2,1)S(1)} all-gather(bf16[8,576]{1,0:T(8,128)(2,1)S(1)} %maximum_select_fusion.3), channel_id=1, replica_groups=mesh['section'=8,'ep'=32] {'ep'}, dimensions={0}, use_global_device_ids=true | all-gather | bytes 304128 | tf_op jit(solution)/shard_map/while/body/eval_jaxpr/all_gather | solution.py:123
  935.9 73.5 %all-gather.9.cloned.1.call-done = bf16[256,3584]{1,0:T(8,128)(2,1)} async-done(((bf16[8,3584]{1,0:T(8,128)(2,1)}), bf16[256,3584]{1,0:T(8,128)(2,1)}) %all-gather.9.cloned.1.call-update) | async-done | bytes 1835024 | tf_op jit(solution)/shard_map/while/body/eval_jaxpr/all_gather | solution.py:135
  1014.3 4.4 convolution_convert_fusion.7
  1020.3 7.4 all-to-all-start
  1028.1 58.9 %all_gather.41 = bf16[256,576]{1,0:T(8,128)(2,1)S(1)} all-gather(bf16[8,576]{1,0:T(8,128)(2,1)S(1)} %maximum_select_fusion.3), channel_id=1, replica_groups=mesh['section'=8,'ep'=32] {'ep'}, dimensions={0}, use_global_device_ids=true | all-gather | bytes 304128 | tf_op jit(solution)/shard_map/while/body/eval_jaxpr/all_gather | solution.py:123
  1103.1 73.5 %all-gather.9.cloned.1.call-done = bf16[256,3584]{1,0:T(8,128)(2,1)} async-done(((bf16[8,3584]{1,0:T(8,128)(2,1)}), bf16[256,3584]{1,0:T(8,128)(2,1)}) %all-gather.9.cloned.1.call-update) | async-done | bytes 1835024 | tf_op jit(solution)/shard_map/while/body/eval_jaxpr/all_gather | solution.py:135
  1181.5 4.4 convolution_convert_fusion.7
  1187.6 7.4 all-to-all-start
  1195.3 58.9 %all_gather.41 = bf16[256,576]{1,0:T(8,128)(2,1)S(1)} all-gather(bf16[8,576]{1,0:T(8,128)(2,1)S(1)} %maximum_select_fusion.3), channel_id=1, replica_groups=mesh['section'=8,'ep'=32] {'ep'}, dimensions={0}, use_global_device_ids=true | all-gather | bytes 304128 | tf_op jit(solution)/shard_map/while/body/eval_jaxpr/all_gather | solution.py:123
  1267.1 76.8 %all-gather.5.cloned.1.call-done = bf16[256,3584]{1,0:T(8,128)(2,1)} async-done(((bf16[8,3584]{1,0:T(8,128)(2,1)}), bf16[256,3584]{1,0:T(8,128)(2,1)}) %all-gather.5.cloned.1.call-update) | async-done | bytes 1835024 | tf_op jit(solution)/shard_map/all_gather | solution.py:135
  1354.8 7.5 all-to-all-start.1
  1365.9 55.7 %all_gather.33 = bf16[256,576]{1,0:T(8,128)(2,1)S(1)} all-gather(bf16[8,576]{1,0:T(8,128)(2,1)S(1)} %maximum_select_fusion.1), channel_id=1, replica_groups=mesh['section'=8,'ep'=32] {'ep'}, dimensions={0}, use_global_device_ids=true | all-gather | bytes 304128 | tf_op jit(solution)/shard_map/all_gather | solution.py:123
  (377 shorter events, 184.5 us)
Async XLA Ops:
  7.2 88.2 %all-gather.7.cloned.1.call-start = ((), (), s32[]{:S(2)}) async-start(), calls=%async_computation.3 | async-start | bytes 4730880 | tf_op jit(solution)/shard_map/all_gather | solution.py:95
  95.4 78.9 %all-gather.9.cloned.1.call-start = ((), (), s32[]{:S(2)}) async-start(), calls=%async_computation.4 | async-start | bytes 1892352 | tf_op jit(solution)/shard_map/while/body/eval_jaxpr/all_gather | solution.py:135
  183.6 9.2 copy-start.2
  185.2 68.9 %all-to-all-start = ((bf16[32,4,3584]{2,1,0:T(4,128)(2,1)}), bf16[32,4,3584]{2,1,0:T(4,128)(2,1)S(1)}, u32[]{:S(2)}, u32[]{:S(2)}) async-start(bf16[32,4,3584]{2,1,0:T(4,128)(2,1)} %copy.85), calls=%async_computation | async-start | bytes 1835008 | tf_op jit(solution)/shard_map/while/body/eval_jaxpr/all_to_all | solution.py:101
  255.6 2.2 collective-permute-start
  257.7 83.8 %all-gather.9.cloned.1.call-start = ((), (), s32[]{:S(2)}) async-start(), calls=%async_computation.4 | async-start | bytes 1892352 | tf_op jit(solution)/shard_map/while/body/eval_jaxpr/all_gather | solution.py:135
  350.8 9.2 copy-start.2
  352.4 68.9 %all-to-all-start = ((bf16[32,4,3584]{2,1,0:T(4,128)(2,1)}), bf16[32,4,3584]{2,1,0:T(4,128)(2,1)S(1)}, u32[]{:S(2)}, u32[]{:S(2)}) async-start(bf16[32,4,3584]{2,1,0:T(4,128)(2,1)} %copy.85), calls=%async_computation | async-start | bytes 1835008 | tf_op jit(solution)/shard_map/while/body/eval_jaxpr/all_to_all | solution.py:101
  422.8 2.2 collective-permute-start
  424.9 83.5 %all-gather.9.cloned.1.call-start = ((), (), s32[]{:S(2)}) async-start(), calls=%async_computation.4 | async-start | bytes 1892352 | tf_op jit(solution)/shard_map/while/body/eval_jaxpr/all_gather | solution.py:135
  517.7 9.2 copy-start.2
  519.3 68.9 %all-to-all-start = ((bf16[32,4,3584]{2,1,0:T(4,128)(2,1)}), bf16[32,4,3584]{2,1,0:T(4,128)(2,1)S(1)}, u32[]{:S(2)}, u32[]{:S(2)}) async-start(bf16[32,4,3584]{2,1,0:T(4,128)(2,1)} %copy.85), calls=%async_computation | async-start | bytes 1835008 | tf_op jit(solution)/shard_map/while/body/eval_jaxpr/all_to_all | solution.py:101
  589.7 2.2 collective-permute-start
  591.8 83.5 %all-gather.9.cloned.1.call-start = ((), (), s32[]{:S(2)}) async-start(), calls=%async_computation.4 | async-start | bytes 1892352 | tf_op jit(solution)/shard_map/while/body/eval_jaxpr/all_gather | solution.py:135
  684.6 9.2 copy-start.2
  686.2 68.9 %all-to-all-start = ((bf16[32,4,3584]{2,1,0:T(4,128)(2,1)}), bf16[32,4,3584]{2,1,0:T(4,128)(2,1)S(1)}, u32[]{:S(2)}, u32[]{:S(2)}) async-start(bf16[32,4,3584]{2,1,0:T(4,128)(2,1)} %copy.85), calls=%async_computation | async-start | bytes 1835008 | tf_op jit(solution)/shard_map/while/body/eval_jaxpr/all_to_all | solution.py:101
  756.6 2.2 collective-permute-start
  758.7 83.5 %all-gather.9.cloned.1.call-start = ((), (), s32[]{:S(2)}) async-start(), calls=%async_computation.4 | async-start | bytes 1892352 | tf_op jit(solution)/shard_map/while/body/eval_jaxpr/all_gather | solution.py:135
  851.5 9.2 copy-start.2
  853.1 68.9 %all-to-all-start = ((bf16[32,4,3584]{2,1,0:T(4,128)(2,1)}), bf16[32,4,3584]{2,1,0:T(4,128)(2,1)S(1)}, u32[]{:S(2)}, u32[]{:S(2)}) async-start(bf16[32,4,3584]{2,1,0:T(4,128)(2,1)} %copy.85), calls=%async_computation | async-start | bytes 1835008 | tf_op jit(solution)/shard_map/while/body/eval_jaxpr/all_to_all | solution.py:101
  923.5 2.2 collective-permute-start
  925.7 83.8 %all-gather.9.cloned.1.call-start = ((), (), s32[]{:S(2)}) async-start(), calls=%async_computation.4 | async-start | bytes 1892352 | tf_op jit(solution)/shard_map/while/body/eval_jaxpr/all_gather | solution.py:135
  1018.7 9.2 copy-start.2
  1020.3 68.9 %all-to-all-start = ((bf16[32,4,3584]{2,1,0:T(4,128)(2,1)}), bf16[32,4,3584]{2,1,0:T(4,128)(2,1)S(1)}, u32[]{:S(2)}, u32[]{:S(2)}) async-start(bf16[32,4,3584]{2,1,0:T(4,128)(2,1)} %copy.85), calls=%async_computation | async-start | bytes 1835008 | tf_op jit(solution)/shard_map/while/body/eval_jaxpr/all_to_all | solution.py:101
  1090.7 2.2 collective-permute-start
  1092.9 83.8 %all-gather.9.cloned.1.call-start = ((), (), s32[]{:S(2)}) async-start(), calls=%async_computation.4 | async-start | bytes 1892352 | tf_op jit(solution)/shard_map/while/body/eval_jaxpr/all_gather | solution.py:135
  1185.9 9.2 copy-start.2
  1187.6 68.9 %all-to-all-start = ((bf16[32,4,3584]{2,1,0:T(4,128)(2,1)}), bf16[32,4,3584]{2,1,0:T(4,128)(2,1)S(1)}, u32[]{:S(2)}, u32[]{:S(2)}) async-start(bf16[32,4,3584]{2,1,0:T(4,128)(2,1)} %copy.85), calls=%async_computation | async-start | bytes 1835008 | tf_op jit(solution)/shard_map/while/body/eval_jaxpr/all_to_all | solution.py:101
  1257.9 2.2 collective-permute-start
  1260.1 83.9 %all-gather.5.cloned.1.call-start = ((), (), s32[]{:S(2)}) async-start(), calls=%async_computation.2 | async-start | bytes 1892352 | tf_op jit(solution)/shard_map/all_gather | solution.py:135
  1354.8 10.9 copy-start.3
  1354.8 67.6 %all-to-all-start.1 = ((bf16[32,4,3584]{2,1,0:T(4,128)(2,1)}), bf16[32,4,3584]{2,1,0:T(4,128)(2,1)S(1)}, u32[]{:S(2)}, u32[]{:S(2)}) async-start(bf16[32,4,3584]{2,1,0:T(4,128)(2,1)} %copy.62), calls=%async_computation.1 | async-start | bytes 1835008 | tf_op jit(solution)/shard_map/all_to_all | solution.py:101
  (2 other events, 11.3 us)
Sparse Core Ops, SparseCore 0:
  10.6 84.7 all-gather.6
  99.4 74.8 all-gather.8
  261.7 79.7 all-gather.8
  428.6 79.7 all-gather.8
  595.5 79.7 all-gather.8
  762.4 79.7 all-gather.8
  929.6 79.7 all-gather.8
  1096.8 79.7 all-gather.8
  1264.1 79.8 all-gather.4
where the time goes:
time: 1440 us; the launch traced here: 1430 us
  waiting for transfers between devices  679 us (47%)
  blocking collectives  468 us (32%)
  matrix products  107 us (7%)
  starting transfers between devices  68.5 us (5%)
  other arithmetic  47.1 us (3%)
  local copies, waits for them, and re-layouts  41.4 us (3%)
  between operations  14.6 us (1%)
    all_gather x8, waiting for transfers between devices, layer_tick(): everything = lax.all_gather(normed_moe, 'ep', axis=0, tiled=True)  586 us
    all_gather x8, blocking collectives, layer_tick(): gathered = lax.all_gather(kv_rows, 'ep', axis=0, tiled=True)  468 us
    all_gather x1, waiting for transfers between devices, body(): latent_full = lax.all_gather(w_latent[0], 'ep', axis=0, tiled=True)  86.7 us
    all_to_all x8, starting transfers between devices, send_back(): lax.all_to_all(partial_value, 'ep', split_axis=0, concat_axis=0, tiled=True)  59.4 us
    dot_general x8, matrix products, expert_slice(): jnp.einsum('smh,hd->smd', hidden, local_down, preferred_element_type=jnp....  35.3 us
  transfers between devices with their start and end apart: 24, of which 16 were waited for; matrix products, arithmetic and copies ran while one was open for 5% of the time, Pallas kernels for 0%

commit v1 on v0

v1 whole, which is shorter than its diff:
```python
import jax
import jax.numpy as jnp
from jax import lax
from jax.sharding import Mesh, PartitionSpec as P

LAT = 512
EXP_SPLIT = 4
TOPK = 2
KVBLK = 4
EARLY = 6


eps = 1e-06


def shifted(block, axis, distance):
    devices = range(lax.axis_size(axis))
    route = [(i - distance, i) for i in devices if i - distance in devices]
    return lax.ppermute(block, axis, route)


def rms_scale(values, gain_vec):
    values = values.astype(jnp.float32)
    return values * lax.rsqrt(jnp.mean(values * values, axis=-1, keepdims=True) + eps) * gain_vec


def rotate_pairs(rope_part, positions):
    half_dim = rope_part.shape[-1] // 2
    frequency = 10000.0 ** (-jnp.arange(half_dim, dtype=jnp.float32) / half_dim)
    angles = positions.astype(jnp.float32)[:, None] * frequency[None, :]
    cosine = jnp.cos(angles)
    sine_part = jnp.sin(angles)
    first_half = rope_part[:, :half_dim]
    second = rope_part[:, half_dim:]
    return jnp.concatenate(
        [first_half * cosine - second * sine_part, second * cosine + first_half * sine_part], axis=1
    )


def latent_rows(latent, gain_vec, positions):
    compressed = rms_scale(latent[:, :LAT], gain_vec)
    rotated = rotate_pairs(latent[:, LAT:], positions)
    return jnp.concatenate([compressed, rotated], axis=1).astype(jnp.bfloat16)


def packing(route_ids, expert_list, capacity):
    matches = route_ids[:, :, None, :] == expert_list[None, None, :, None]
    picked = jnp.any(matches, axis=3).astype(jnp.int32)
    slot_rank = jnp.cumsum(picked, axis=1) - 1
    slot_ids = jnp.arange(capacity, dtype=jnp.int32)
    slot_table = (slot_rank[..., None] == slot_ids) & (picked[..., None] > 0)
    return jnp.transpose(slot_table, (0, 2, 3, 1))


def expert_slice(token_rows, local_gate, local_up, local_down):
    gate_proj = jnp.dot(token_rows, local_gate, preferred_element_type=jnp.float32)
    up_proj = jnp.dot(token_rows, local_up, preferred_element_type=jnp.float32)
    hidden = (jax.nn.silu(gate_proj) * up_proj).astype(jnp.bfloat16)
    return jnp.dot(hidden, local_down, preferred_element_type=jnp.float32).astype(jnp.bfloat16)


def body(
    spans,
    attn_gain,
    kv_gain,
    moe_gain,
    w_latent,
    w_gate,
    w_up,
    w_down,
    expert_ids,
    gate_vals,
    owner_map,
    offsets,
):
    section_id = lax.axis_index("section")
    plane = lax.axis_index("z")
    column = lax.axis_index("y")
    n_planes = lax.axis_size("z")
    n_columns = lax.axis_size("y")
    member = plane * n_columns + column
    n_members = n_planes * n_columns
    n_sections = lax.axis_size("section")
    n_spans, span_dev, model_width = spans.shape
    kv_width = w_latent.shape[2]
    experts = n_members // EXP_SPLIT
    capacity = min(span_dev, 2 * span_dev * TOPK // experts)
    per_owner = span_dev // KVBLK
    all_experts = jnp.arange(experts, dtype=jnp.int32)
    local_gate = w_gate[0]
    local_up = w_up[0]
    local_down = w_down[0]
    latent_full = lax.all_gather(w_latent[0], ("z", "y"), axis=0, tiled=True)

    ticks = jnp.arange(n_sections, dtype=jnp.int32)
    tick_span = jnp.clip(ticks - section_id, 0, n_spans - 1)
    own_ids = lax.dynamic_slice_in_dim(expert_ids[0], member * span_dev, span_dev, 1)
    own_ids = jnp.take(own_ids, tick_span, axis=0)
    gate_rows = jnp.take(gate_vals[0], tick_span, axis=0)
    own_table = packing(own_ids, all_experts, capacity)
    gate_for = jnp.sum(
        jnp.where(
            own_ids[..., None] == all_experts[None, None, None, :], gate_rows[..., None], 0.0
        ),
        axis=2,
    )
    weighting = own_table.astype(jnp.float32) * jnp.transpose(gate_for, (0, 2, 1))[:, :, None, :]
    choose = own_table.astype(jnp.bfloat16).reshape(n_sections, experts * capacity, span_dev)
    weighting = jnp.transpose(
        weighting.reshape(n_sections, experts * capacity, span_dev), (0, 2, 1)
    )
    positions = (
        jnp.take(offsets, tick_span)[:, None]
        + member * span_dev
        + jnp.arange(span_dev, dtype=jnp.int32)[None, :]
    )
    block_order = jnp.take(owner_map[0], tick_span, axis=0)

    def project(first, last):
        rows = jnp.concatenate(tick_rows[first:last], axis=0)
        normed = rms_scale(rows, attn_gain[0]).astype(jnp.bfloat16)
        latent = jnp.dot(normed, latent_full, preferred_element_type=jnp.float32)
        return latent_rows(latent, kv_gain[0], positions[first:last].reshape(-1))

    def deliver_whole(first, last):
        count = last - first
        kv_rows = project(first, last)
        gathered = lax.all_gather(kv_rows, ("z", "y"), axis=0)
        blocks = gathered.reshape(n_members, count, per_owner, KVBLK * kv_width)
        blocks = jnp.transpose(blocks, (1, 0, 2, 3)).reshape(count, -1, KVBLK * kv_width)
        owned = lax.dynamic_slice_in_dim(
            block_order[first:last], member * per_owner, per_owner, 1
        )
        taken = jnp.take_along_axis(blocks, owned[:, :, None], axis=1)
        return taken.reshape(count, span_dev, kv_width)

    def deliver_planes(first, last):
        count = last - first
        kv_rows = project(first, last).reshape(count, per_owner, KVBLK * kv_width)
        column_rows = lax.all_gather(kv_rows, "y", axis=1, tiled=True)
        held = plane * n_columns * per_owner + jnp.arange(n_columns * per_owner, dtype=jnp.int32)
        wanted = block_order[first:last].reshape(count, n_planes, n_columns, per_owner)
        wanted = lax.dynamic_index_in_dim(wanted, column, 2, keepdims=False)
        pick = (wanted[..., None] == held).astype(jnp.bfloat16)
        packed = jnp.einsum(
            "tpib,tbk->ptik", pick, column_rows, preferred_element_type=jnp.float32
        ).astype(jnp.bfloat16)
        arrived = lax.all_to_all(packed, "z", split_axis=0, concat_axis=0, tiled=True)
        taken = jnp.sum(arrived.astype(jnp.float32), axis=0).astype(jnp.bfloat16)
        return taken.reshape(count, span_dev, kv_width)

    tick_rows = []
    delivered = []
    layer_in = jnp.zeros((span_dev, model_width), jnp.bfloat16)
    for tick in range(n_sections):
        tokens = jnp.where(section_id == 0, spans[tick], layer_in)
        tick_rows.append(tokens)
        if tick == EARLY:
            delivered.append(deliver_whole(0, EARLY))
        normed_moe = rms_scale(tokens, moe_gain[0]).astype(jnp.bfloat16)
        chosen = jnp.dot(
            choose[tick], normed_moe, preferred_element_type=jnp.float32
        ).astype(jnp.bfloat16)
        arrived = lax.all_to_all(chosen, "z", split_axis=0, concat_axis=0, tiled=True)
        token_rows = lax.all_gather(arrived, "y", axis=0, tiled=True)
        parts = expert_slice(token_rows, local_gate, local_up, local_down)
        quarters = lax.all_to_all(parts, "y", split_axis=0, concat_axis=0, tiled=True)
        summed = jnp.sum(
            quarters.reshape(n_columns, -1, model_width).astype(jnp.float32), axis=0
        ).astype(jnp.bfloat16)
        returned = lax.all_to_all(summed, "z", split_axis=0, concat_axis=0, tiled=True)
        moe_sum = jnp.dot(
            weighting[tick], returned.astype(jnp.float32), precision=lax.Precision.HIGHEST
        )
        layer_out = (tokens.astype(jnp.float32) + moe_sum).astype(jnp.bfloat16)
        if tick + 1 < n_sections:
            layer_in = shifted(layer_out, "section", 1)
    delivered.append(deliver_planes(EARLY, n_sections))
    blank = jnp.zeros((n_spans, span_dev, kv_width), jnp.bfloat16)
    kv_ticks = jnp.concatenate(delivered + [blank], axis=0)
    kv_store = lax.dynamic_slice_in_dim(kv_ticks, section_id, n_spans, 0)
    return (layer_out[None], kv_store[None])


def solution(mesh):
    n_members = mesh.shape["ep"]
    grid = Mesh(
        mesh.devices.reshape(mesh.shape["section"], n_members // EXP_SPLIT, EXP_SPLIT),
        ("section", "z", "y"),
    )
    ep = ("z", "y")
    in_specs = (
        P(None, ep, None),
        P("section", None),
        P("section", None),
        P("section", None),
        P("section", ep, None),
        P("section", None, ep),
        P("section", None, ep),
        P("section", ep, None),
        P("section", None, None, None),
        P("section", None, ep, None),
        P("section", None, None),
        P(),
    )
    out_specs = (P("section", ep, None), P("section", None, ep, None))
    return jax.shard_map(body, mesh=grid, in_specs=in_specs, out_specs=out_specs, check_vma=False)
```

time: 1440 us -> 608 us (0.42)
  waiting for transfers between devices: 679 us -> 113 us
  blocking collectives: 468 us -> 301 us
  other arithmetic: 47.1 us -> 10.7 us
  matrix products: 107 us -> 74.6 us
  local copies, waits for them, and re-layouts: 41.4 us -> 22.1 us
    all_gather x9 -> x2, waiting for transfers between devices: 672 us -> 11.5 us  [the longest x1 11.5 us: deliver_whole(): gathered = lax.all_gather(kv_rows, ('z', 'y'), axis=0)]
    all_gather x8 -> x9, blocking collectives: 468 us -> 125 us  [the longest x8 114 us: body(): token_rows = lax.all_gather(arrived, 'y', axis=0, tiled=True)]
    all_to_all x0 -> x12, blocking collectives: none -> 175 us  [the longest x5 77 us: body(): lax.all_to_all(chosen, 'z', split_axis=0, concat_axis=0, tiled=True)]
    all_to_all x8 -> x13, waiting for transfers between devices: 0.02 us -> 95.5 us  [the longest x4 37.8 us: body(): lax.all_to_all(summed, 'z', split_axis=0, concat_axis=0, tiled=True)]
    dot_general x40 -> x35, matrix products: 107 us -> 74.6 us  [the longest x8 39.9 us: expert_slice(): jnp.dot(hidden, local_down, preferred_element_type=jnp.float32)]
    all_to_all x8 -> x13, starting transfers between devices: 59.4 us -> 58.7 us  [the longest x5 26.5 us: body(): lax.all_to_all(parts, 'y', split_axis=0, concat_axis=0, tiled=True)]
  transfers between devices with their start and end apart: 24 -> 22, of which waited for: 16 -> 18; matrix products, arithmetic and copies ran while one was open for 5% -> 9% of each run, Pallas kernels for 0% -> 0%
where the time goes in v1:
time: 608 us; the launch traced here: 604 us
  blocking collectives  301 us (50%)
  waiting for transfers between devices  113 us (19%)
  matrix products  74.6 us (12%)
  starting transfers between devices  68 us (11%)
  local copies, waits for them, and re-layouts  22.1 us (4%)
  between operations  14.9 us (2%)
  other arithmetic  10.7 us (2%)
    all_gather x8, blocking collectives, body(): token_rows = lax.all_gather(arrived, 'y', axis=0, tiled=True)  114 us
    all_to_all x5, blocking collectives, body(): lax.all_to_all(chosen, 'z', split_axis=0, concat_axis=0, tiled=True)  77 us
    all_to_all x4, blocking collectives, body(): lax.all_to_all(summed, 'z', split_axis=0, concat_axis=0, tiled=True)  52.3 us
    all_to_all x3, blocking collectives, body(): lax.all_to_all(parts, 'y', split_axis=0, concat_axis=0, tiled=True)  46.1 us
    dot_general x8, matrix products, expert_slice(): jnp.dot(hidden, local_down, preferred_element_type=jnp.float32)  39.9 us
    all_to_all x4, waiting for transfers between devices, body(): lax.all_to_all(summed, 'z', split_axis=0, concat_axis=0, tiled=True)  37.8 us
    all_to_all x5, waiting for transfers between devices, body(): lax.all_to_all(parts, 'y', split_axis=0, concat_axis=0, tiled=True)  35.6 us
    all_to_all x5, starting transfers between devices, body(): lax.all_to_all(parts, 'y', split_axis=0, concat_axis=0, tiled=True)  26.5 us
  transfers between devices with their start and end apart: 22, of which 18 were waited for; matrix products, arithmetic and copies ran while one was open for 9% of the time, Pallas kernels for 0%

profile of v1, /device:TPU:8, one launch (start us, length us, event | category | flops | bytes accessed | tf_op | source)
XLA Modules:
  0.0 603.8 jit_solution(14209103846554707275)
XLA Ops:
  12.0 19.4 %all_to_all.269 = bf16[8,4,3584]{2,1,0:T(4,128)(2,1)S(1)} all-to-all(bf16[8,4,3584]{2,1,0:T(4,128)(2,1)S(1)} %all_to_all.179), channel_id=1, replica_groups=mesh['section'=8,'z'=8,'y'=4] {'z'}, dimensions={0} | all-to-all | bytes 458752 | tf_op jit(solution)/shard_map/all_to_all | solution.py:164
  31.5 13.9 %all_gather.34 = bf16[128,3584]{1,0:T(8,128)(2,1)S(1)} all-gather(bf16[32,3584]{1,0:T(8,128)(2,1)S(1)} %all_to_all.181), channel_id=1, replica_groups=mesh['section'=8,'z'=8,'y'=4] {'y'}, dimensions={0}, use_global_device_ids=true | all-gather | bytes 1146880 | tf_op jit(solution)/shard_map/all_gather | solution.py:165
  59.1 8.2 %all-to-all-done.1 = bf16[4,32,3584]{2,1,0:T(8,128)(2,1)S(1)} async-done(((bf16[4,32,3584]{2,1,0:T(8,128)(2,1)}), bf16[4,32,3584]{2,1,0:T(8,128)(2,1)S(1)}, u32[]{:S(2)}, u32[]{:S(2)}) %all-to-all-start.1) | async-done | bytes 917536 | tf_op jit(solution)/shard_map/all_to_all | solution.py:167
  72.2 9.5 %all-to-all-done.2 = bf16[8,4,3584]{2,1,0:T(4,128)(2,1)S(1)} async-done(((bf16[8,4,3584]{2,1,0:T(4,128)(2,1)}), bf16[8,4,3584]{2,1,0:T(4,128)(2,1)S(1)}, u32[]{:S(2)}, u32[]{:S(2)}) %all-to-all-start.2) | async-done | bytes 229408 | tf_op jit(solution)/shard_map/all_to_all | solution.py:171
  84.7 13.1 %all_to_all.270 = bf16[8,4,3584]{2,1,0:T(4,128)(2,1)S(1)} all-to-all(bf16[8,4,3584]{2,1,0:T(4,128)(2,1)S(1)} %all_to_all.187), channel_id=1, replica_groups=mesh['section'=8,'z'=8,'y'=4] {'z'}, dimensions={0} | all-to-all | bytes 458752 | tf_op jit(solution)/shard_map/all_to_all | solution.py:164
  97.9 14.1 %all_gather.35 = bf16[128,3584]{1,0:T(8,128)(2,1)S(1)} all-gather(bf16[32,3584]{1,0:T(8,128)(2,1)S(1)} %all_to_all.189), channel_id=1, replica_groups=mesh['section'=8,'z'=8,'y'=4] {'y'}, dimensions={0}, use_global_device_ids=true | all-gather | bytes 1146880 | tf_op jit(solution)/shard_map/all_gather | solution.py:165
  119.1 17.3 %all_to_all.271 = bf16[4,32,3584]{2,1,0:T(8,128)(2,1)S(1)} all-to-all(bf16[4,32,3584]{2,1,0:T(8,128)(2,1)S(1)} %bitcast.246), channel_id=1, replica_groups=mesh['section'=8,'z'=8,'y'=4] {'y'}, dimensions={0} | all-to-all | bytes 1835008 | tf_op jit(solution)/shard_map/all_to_all | solution.py:167
  136.6 13.2 %all_to_all.272 = bf16[8,4,3584]{2,1,0:T(4,128)(2,1)S(1)} all-to-all(bf16[8,4,3584]{2,1,0:T(4,128)(2,1)S(1)} %all_to_all.192), channel_id=1, replica_groups=mesh['section'=8,'z'=8,'y'=4] {'z'}, dimensions={0} | all-to-all | bytes 458752 | tf_op jit(solution)/shard_map/all_to_all | solution.py:171
  152.8 14.9 %all_to_all.273 = bf16[8,4,3584]{2,1,0:T(4,128)(2,1)S(1)} all-to-all(bf16[8,4,3584]{2,1,0:T(4,128)(2,1)S(1)} %all_to_all.195), channel_id=1, replica_groups=mesh['section'=8,'z'=8,'y'=4] {'z'}, dimensions={0} | all-to-all | bytes 458752 | tf_op jit(solution)/shard_map/all_to_all | solution.py:164
  167.8 13.6 %all_gather.36 = bf16[128,3584]{1,0:T(8,128)(2,1)S(1)} all-gather(bf16[32,3584]{1,0:T(8,128)(2,1)S(1)} %all_to_all.197), channel_id=1, replica_groups=mesh['section'=8,'z'=8,'y'=4] {'y'}, dimensions={0}, use_global_device_ids=true | all-gather | bytes 1146880 | tf_op jit(solution)/shard_map/all_gather | solution.py:165
  188.5 14.4 %all_to_all.274 = bf16[4,32,3584]{2,1,0:T(8,128)(2,1)S(1)} all-to-all(bf16[4,32,3584]{2,1,0:T(8,128)(2,1)S(1)} %bitcast.247), channel_id=1, replica_groups=mesh['section'=8,'z'=8,'y'=4] {'y'}, dimensions={0} | all-to-all | bytes 1835008 | tf_op jit(solution)/shard_map/all_to_all | solution.py:167
  203.2 13.1 %all_to_all.275 = bf16[8,4,3584]{2,1,0:T(4,128)(2,1)S(1)} all-to-all(bf16[8,4,3584]{2,1,0:T(4,128)(2,1)S(1)} %all_to_all.200), channel_id=1, replica_groups=mesh['section'=8,'z'=8,'y'=4] {'z'}, dimensions={0} | all-to-all | bytes 458752 | tf_op jit(solution)/shard_map/all_to_all | solution.py:171
  219.3 14.8 %all_to_all.276 = bf16[8,4,3584]{2,1,0:T(4,128)(2,1)S(1)} all-to-all(bf16[8,4,3584]{2,1,0:T(4,128)(2,1)S(1)} %all_to_all.203), channel_id=1, replica_groups=mesh['section'=8,'z'=8,'y'=4] {'z'}, dimensions={0} | all-to-all | bytes 458752 | tf_op jit(solution)/shard_map/all_to_all | solution.py:164
  234.1 13.7 %all_gather.37 = bf16[128,3584]{1,0:T(8,128)(2,1)S(1)} all-gather(bf16[32,3584]{1,0:T(8,128)(2,1)S(1)} %all_to_all.205), channel_id=1, replica_groups=mesh['section'=8,'z'=8,'y'=4] {'y'}, dimensions={0}, use_global_device_ids=true | all-gather | bytes 1146880 | tf_op jit(solution)/shard_map/all_gather | solution.py:165
  254.9 14.4 %all_to_all.277 = bf16[4,32,3584]{2,1,0:T(8,128)(2,1)S(1)} all-to-all(bf16[4,32,3584]{2,1,0:T(8,128)(2,1)S(1)} %bitcast.248), channel_id=1, replica_groups=mesh['section'=8,'z'=8,'y'=4] {'y'}, dimensions={0} | all-to-all | bytes 1835008 | tf_op jit(solution)/shard_map/all_to_all | solution.py:167
  269.6 12.5 %all_to_all.278 = bf16[8,4,3584]{2,1,0:T(4,128)(2,1)S(1)} all-to-all(bf16[8,4,3584]{2,1,0:T(4,128)(2,1)S(1)} %all_to_all.208), channel_id=1, replica_groups=mesh['section'=8,'z'=8,'y'=4] {'z'}, dimensions={0} | all-to-all | bytes 458752 | tf_op jit(solution)/shard_map/all_to_all | solution.py:171
  285.1 14.7 %all_to_all.279 = bf16[8,4,3584]{2,1,0:T(4,128)(2,1)S(1)} all-to-all(bf16[8,4,3584]{2,1,0:T(4,128)(2,1)S(1)} %all_to_all.211), channel_id=1, replica_groups=mesh['section'=8,'z'=8,'y'=4] {'z'}, dimensions={0} | all-to-all | bytes 458752 | tf_op jit(solution)/shard_map/all_to_all | solution.py:164
  299.9 13.6 %all_gather.38 = bf16[128,3584]{1,0:T(8,128)(2,1)S(1)} all-gather(bf16[32,3584]{1,0:T(8,128)(2,1)S(1)} %all_to_all.213), channel_id=1, replica_groups=mesh['section'=8,'z'=8,'y'=4] {'y'}, dimensions={0}, use_global_device_ids=true | all-gather | bytes 1146880 | tf_op jit(solution)/shard_map/all_gather | solution.py:165
  328.2 8.9 %all-to-all-done.13 = bf16[4,32,3584]{2,1,0:T(8,128)(2,1)S(1)} async-done(((bf16[4,32,3584]{2,1,0:T(8,128)(2,1)}), bf16[4,32,3584]{2,1,0:T(8,128)(2,1)S(1)}, u32[]{:S(2)}, u32[]{:S(2)}) %all-to-all-start.13) | async-done | bytes 917536 | tf_op jit(solution)/shard_map/all_to_all | solution.py:167
  337.3 13.5 %all_to_all.280 = bf16[8,4,3584]{2,1,0:T(4,128)(2,1)S(1)} all-to-all(bf16[8,4,3584]{2,1,0:T(4,128)(2,1)S(1)} %all_to_all.216), channel_id=1, replica_groups=mesh['section'=8,'z'=8,'y'=4] {'z'}, dimensions={0} | all-to-all | bytes 458752 | tf_op jit(solution)/shard_map/all_to_all | solution.py:171
  359.2 10.9 %all-to-all-done.15 = bf16[8,4,3584]{2,1,0:T(4,128)(2,1)S(1)} async-done(((bf16[8,4,3584]{2,1,0:T(4,128)(2,1)}), bf16[8,4,3584]{2,1,0:T(4,128)(2,1)S(1)}, u32[]{:S(2)}, u32[]{:S(2)}) %all-to-all-start.15) | async-done | bytes 229408 | tf_op jit(solution)/shard_map/all_to_all | solution.py:164
  370.2 16.9 %all_gather.39 = bf16[128,3584]{1,0:T(8,128)(2,1)S(1)} all-gather(bf16[32,3584]{1,0:T(8,128)(2,1)S(1)} %all_to_all.221), channel_id=1, replica_groups=mesh['section'=8,'z'=8,'y'=4] {'y'}, dimensions={0}, use_global_device_ids=true | all-gather | bytes 1146880 | tf_op jit(solution)/shard_map/all_gather | solution.py:165
  400.6 9.7 %all-to-all-done.16 = bf16[4,32,3584]{2,1,0:T(8,128)(2,1)S(1)} async-done(((bf16[4,32,3584]{2,1,0:T(8,128)(2,1)}), bf16[4,32,3584]{2,1,0:T(8,128)(2,1)S(1)}, u32[]{:S(2)}, u32[]{:S(2)}) %all-to-all-start.16) | async-done | bytes 917536 | tf_op jit(solution)/shard_map/all_to_all | solution.py:167
  415.2 10.1 %all-to-all-done.17 = bf16[8,4,3584]{2,1,0:T(4,128)(2,1)S(1)} async-done(((bf16[8,4,3584]{2,1,0:T(4,128)(2,1)}), bf16[8,4,3584]{2,1,0:T(4,128)(2,1)S(1)}, u32[]{:S(2)}, u32[]{:S(2)}) %all-to-all-start.17) | async-done | bytes 229408 | tf_op jit(solution)/shard_map/all_to_all | solution.py:171
  432.9 11.2 %all-to-all-done.18 = bf16[8,4,3584]{2,1,0:T(4,128)(2,1)S(1)} async-done(((bf16[8,4,3584]{2,1,0:T(4,128)(2,1)}), bf16[8,4,3584]{2,1,0:T(4,128)(2,1)S(1)}, u32[]{:S(2)}, u32[]{:S(2)}) %all-to-all-start.18) | async-done | bytes 229408 | tf_op jit(solution)/shard_map/all_to_all | solution.py:164
  444.2 13.5 %all_gather.40 = bf16[128,3584]{1,0:T(8,128)(2,1)S(1)} all-gather(bf16[32,3584]{1,0:T(8,128)(2,1)S(1)} %all_to_all.229), channel_id=1, replica_groups=mesh['section'=8,'z'=8,'y'=4] {'y'}, dimensions={0}, use_global_device_ids=true | all-gather | bytes 1146880 | tf_op jit(solution)/shard_map/all_gather | solution.py:165
  474.3 8.9 %all-to-all-done.19 = bf16[4,32,3584]{2,1,0:T(8,128)(2,1)S(1)} async-done(((bf16[4,32,3584]{2,1,0:T(8,128)(2,1)}), bf16[4,32,3584]{2,1,0:T(8,128)(2,1)S(1)}, u32[]{:S(2)}, u32[]{:S(2)}) %all-to-all-start.19) | async-done | bytes 917536 | tf_op jit(solution)/shard_map/all_to_all | solution.py:167
  487.7 10.3 %all-to-all-done.20 = bf16[8,4,3584]{2,1,0:T(4,128)(2,1)S(1)} async-done(((bf16[8,4,3584]{2,1,0:T(4,128)(2,1)}), bf16[8,4,3584]{2,1,0:T(4,128)(2,1)S(1)}, u32[]{:S(2)}, u32[]{:S(2)}) %all-to-all-start.20) | async-done | bytes 229408 | tf_op jit(solution)/shard_map/all_to_all | solution.py:171
  508.8 11.3 %all_gather.44 = bf16[2,8,2304]{2,0,1:T(2,128)(2,1)S(1)} all-gather(bf16[2,2,2304]{2,0,1:T(2,128)(2,1)S(1)} %copy.72), channel_id=1, replica_groups=mesh['section'=8,'z'=8,'y'=4] {'y'}, dimensions={1}, use_global_device_ids=true | all-gather | bytes 92160 | tf_op jit(solution)/shard_map/all_gather | solution.py:140
  528.3 14.6 %all_gather.41 = bf16[128,3584]{1,0:T(8,128)(2,1)S(1)} all-gather(bf16[32,3584]{1,0:T(8,128)(2,1)S(1)} %all_to_all.237), channel_id=1, replica_groups=mesh['section'=8,'z'=8,'y'=4] {'y'}, dimensions={0}, use_global_device_ids=true | all-gather | bytes 1146880 | tf_op jit(solution)/shard_map/all_gather | solution.py:165
  559.6 11.5 %all-gather.4.cloned.1.call-done = bf16[32,48,576]{2,1,0:T(8,128)(2,1)} async-done(((bf16[1,48,576]{2,1,0:T(8,128)(2,1)}), bf16[32,48,576]{2,1,0:T(8,128)(2,1)}) %all-gather.4.cloned.1.call-update) | async-done | bytes 1769488 | tf_op jit(solution)/shard_map/all_gather | solution.py:128
  587.2 7.9 %all-to-all-done.23 = bf16[8,4,3584]{2,1,0:T(4,128)(2,1)S(1)} async-done(((bf16[8,4,3584]{2,1,0:T(4,128)(2,1)}), bf16[8,4,3584]{2,1,0:T(4,128)(2,1)S(1)}, u32[]{:S(2)}, u32[]{:S(2)}) %all-to-all-start.23) | async-done | bytes 229408 | tf_op jit(solution)/shard_map/all_to_all | solution.py:171
  (230 shorter events, 181.3 us)
Async XLA Ops:
  7.2 0.7 copy-start
  48.1 10.5 %copy-start.6 = (f32[1,8,8,2]{2,3,1,0:T(2,128)S(1)}, f32[1,8,8,2]{2,3,1,0:T(2,128)}, u32[]{:S(2)}) copy-start(f32[1,8,8,2]{2,3,1,0:T(2,128)} %param.21) | copy-start | bytes 1540
  53.4 28.3 %copy-start.3 = (bf16[8,8,3584]{2,1,0:T(8,128)(2,1)S(1)}, bf16[8,8,3584]{2,1,0:T(8,128)(2,1)}, u32[]{:S(2)}) copy-start(bf16[8,8,3584]{2,1,0:T(8,128)(2,1)} %param.12) | copy-start | bytes 1376260
  53.4 13.9 %all-to-all-start.1 = ((bf16[4,32,3584]{2,1,0:T(8,128)(2,1)}), bf16[4,32,3584]{2,1,0:T(8,128)(2,1)S(1)}, u32[]{:S(2)}, u32[]{:S(2)}) async-start(bf16[4,32,3584]{2,1,0:T(8,128)(2,1)} %bitcast.24), calls=%async_computation.1 | async-start | bytes 1835008 | tf_op jit(solution)/shard_map/all_to_all | solution.py:167
  68.2 13.4 %all-to-all-start.2 = ((bf16[8,4,3584]{2,1,0:T(4,128)(2,1)}), bf16[8,4,3584]{2,1,0:T(4,128)(2,1)S(1)}, u32[]{:S(2)}, u32[]{:S(2)}) async-start(bf16[8,4,3584]{2,1,0:T(4,128)(2,1)} %all_to_all.184), calls=%async_computation.2 | async-start | bytes 458752 | tf_op jit(solution)/shard_map/all_to_all | solution.py:171
  72.2 425.8 %copy-start.4 = (f32[8,8,32]{1,2,0:T(8,128)}, f32[8,8,32]{1,2,0:T(8,128)S(1)}, u32[]{:S(2)}) copy-start(f32[8,8,32]{1,2,0:T(8,128)S(1)} %select_bitcast_fusion) | copy-start | bytes 24580
  82.0 2.2 collective-permute-start
  150.1 2.2 collective-permute-start.1
  216.6 2.2 collective-permute-start.2
  282.4 2.2 collective-permute-start.3
  321.5 36.4 %copy-start.1 = (s32[8]{0:T(128)S(1)}, s32[8]{0:T(128)}, u32[]{:S(2)}) copy-start(s32[8]{0:T(128)} %param.23) | copy-start | bytes 100
  321.5 37.1 %copy-start.5 = (s32[1,8,64]{2,1,0:T(8,128)S(1)}, s32[1,8,64]{2,1,0:T(8,128)}, u32[]{:S(2)}) copy-start(s32[1,8,64]{2,1,0:T(8,128)} %param.22) | copy-start | bytes 6148
  321.5 15.5 %all-to-all-start.13 = ((bf16[4,32,3584]{2,1,0:T(8,128)(2,1)}), bf16[4,32,3584]{2,1,0:T(8,128)(2,1)S(1)}, u32[]{:S(2)}, u32[]{:S(2)}) async-start(bf16[4,32,3584]{2,1,0:T(8,128)(2,1)} %bitcast.36), calls=%async_computation.13 | async-start | bytes 1835008 | tf_op jit(solution)/shard_map/all_to_all | solution.py:167
  327.5 143.2 %all-gather.6.cloned.1.call-start = ((), (), s32[]{:S(2)}) async-start(), calls=%async_computation.26 | async-start | bytes 4730880 | tf_op jit(solution)/shard_map/all_gather | solution.py:93
  351.2 2.2 collective-permute-start.4
  354.6 15.6 %all-to-all-start.15 = ((bf16[8,4,3584]{2,1,0:T(4,128)(2,1)}), bf16[8,4,3584]{2,1,0:T(4,128)(2,1)S(1)}, u32[]{:S(2)}, u32[]{:S(2)}) async-start(bf16[8,4,3584]{2,1,0:T(4,128)(2,1)} %all_to_all.219), calls=%async_computation.15 | async-start | bytes 458752 | tf_op jit(solution)/shard_map/all_to_all | solution.py:164
  395.3 37.2 %copy-start.7 = (f32[1,3584]{1,0:T(1,128)S(1)}, f32[1,3584]{1,0:T(1,128)}, u32[]{:S(2)}) copy-start(f32[1,3584]{1,0:T(1,128)} %param.13) | copy-start | bytes 43012
  395.3 15.0 %all-to-all-start.16 = ((bf16[4,32,3584]{2,1,0:T(8,128)(2,1)}), bf16[4,32,3584]{2,1,0:T(8,128)(2,1)S(1)}, u32[]{:S(2)}, u32[]{:S(2)}) async-start(bf16[4,32,3584]{2,1,0:T(8,128)(2,1)} %bitcast.39), calls=%async_computation.16 | async-start | bytes 1835008 | tf_op jit(solution)/shard_map/all_to_all | solution.py:167
  411.2 14.1 %all-to-all-start.17 = ((bf16[8,4,3584]{2,1,0:T(4,128)(2,1)}), bf16[8,4,3584]{2,1,0:T(4,128)(2,1)S(1)}, u32[]{:S(2)}, u32[]{:S(2)}) async-start(bf16[8,4,3584]{2,1,0:T(4,128)(2,1)} %all_to_all.224), calls=%async_computation.17 | async-start | bytes 458752 | tf_op jit(solution)/shard_map/all_to_all | solution.py:171
  425.7 2.2 collective-permute-start.5
  429.0 15.1 %all-to-all-start.18 = ((bf16[8,4,3584]{2,1,0:T(4,128)(2,1)}), bf16[8,4,3584]{2,1,0:T(4,128)(2,1)S(1)}, u32[]{:S(2)}, u32[]{:S(2)}) async-start(bf16[8,4,3584]{2,1,0:T(4,128)(2,1)} %all_to_all.227), calls=%async_computation.18 | async-start | bytes 458752 | tf_op jit(solution)/shard_map/all_to_all | solution.py:164
  465.7 17.4 %all-to-all-start.19 = ((bf16[4,32,3584]{2,1,0:T(8,128)(2,1)}), bf16[4,32,3584]{2,1,0:T(8,128)(2,1)S(1)}, u32[]{:S(2)}, u32[]{:S(2)}) async-start(bf16[4,32,3584]{2,1,0:T(8,128)(2,1)} %bitcast.42), calls=%async_computation.19 | async-start | bytes 1835008 | tf_op jit(solution)/shard_map/all_to_all | solution.py:167
  470.7 16.9 %copy-start.8 = (f32[1,512]{1,0:T(1,128)S(1)}, f32[1,512]{1,0:T(1,128)}, u32[]{:S(2)}) copy-start(f32[1,512]{1,0:T(1,128)} %param.14) | copy-start | bytes 6148
  484.1 13.8 %all-to-all-start.20 = ((bf16[8,4,3584]{2,1,0:T(4,128)(2,1)}), bf16[8,4,3584]{2,1,0:T(4,128)(2,1)S(1)}, u32[]{:S(2)}, u32[]{:S(2)}) async-start(bf16[8,4,3584]{2,1,0:T(4,128)(2,1)} %all_to_all.232), calls=%async_computation.20 | async-start | bytes 458752 | tf_op jit(solution)/shard_map/all_to_all | solution.py:171
  487.5 83.6 %all-gather.4.cloned.1.call-start = ((), (), s32[]{:S(2)}) async-start(), calls=%async_computation.25 | async-start | bytes 2027520 | tf_op jit(solution)/shard_map/all_gather | solution.py:128
  498.3 2.2 collective-permute-start.6
  500.6 27.6 %copy-start.2 = (bf16[8,3584]{1,0:T(8,128)(2,1)}, bf16[8,3584]{1,0:T(8,128)(2,1)S(1)}, u32[]{:S(2)}) copy-start(bf16[8,3584]{1,0:T(8,128)(2,1)S(1)} %get-tuple-element.13) | copy-start | bytes 172036
  501.8 19.3 %all-to-all-start.21 = ((bf16[8,4,3584]{2,1,0:T(4,128)(2,1)}), bf16[8,4,3584]{2,1,0:T(4,128)(2,1)S(1)}, u32[]{:S(2)}, u32[]{:S(2)}) async-start(bf16[8,4,3584]{2,1,0:T(4,128)(2,1)} %all_to_all.235), calls=%async_computation.21 | async-start | bytes 458752 | tf_op jit(solution)/shard_map/all_to_all | solution.py:164
  521.1 29.9 %all-to-all-start.24 = ((bf16[8,2,2,2304]{3,2,1,0:T(2,128)(2,1)}), bf16[8,2,2,2304]{3,2,1,0:T(2,128)(2,1)S(1)}, u32[]{:S(2)}, u32[]{:S(2)}) async-start(bf16[8,2,2,2304]{3,2,1,0:T(2,128)(2,1)} %copy.75), calls=%async_computation.24 | async-start | bytes 294912 | tf_op jit(solution)/shard_map/all_to_all | solution.py:148
  551.0 27.7 %all-to-all-start.22 = ((bf16[4,32,3584]{2,1,0:T(8,128)(2,1)}), bf16[4,32,3584]{2,1,0:T(8,128)(2,1)}, u32[]{:S(2)}, u32[]{:S(2)}) async-start(bf16[4,32,3584]{2,1,0:T(8,128)(2,1)} %bitcast.45), calls=%async_computation.22 | async-start | bytes 1835008 | tf_op jit(solution)/shard_map/all_to_all | solution.py:167
  580.8 14.3 %all-to-all-start.23 = ((bf16[8,4,3584]{2,1,0:T(4,128)(2,1)}), bf16[8,4,3584]{2,1,0:T(4,128)(2,1)S(1)}, u32[]{:S(2)}, u32[]{:S(2)}) async-start(bf16[8,4,3584]{2,1,0:T(4,128)(2,1)} %all_to_all.240), calls=%async_computation.23 | async-start | bytes 458752 | tf_op jit(solution)/shard_map/all_to_all | solution.py:171
Sparse Core Ops, SparseCore 0:
  330.9 80.6 all-gather.5
  500.4 70.6 all-gather.3

commit v2 on v1

--- a/solution.py
+++ b/solution.py
@@ -1,6 +1,8 @@
 import jax
 import jax.numpy as jnp
 from jax import lax
+from jax.experimental import pallas as pl
+from jax.experimental.pallas import tpu as pltpu
 from jax.sharding import Mesh, PartitionSpec as P
 
 LAT = 512
@@ -17,6 +19,14 @@
     devices = range(lax.axis_size(axis))
     route = [(i - distance, i) for i in devices if i - distance in devices]
     return lax.ppermute(block, axis, route)
+
+
+def turned(block, distance, live):
+    size = lax.axis_size("y")
+    route = [
+        (s * size + i, s * size + (i + distance) % size) for s in range(live) for i in range(size)
+    ]
+    return lax.ppermute(block, ("section", "y"), route)
 
 
 def rms_scale(values, gain_vec):
@@ -52,11 +62,79 @@
     return jnp.transpose(slot_table, (0, 2, 3, 1))
 
 
-def expert_slice(token_rows, local_gate, local_up, local_down):
-    gate_proj = jnp.dot(token_rows, local_gate, preferred_element_type=jnp.float32)
-    up_proj = jnp.dot(token_rows, local_up, preferred_element_type=jnp.float32)
-    hidden = (jax.nn.silu(gate_proj) * up_proj).astype(jnp.bfloat16)
-    return jnp.dot(hidden, local_down, preferred_element_type=jnp.float32).astype(jnp.bfloat16)
+def expert_kernel(
+    n_chunks, rows, first, second, third, fourth, gate_hbm, up_hbm, down_hbm,
+    first_out, second_out, third_out, fourth_out,
+    tokens, gate_buf, up_buf, down_buf, gate_sem, up_sem, down_sem,
+):
+    depth = gate_buf.shape[0] // n_chunks
+    width = down_buf.shape[1] // n_chunks
+    gate_copies = []
+    up_copies = []
+    down_copies = []
+    for i in range(n_chunks):
+        span = pl.ds(i * depth, depth)
+        gate_copies.append(
+            pltpu.make_async_copy(gate_hbm.at[span, :], gate_buf.at[span, :], gate_sem.at[i])
+        )
+        up_copies.append(
+            pltpu.make_async_copy(up_hbm.at[span, :], up_buf.at[span, :], up_sem.at[i])
+        )
+        cols = pl.ds(i * width, width)
+        down_copies.append(
+            pltpu.make_async_copy(down_hbm.at[:, cols], down_buf.at[:, cols], down_sem.at[i])
+        )
+    for i in range(n_chunks):
+        gate_copies[i].start()
+        up_copies[i].start()
+    for i in range(n_chunks):
+        down_copies[i].start()
+    for k, chunk in enumerate((first, second, third, fourth)):
+        tokens[pl.ds(k * rows, rows), :] = chunk[...]
+    gate_proj = jnp.zeros((4 * rows, gate_buf.shape[1]), jnp.float32)
+    up_proj = jnp.zeros((4 * rows, gate_buf.shape[1]), jnp.float32)
+    for i in range(n_chunks):
+        span = pl.ds(i * depth, depth)
+        gate_copies[i].wait()
+        gate_proj += jnp.dot(
+            tokens[:, span], gate_buf[span, :], preferred_element_type=jnp.float32
+        )
+        up_copies[i].wait()
+        up_proj += jnp.dot(tokens[:, span], up_buf[span, :], preferred_element_type=jnp.float32)
+    hidden = (gate_proj / (1.0 + jnp.exp(-gate_proj)) * up_proj).astype(jnp.bfloat16)
+    for i in range(n_chunks):
+        cols = pl.ds(i * width, width)
+        down_copies[i].wait()
+        part = jnp.dot(hidden, down_buf[:, cols], preferred_element_type=jnp.float32)
+        part = part.astype(jnp.bfloat16)
+        for k, out in enumerate((first_out, second_out, third_out, fourth_out)):
+            out[:, cols] = part[k * rows : (k + 1) * rows, :]
+
+
+def expert_slice(chunks, local_gate, local_up, local_down):
+    rows, model_width = chunks[0].shape
+    hidden_width = local_gate.shape[1]
+    n_chunks = 7
+    flops = 2 * 4 * rows * model_width * hidden_width * 3
+    moved = 3 * 2 * model_width * hidden_width
+    return pl.pallas_call(
+        lambda *refs: expert_kernel(n_chunks, rows, *refs),
+        out_shape=[jax.ShapeDtypeStruct((rows, model_width), jnp.bfloat16)] * 4,
+        in_specs=[pl.BlockSpec(memory_space=pltpu.VMEM)] * 4
+        + [pl.BlockSpec(memory_space=pl.ANY)] * 3,
+        out_specs=[pl.BlockSpec(memory_space=pltpu.VMEM)] * 4,
+        scratch_shapes=[
+            pltpu.VMEM((4 * rows, model_width), jnp.bfloat16),
+            pltpu.VMEM((model_width, hidden_width), jnp.bfloat16),
+            pltpu.VMEM((model_width, hidden_width), jnp.bfloat16),
+            pltpu.VMEM((hidden_width, model_width), jnp.bfloat16),
+            pltpu.SemaphoreType.DMA((n_chunks,)),
+            pltpu.SemaphoreType.DMA((n_chunks,)),
+            pltpu.SemaphoreType.DMA((n_chunks,)),
+        ],
+        compiler_params=pltpu.CompilerParams(vmem_limit_bytes=40 * 1024 * 1024),
+        cost_estimate=pl.CostEstimate(flops=flops, bytes_accessed=moved, transcendentals=0),
+    )(*chunks, local_gate, local_up, local_down)
 
 
 def body(
@@ -92,11 +170,12 @@
     local_down = w_down[0]
     latent_full = lax.all_gather(w_latent[0], ("z", "y"), axis=0, tiled=True)
 
-    ticks = jnp.arange(n_sections, dtype=jnp.int32)
-    tick_span = jnp.clip(ticks - section_id, 0, n_spans - 1)
-    own_ids = lax.dynamic_slice_in_dim(expert_ids[0], member * span_dev, span_dev, 1)
-    own_ids = jnp.take(own_ids, tick_span, axis=0)
-    gate_rows = jnp.take(gate_vals[0], tick_span, axis=0)
+    def by_tick(values):
+        padded = jnp.concatenate([jnp.zeros_like(values), values], axis=0)
+        return lax.dynamic_slice_in_dim(padded, n_spans - section_id, n_sections, 0)
+
+    own_ids = by_tick(lax.dynamic_slice_in_dim(expert_ids[0], member * span_dev, span_dev, 1))
+    gate_rows = by_tick(gate_vals[0])
     own_table = packing(own_ids, all_experts, capacity)
     gate_for = jnp.sum(
         jnp.where(
@@ -110,11 +189,11 @@
         weighting.reshape(n_sections, experts * capacity, span_dev), (0, 2, 1)
     )
     positions = (
-        jnp.take(offsets, tick_span)[:, None]
+        by_tick(offsets)[:, None]
         + member * span_dev
         + jnp.arange(span_dev, dtype=jnp.int32)[None, :]
     )
-    block_order = jnp.take(owner_map[0], tick_span, axis=0)
+    block_order = by_tick(owner_map[0])
 
     def project(first, last):
         rows = jnp.concatenate(tick_rows[first:last], axis=0)
@@ -134,48 +213,70 @@
         taken = jnp.take_along_axis(blocks, owned[:, :, None], axis=1)
         return taken.reshape(count, span_dev, kv_width)
 
-    def deliver_planes(first, last):
+    def to_planes(first, last):
         count = last - first
-        kv_rows = project(first, last).reshape(count, per_owner, KVBLK * kv_width)
-        column_rows = lax.all_gather(kv_rows, "y", axis=1, tiled=True)
-        held = plane * n_columns * per_owner + jnp.arange(n_columns * per_owner, dtype=jnp.int32)
-        wanted = block_order[first:last].reshape(count, n_planes, n_columns, per_owner)
-        wanted = lax.dynamic_index_in_dim(wanted, column, 2, keepdims=False)
-        pick = (wanted[..., None] == held).astype(jnp.bfloat16)
-        packed = jnp.einsum(
-            "tpib,tbk->ptik", pick, column_rows, preferred_element_type=jnp.float32
-        ).astype(jnp.bfloat16)
-        arrived = lax.all_to_all(packed, "z", split_axis=0, concat_axis=0, tiled=True)
-        taken = jnp.sum(arrived.astype(jnp.float32), axis=0).astype(jnp.bfloat16)
-        return taken.reshape(count, span_dev, kv_width)
+        blocks = project(first, last).reshape(count, per_owner, KVBLK * kv_width)
+        held = member * per_owner + jnp.arange(per_owner, dtype=jnp.int32)
+        wanted = block_order[first:last].reshape(count, n_planes, 1, n_columns * per_owner)
+        pick = (wanted == held[:, None]).any(axis=3).astype(jnp.bfloat16)
+        packed = jnp.transpose(pick, (1, 0, 2))[..., None] * blocks[None]
+        return lax.all_to_all(packed, "z", split_axis=0, concat_axis=0, tiled=True)
+
+    def to_columns(arrived, first, last, live):
+        count = last - first
+        held = (
+            jnp.arange(n_planes, dtype=jnp.int32)[:, None] * n_columns * per_owner
+            + column * per_owner
+            + jnp.arange(per_owner, dtype=jnp.int32)[None, :]
+        )
+        blocks = jnp.transpose(arrived, (1, 0, 2, 3)).reshape(count, -1, KVBLK * kv_width)
+        order = block_order[first:last].reshape(count, n_planes, n_columns, per_owner)
+        order = lax.dynamic_index_in_dim(order, plane, 1, keepdims=False)
+        total = 0.0
+        for distance in range(n_columns):
+            target = (column + distance) % n_columns
+            wanted = lax.dynamic_index_in_dim(order, target, 1, keepdims=False)
+            pick = (wanted[..., None] == held.reshape(-1)).astype(jnp.bfloat16)
+            packed = jnp.einsum(
+                "tib,tbk->tik", pick, blocks, preferred_element_type=jnp.float32
+            ).astype(jnp.bfloat16)
+            if distance:
+                packed = turned(packed, distance, live)
+            total = total + packed.astype(jnp.float32)
+        return total.astype(jnp.bfloat16).reshape(count, span_dev, kv_width)
 
     tick_rows = []
-    delivered = []
     layer_in = jnp.zeros((span_dev, model_width), jnp.bfloat16)
+    early = None
     for tick in range(n_sections):
+        last_tick = tick + 1 == n_sections
+        live = tick + 1
         tokens = jnp.where(section_id == 0, spans[tick], layer_in)
         tick_rows.append(tokens)
         if tick == EARLY:
-            delivered.append(deliver_whole(0, EARLY))
+            early = deliver_whole(0, EARLY)
         normed_moe = rms_scale(tokens, moe_gain[0]).astype(jnp.bfloat16)
         chosen = jnp.dot(
             choose[tick], normed_moe, preferred_element_type=jnp.float32
         ).astype(jnp.bfloat16)
         arrived = lax.all_to_all(chosen, "z", split_axis=0, concat_axis=0, tiled=True)
-        token_rows = lax.all_gather(arrived, "y", axis=0, tiled=True)
-        parts = expert_slice(token_rows, local_gate, local_up, local_down)
-        quarters = lax.all_to_all(parts, "y", split_axis=0, concat_axis=0, tiled=True)
-        summed = jnp.sum(
-            quarters.reshape(n_columns, -1, model_width).astype(jnp.float32), axis=0
-        ).astype(jnp.bfloat16)
+        chunks = [arrived] + [turned(arrived, k, live) for k in range(1, n_columns)]
+        parts = expert_slice(chunks, local_gate, local_up, local_down)
+        summed = parts[0].astype(jnp.float32)
+        for k in range(1, n_columns):
+            summed = summed + turned(parts[k], n_columns - k, live).astype(jnp.float32)
+        summed = summed.astype(jnp.bfloat16)
+        if last_tick:
+            late = to_planes(EARLY, n_sections)
+            late = to_columns(late, EARLY, n_sections, live)
         returned = lax.all_to_all(summed, "z", split_axis=0, concat_axis=0, tiled=True)
         moe_sum = jnp.dot(
             weighting[tick], returned.astype(jnp.float32), precision=lax.Precision.HIGHEST
         )
         layer_out = (tokens.astype(jnp.float32) + moe_sum).astype(jnp.bfloat16)
-        if tick + 1 < n_sections:
+        if not last_tick:
             layer_in = shifted(layer_out, "section", 1)
-    delivered.append(deliver_planes(EARLY, n_sections))
+    delivered = [early, late]
     blank = jnp.zeros((n_spans, span_dev, kv_width), jnp.bfloat16)
     kv_ticks = jnp.concatenate(delivered + [blank], axis=0)
     kv_store = lax.dynamic_slice_in_dim(kv_ticks, section_id, n_spans, 0)

time: 608 us -> 704 us (1.16); the launches traced: 604 us -> 692 us
  blocking collectives: 301 us -> 102 us
  starting transfers between devices: 68 us -> 223 us
  waiting for transfers between devices: 113 us -> 225 us
  matrix products: 74.6 us -> 13 us
  local copies, waits for them, and re-layouts: 22.1 us -> 67.6 us
  Pallas kernels: 0 us -> 36.2 us
    ppermute x0 -> x51, starting transfers between devices: none -> 177 us  [turned(): return lax.ppermute(block, ('section', 'y'), route)]
    all_gather x9 -> x0, blocking collectives: 125 us -> none  [the longest x8 114 us: body(): token_rows = lax.all_gather(arrived, 'y', axis=0, tiled=True)]
    ppermute x0 -> x51, waiting for transfers between devices: none -> 121 us  [turned(): return lax.ppermute(block, ('section', 'y'), route)]
    dot_general x17 -> x4, matrix products: 61.7 us -> 0.86 us  [to_columns(): jnp.einsum('tib,tbk->tik', pick, blocks, preferred_element_type=jnp.float32)]
    unnamed x19 -> x64, local copies, waits for them, and re-layouts: 0.7 us -> 47.6 us
    all_to_all x3 -> x0, blocking collectives: 46.1 us -> none  [body(): lax.all_to_all(parts, 'y', split_axis=0, concat_axis=0, tiled=True)]
    pallas_call x0 -> x8, Pallas kernels: none -> 36.2 us  [expert_slice(): pl.pallas_call(lambda *refs: expert_kernel(n_chunks, rows, *refs), out_sh...]
    all_to_all x6 -> x1, waiting for transfers between devices: 35.6 us -> 3.32 us  [to_planes(): return lax.all_to_all(packed, 'z', split_axis=0, concat_axis=0, tiled=True)]
  transfers between devices with their start and end apart: 22 -> 70, of which waited for: 18 -> 55; matrix products, arithmetic and copies ran while one was open for 9% -> 3% of each run, Pallas kernels for 0% -> 2%
where the time goes in v2:
time: 704 us; the launch traced here: 692 us
  waiting for transfers between devices  225 us (32%)
  starting transfers between devices  223 us (32%)
  blocking collectives  102 us (14%)
  local copies, waits for them, and re-layouts  67.6 us (10%)
  Pallas kernels  36.2 us (5%)
  between operations  15.8 us (2%)
  matrix products  13 us (2%)
  other arithmetic  9.85 us (1%)
    ppermute x51, starting transfers between devices, turned(): return lax.ppermute(block, ('section', 'y'), route)  177 us
    ppermute x51, waiting for transfers between devices, turned(): return lax.ppermute(block, ('section', 'y'), route)  121 us
    all_to_all x4, blocking collectives, body(): lax.all_to_all(chosen, 'z', split_axis=0, concat_axis=0, tiled=True)  62.5 us
    all_to_all x5, waiting for transfers between devices, body(): lax.all_to_all(summed, 'z', split_axis=0, concat_axis=0, tiled=True)  48.7 us
    unnamed x64, local copies, waits for them, and re-layouts  47.6 us
    all_to_all x4, waiting for transfers between devices, body(): lax.all_to_all(chosen, 'z', split_axis=0, concat_axis=0, tiled=True)  45.7 us
    all_to_all x3, blocking collectives, body(): lax.all_to_all(summed, 'z', split_axis=0, concat_axis=0, tiled=True)  39.3 us
    pallas_call x8, Pallas kernels, expert_slice(): pl.pallas_call(lambda *refs: expert_kernel(n_chunks, rows, *refs), out_sh...  36.2 us
  transfers between devices with their start and end apart: 70, of which 55 were waited for; matrix products, arithmetic and copies ran while one was open for 3% of the time, Pallas kernels for 2%

profile of v2, /device:TPU:8, one launch (start us, length us, event | category | flops | bytes accessed | tf_op | source)
XLA Modules:
  0.0 691.9 jit_solution(9456529549074362836)
XLA Ops:
  11.3 19.4 %all_to_all.189 = bf16[8,4,3584]{2,1,0:T(4,128)(2,1)S(1)} all-to-all(bf16[8,4,3584]{2,1,0:T(4,128)(2,1)S(1)} %all_to_all.123), channel_id=1, replica_groups=mesh['section'=8,'z'=8,'y'=4] {'z'}, dimensions={0} | all-to-all | bytes 458752 | tf_op jit(solution)/shard_map/all_to_all | solution.py:262
  63.4 4.5 collective-permute-start.5
  76.2 9.5 %all-to-all-done.1 = bf16[8,4,3584]{2,1,0:T(4,128)(2,1)S(1)} async-done(((bf16[8,4,3584]{2,1,0:T(4,128)(2,1)}), bf16[8,4,3584]{2,1,0:T(4,128)(2,1)S(1)}, u32[]{:S(2)}, u32[]{:S(2)}) %all-to-all-start.1) | async-done | bytes 229408 | tf_op jit(solution)/shard_map/all_to_all | solution.py:272
  88.8 14.4 %all_to_all.190 = bf16[8,4,3584]{2,1,0:T(4,128)(2,1)S(1)} all-to-all(bf16[8,4,3584]{2,1,0:T(4,128)(2,1)S(1)} %all_to_all.129), channel_id=1, replica_groups=mesh['section'=8,'z'=8,'y'=4] {'z'}, dimensions={0} | all-to-all | bytes 458752 | tf_op jit(solution)/shard_map/all_to_all | solution.py:262
  107.6 4.6 collective-permute-start.8
  114.6 4.9 collective-permute-done.8.refs_2_
  152.2 12.9 %all_to_all.191 = bf16[8,4,3584]{2,1,0:T(4,128)(2,1)S(1)} all-to-all(bf16[8,4,3584]{2,1,0:T(4,128)(2,1)S(1)} %all_to_all.132), channel_id=1, replica_groups=mesh['section'=8,'z'=8,'y'=4] {'z'}, dimensions={0} | all-to-all | bytes 458752 | tf_op jit(solution)/shard_map/all_to_all | solution.py:272
  168.1 14.4 %all_to_all.192 = bf16[8,4,3584]{2,1,0:T(4,128)(2,1)S(1)} all-to-all(bf16[8,4,3584]{2,1,0:T(4,128)(2,1)S(1)} %all_to_all.135), channel_id=1, replica_groups=mesh['section'=8,'z'=8,'y'=4] {'z'}, dimensions={0} | all-to-all | bytes 458752 | tf_op jit(solution)/shard_map/all_to_all | solution.py:262
  186.5 6.4 collective-permute-start.15
  221.0 4.7 collective-permute-start.19
  232.8 13.2 %all_to_all.193 = bf16[8,4,3584]{2,1,0:T(4,128)(2,1)S(1)} all-to-all(bf16[8,4,3584]{2,1,0:T(4,128)(2,1)S(1)} %all_to_all.138), channel_id=1, replica_groups=mesh['section'=8,'z'=8,'y'=4] {'z'}, dimensions={0} | all-to-all | bytes 458752 | tf_op jit(solution)/shard_map/all_to_all | solution.py:272
  249.0 14.4 %all_to_all.194 = bf16[8,4,3584]{2,1,0:T(4,128)(2,1)S(1)} all-to-all(bf16[8,4,3584]{2,1,0:T(4,128)(2,1)S(1)} %all_to_all.141), channel_id=1, replica_groups=mesh['section'=8,'z'=8,'y'=4] {'z'}, dimensions={0} | all-to-all | bytes 458752 | tf_op jit(solution)/shard_map/all_to_all | solution.py:262
  267.3 6.3 collective-permute-start.22
  313.5 13.2 %all_to_all.195 = bf16[8,4,3584]{2,1,0:T(4,128)(2,1)S(1)} all-to-all(bf16[8,4,3584]{2,1,0:T(4,128)(2,1)S(1)} %all_to_all.144), channel_id=1, replica_groups=mesh['section'=8,'z'=8,'y'=4] {'z'}, dimensions={0} | all-to-all | bytes 458752 | tf_op jit(solution)/shard_map/all_to_all | solution.py:272
  334.5 11.1 %all-to-all-done.8 = bf16[8,4,3584]{2,1,0:T(4,128)(2,1)S(1)} async-done(((bf16[8,4,3584]{2,1,0:T(4,128)(2,1)}), bf16[8,4,3584]{2,1,0:T(4,128)(2,1)S(1)}, u32[]{:S(2)}, u32[]{:S(2)}) %all-to-all-start.8) | async-done | bytes 229408 | tf_op jit(solution)/shard_map/all_to_all | solution.py:262
  349.6 6.3 collective-permute-start.29
  363.0 4.6 collective-permute-done.30.refs_3_
  389.7 6.4 collective-permute-done.32
  396.1 7.6 %collective-permute-done.33 = bf16[32,3584]{1,0:T(8,128)(2,1)S(1)} collective-permute-done((bf16[32,3584]{1,0:T(8,128)(2,1)S(1)}, bf16[32,3584]{1,0:T(8,128)(2,1)S(1)}, u32[]{:S(2)}, u32[]{:S(2)}) %collective-permute-start.33) | collective-permute-done | bytes 229408 | tf_op jit(solution)/shard_map/ppermute | solution.py:29
  408.2 12.8 %all-to-all-done.9 = bf16[8,4,3584]{2,1,0:T(4,128)(2,1)S(1)} async-done(((bf16[8,4,3584]{2,1,0:T(4,128)(2,1)}), bf16[8,4,3584]{2,1,0:T(4,128)(2,1)S(1)}, u32[]{:S(2)}, u32[]{:S(2)}) %all-to-all-start.9) | async-done | bytes 229408 | tf_op jit(solution)/shard_map/all_to_all | solution.py:272
  428.4 11.6 %all-to-all-done.10 = bf16[8,4,3584]{2,1,0:T(4,128)(2,1)S(1)} async-done(((bf16[8,4,3584]{2,1,0:T(4,128)(2,1)}), bf16[8,4,3584]{2,1,0:T(4,128)(2,1)S(1)}, u32[]{:S(2)}, u32[]{:S(2)}) %all-to-all-start.10) | async-done | bytes 229408 | tf_op jit(solution)/shard_map/all_to_all | solution.py:262
  443.5 5.0 collective-permute-start.36
  476.6 4.7 collective-permute-start.40
  492.5 10.7 %all-to-all-done.11 = bf16[8,4,3584]{2,1,0:T(4,128)(2,1)S(1)} async-done(((bf16[8,4,3584]{2,1,0:T(4,128)(2,1)}), bf16[8,4,3584]{2,1,0:T(4,128)(2,1)S(1)}, u32[]{:S(2)}, u32[]{:S(2)}) %all-to-all-start.11) | async-done | bytes 229408 | tf_op jit(solution)/shard_map/all_to_all | solution.py:272
  510.8 11.4 %all-to-all-done.12 = bf16[8,4,3584]{2,1,0:T(4,128)(2,1)S(1)} async-done(((bf16[8,4,3584]{2,1,0:T(4,128)(2,1)}), bf16[8,4,3584]{2,1,0:T(4,128)(2,1)S(1)}, u32[]{:S(2)}, u32[]{:S(2)}) %all-to-all-start.12) | async-done | bytes 229408 | tf_op jit(solution)/shard_map/all_to_all | solution.py:262
  526.0 6.3 collective-permute-start.43
  574.4 10.6 %all-to-all-done.13 = bf16[8,4,3584]{2,1,0:T(4,128)(2,1)S(1)} async-done(((bf16[8,4,3584]{2,1,0:T(4,128)(2,1)}), bf16[8,4,3584]{2,1,0:T(4,128)(2,1)S(1)}, u32[]{:S(2)}, u32[]{:S(2)}) %all-to-all-start.13) | async-done | bytes 229408 | tf_op jit(solution)/shard_map/all_to_all | solution.py:272
  596.7 11.6 %all-to-all-done.14 = bf16[8,4,3584]{2,1,0:T(4,128)(2,1)S(1)} async-done(((bf16[8,4,3584]{2,1,0:T(4,128)(2,1)}), bf16[8,4,3584]{2,1,0:T(4,128)(2,1)S(1)}, u32[]{:S(2)}, u32[]{:S(2)}) %all-to-all-start.14) | async-done | bytes 229408 | tf_op jit(solution)/shard_map/all_to_all | solution.py:262
  649.7 5.5 collective-permute-done.53
  657.2 6.1 all-to-all-start.15
  668.7 5.1 all-to-all-done.15
  674.7 4.6 reshape.333
  (352 shorter events, 391.4 us)
Async XLA Ops:
  72.3 13.4 %all-to-all-start.1 = ((bf16[8,4,3584]{2,1,0:T(4,128)(2,1)}), bf16[8,4,3584]{2,1,0:T(4,128)(2,1)S(1)}, u32[]{:S(2)}, u32[]{:S(2)}) async-start(bf16[8,4,3584]{2,1,0:T(4,128)(2,1)} %all_to_all.126), calls=%async_computation.1 | async-start | bytes 458752 | tf_op jit(solution)/shard_map/all_to_all | solution.py:272
  136.9 12.2 %collective-permute-start.11 = (bf16[32,3584]{1,0:T(8,128)(2,1)S(1)}, bf16[32,3584]{1,0:T(8,128)(2,1)S(1)}, u32[]{:S(2)}, u32[]{:S(2)}) collective-permute-start(bf16[32,3584]{1,0:T(8,128)(2,1)S(1)} %get-tuple-element.40), channel_id=1, source_target_pairs={{0,2},{1,3},{2,0},{3,1},{32,34},{33,35},{34,32},{35,33},{4,6},{5,7... | collective-permute-start | bytes 688136 | tf_op jit(solution)/shard_map/ppermute | solution.py:29
  182.5 12.8 %collective-permute-start.14 = (bf16[32,3584]{1,0:T(8,128)(2,1)S(1)}, bf16[32,3584]{1,0:T(8,128)(2,1)S(1)}, u32[]{:S(2)}, u32[]{:S(2)}) collective-permute-start(bf16[32,3584]{1,0:T(8,128)(2,1)S(1)} %all_to_all.137.refs_0_), channel_id=1, source_target_pairs={{0,1},{1,2},{2,3},{3,0},{32,33},{33,34},{34,35},{35,32},{64,65},{6... | collective-permute-start | bytes 688136 | tf_op jit(solution)/shard_map/ppermute | solution.py:29
  186.5 12.8 %collective-permute-start.15 = (bf16[32,3584]{1,0:T(8,128)(2,1)S(1)}, bf16[32,3584]{1,0:T(8,128)(2,1)S(1)}, u32[]{:S(2)}, u32[]{:S(2)}) collective-permute-start(bf16[32,3584]{1,0:T(8,128)(2,1)S(1)} %all_to_all.137.refs_0_), channel_id=1, source_target_pairs={{0,2},{1,3},{2,0},{3,1},{32,34},{33,35},{34,32},{35,33},{64,66},{6... | collective-permute-start | bytes 688136 | tf_op jit(solution)/shard_map/ppermute | solution.py:29
  217.7 12.2 %collective-permute-start.18 = (bf16[32,3584]{1,0:T(8,128)(2,1)S(1)}, bf16[32,3584]{1,0:T(8,128)(2,1)S(1)}, u32[]{:S(2)}, u32[]{:S(2)}) collective-permute-start(bf16[32,3584]{1,0:T(8,128)(2,1)S(1)} %get-tuple-element.44), channel_id=1, source_target_pairs={{0,2},{1,3},{2,0},{3,1},{32,34},{33,35},{34,32},{35,33},{64,66},{6... | collective-permute-start | bytes 688136 | tf_op jit(solution)/shard_map/ppermute | solution.py:29
  263.5 12.5 %collective-permute-start.21 = (bf16[32,3584]{1,0:T(8,128)(2,1)S(1)}, bf16[32,3584]{1,0:T(8,128)(2,1)S(1)}, u32[]{:S(2)}, u32[]{:S(2)}) collective-permute-start(bf16[32,3584]{1,0:T(8,128)(2,1)S(1)} %all_to_all.143.refs_0_), channel_id=1, source_target_pairs={{0,1},{1,2},{2,3},{3,0},{32,33},{33,34},{34,35},{35,32},{64,65},{6... | collective-permute-start | bytes 688136 | tf_op jit(solution)/shard_map/ppermute | solution.py:29
  267.3 12.7 %collective-permute-start.22 = (bf16[32,3584]{1,0:T(8,128)(2,1)S(1)}, bf16[32,3584]{1,0:T(8,128)(2,1)S(1)}, u32[]{:S(2)}, u32[]{:S(2)}) collective-permute-start(bf16[32,3584]{1,0:T(8,128)(2,1)S(1)} %all_to_all.143.refs_0_), channel_id=1, source_target_pairs={{0,2},{1,3},{2,0},{3,1},{32,34},{33,35},{34,32},{35,33},{64,66},{6... | collective-permute-start | bytes 688136 | tf_op jit(solution)/shard_map/ppermute | solution.py:29
  298.3 12.2 %collective-permute-start.25 = (bf16[32,3584]{1,0:T(8,128)(2,1)S(1)}, bf16[32,3584]{1,0:T(8,128)(2,1)S(1)}, u32[]{:S(2)}, u32[]{:S(2)}) collective-permute-start(bf16[32,3584]{1,0:T(8,128)(2,1)S(1)} %get-tuple-element.48), channel_id=1, source_target_pairs={{0,2},{1,3},{2,0},{3,1},{32,34},{33,35},{34,32},{35,33},{64,66},{6... | collective-permute-start | bytes 688136 | tf_op jit(solution)/shard_map/ppermute | solution.py:29
  330.4 15.3 %all-to-all-start.8 = ((bf16[8,4,3584]{2,1,0:T(4,128)(2,1)}), bf16[8,4,3584]{2,1,0:T(4,128)(2,1)S(1)}, u32[]{:S(2)}, u32[]{:S(2)}) async-start(bf16[8,4,3584]{2,1,0:T(4,128)(2,1)} %all_to_all.147), calls=%async_computation.8 | async-start | bytes 458752 | tf_op jit(solution)/shard_map/all_to_all | solution.py:262
  333.8 200.4 %all-gather.6.cloned.1.call-start = ((), (), s32[]{:S(2)}) async-start(), calls=%async_computation.18 | async-start | bytes 4730880 | tf_op jit(solution)/shard_map/all_gather | solution.py:171
  345.8 13.8 %collective-permute-start.28 = (bf16[32,3584]{1,0:T(8,128)(2,1)S(1)}, bf16[32,3584]{1,0:T(8,128)(2,1)S(1)}, u32[]{:S(2)}, u32[]{:S(2)}) collective-permute-start(bf16[32,3584]{1,0:T(8,128)(2,1)S(1)} %all_to_all.149.refs_0_), channel_id=1, source_target_pairs={{0,1},{1,2},{2,3},{3,0},{32,33},{33,34},{34,35},{35,32},{64,65},{6... | collective-permute-start | bytes 688136 | tf_op jit(solution)/shard_map/ppermute | solution.py:29
  349.6 13.5 %collective-permute-start.29 = (bf16[32,3584]{1,0:T(8,128)(2,1)S(1)}, bf16[32,3584]{1,0:T(8,128)(2,1)S(1)}, u32[]{:S(2)}, u32[]{:S(2)}) collective-permute-start(bf16[32,3584]{1,0:T(8,128)(2,1)S(1)} %all_to_all.149.refs_0_), channel_id=1, source_target_pairs={{0,2},{1,3},{2,0},{3,1},{32,34},{33,35},{34,32},{35,33},{64,66},{6... | collective-permute-start | bytes 688136 | tf_op jit(solution)/shard_map/ppermute | solution.py:29
  381.9 14.2 %collective-permute-start.32 = (bf16[32,3584]{1,0:T(8,128)(2,1)S(1)}, bf16[32,3584]{1,0:T(8,128)(2,1)S(1)}, u32[]{:S(2)}, u32[]{:S(2)}) collective-permute-start(bf16[32,3584]{1,0:T(8,128)(2,1)S(1)} %get-tuple-element.52), channel_id=1, source_target_pairs={{0,2},{1,3},{2,0},{3,1},{32,34},{33,35},{34,32},{35,33},{64,66},{6... | collective-permute-start | bytes 688136 | tf_op jit(solution)/shard_map/ppermute | solution.py:29
  385.2 18.6 %collective-permute-start.33 = (bf16[32,3584]{1,0:T(8,128)(2,1)S(1)}, bf16[32,3584]{1,0:T(8,128)(2,1)S(1)}, u32[]{:S(2)}, u32[]{:S(2)}) collective-permute-start(bf16[32,3584]{1,0:T(8,128)(2,1)S(1)} %get-tuple-element.53), channel_id=1, source_target_pairs={{0,1},{1,2},{2,3},{3,0},{32,33},{33,34},{34,35},{35,32},{64,65},{6... | collective-permute-start | bytes 688136 | tf_op jit(solution)/shard_map/ppermute | solution.py:29
  404.6 16.3 %all-to-all-start.9 = ((bf16[8,4,3584]{2,1,0:T(4,128)(2,1)}), bf16[8,4,3584]{2,1,0:T(4,128)(2,1)S(1)}, u32[]{:S(2)}, u32[]{:S(2)}) async-start(bf16[8,4,3584]{2,1,0:T(4,128)(2,1)} %all_to_all.150), calls=%async_computation.9 | async-start | bytes 458752 | tf_op jit(solution)/shard_map/all_to_all | solution.py:272
  424.7 15.3 %all-to-all-start.10 = ((bf16[8,4,3584]{2,1,0:T(4,128)(2,1)}), bf16[8,4,3584]{2,1,0:T(4,128)(2,1)S(1)}, u32[]{:S(2)}, u32[]{:S(2)}) async-start(bf16[8,4,3584]{2,1,0:T(4,128)(2,1)} %all_to_all.153), calls=%async_computation.10 | async-start | bytes 458752 | tf_op jit(solution)/shard_map/all_to_all | solution.py:262
  469.7 11.9 %collective-permute-start.38 = (bf16[32,3584]{1,0:T(8,128)(2,1)S(1)}, bf16[32,3584]{1,0:T(8,128)(2,1)S(1)}, u32[]{:S(2)}, u32[]{:S(2)}) collective-permute-start(bf16[32,3584]{1,0:T(8,128)(2,1)S(1)} %get-tuple-element.55), channel_id=1, source_target_pairs={{0,3},{1,0},{2,1},{3,2},{32,35},{33,32},{34,33},{35,34},{64,67},{6... | collective-permute-start | bytes 688136 | tf_op jit(solution)/shard_map/ppermute | solution.py:29
  473.3 12.1 %collective-permute-start.39 = (bf16[32,3584]{1,0:T(8,128)(2,1)S(1)}, bf16[32,3584]{1,0:T(8,128)(2,1)S(1)}, u32[]{:S(2)}, u32[]{:S(2)}) collective-permute-start(bf16[32,3584]{1,0:T(8,128)(2,1)S(1)} %get-tuple-element.56), channel_id=1, source_target_pairs={{0,2},{1,3},{2,0},{3,1},{32,34},{33,35},{34,32},{35,33},{64,66},{6... | collective-permute-start | bytes 688136 | tf_op jit(solution)/shard_map/ppermute | solution.py:29
  489.1 14.1 %all-to-all-start.11 = ((bf16[8,4,3584]{2,1,0:T(4,128)(2,1)}), bf16[8,4,3584]{2,1,0:T(4,128)(2,1)S(1)}, u32[]{:S(2)}, u32[]{:S(2)}) async-start(bf16[8,4,3584]{2,1,0:T(4,128)(2,1)} %all_to_all.156), calls=%async_computation.11 | async-start | bytes 458752 | tf_op jit(solution)/shard_map/all_to_all | solution.py:272
  506.9 15.3 %all-to-all-start.12 = ((bf16[8,4,3584]{2,1,0:T(4,128)(2,1)}), bf16[8,4,3584]{2,1,0:T(4,128)(2,1)S(1)}, u32[]{:S(2)}, u32[]{:S(2)}) async-start(bf16[8,4,3584]{2,1,0:T(4,128)(2,1)} %all_to_all.159), calls=%async_computation.12 | async-start | bytes 458752 | tf_op jit(solution)/shard_map/all_to_all | solution.py:262
  522.2 15.5 %collective-permute-start.42 = (bf16[32,3584]{1,0:T(8,128)(2,1)S(1)}, bf16[32,3584]{1,0:T(8,128)(2,1)S(1)}, u32[]{:S(2)}, u32[]{:S(2)}) collective-permute-start(bf16[32,3584]{1,0:T(8,128)(2,1)S(1)} %all_to_all.161.refs_0_), channel_id=1, source_target_pairs={{0,1},{1,2},{2,3},{3,0},{32,33},{33,34},{34,35},{35,32},{64,65},{6... | collective-permute-start | bytes 688136 | tf_op jit(solution)/shard_map/ppermute | solution.py:29
  526.0 12.7 %collective-permute-start.43 = (bf16[32,3584]{1,0:T(8,128)(2,1)S(1)}, bf16[32,3584]{1,0:T(8,128)(2,1)S(1)}, u32[]{:S(2)}, u32[]{:S(2)}) collective-permute-start(bf16[32,3584]{1,0:T(8,128)(2,1)S(1)} %all_to_all.161.refs_0_), channel_id=1, source_target_pairs={{0,2},{1,3},{2,0},{3,1},{32,34},{33,35},{34,32},{35,33},{64,66},{6... | collective-permute-start | bytes 688136 | tf_op jit(solution)/shard_map/ppermute | solution.py:29
  555.0 12.2 %collective-permute-start.46 = (bf16[32,3584]{1,0:T(8,128)(2,1)S(1)}, bf16[32,3584]{1,0:T(8,128)(2,1)S(1)}, u32[]{:S(2)}, u32[]{:S(2)}) collective-permute-start(bf16[32,3584]{1,0:T(8,128)(2,1)S(1)} %get-tuple-element.60), channel_id=1, source_target_pairs={{0,2},{1,3},{2,0},{3,1},{32,34},{33,35},{34,32},{35,33},{64,66},{6... | collective-permute-start | bytes 688136 | tf_op jit(solution)/shard_map/ppermute | solution.py:29
  570.9 14.1 %all-to-all-start.13 = ((bf16[8,4,3584]{2,1,0:T(4,128)(2,1)}), bf16[8,4,3584]{2,1,0:T(4,128)(2,1)S(1)}, u32[]{:S(2)}, u32[]{:S(2)}) async-start(bf16[8,4,3584]{2,1,0:T(4,128)(2,1)} %all_to_all.162), calls=%async_computation.13 | async-start | bytes 458752 | tf_op jit(solution)/shard_map/all_to_all | solution.py:272
  574.3 100.5 %all-gather.4.cloned.1.call-start = ((), (), s32[]{:S(2)}) async-start(), calls=%async_computation.17 | async-start | bytes 2027520 | tf_op jit(solution)/shard_map/all_gather | solution.py:207
  592.4 15.8 %all-to-all-start.14 = ((bf16[8,4,3584]{2,1,0:T(4,128)(2,1)}), bf16[8,4,3584]{2,1,0:T(4,128)(2,1)S(1)}, u32[]{:S(2)}, u32[]{:S(2)}) async-start(bf16[8,4,3584]{2,1,0:T(4,128)(2,1)} %all_to_all.165), calls=%async_computation.14 | async-start | bytes 458752 | tf_op jit(solution)/shard_map/all_to_all | solution.py:262
  608.2 13.4 %all-to-all-start.16 = ((bf16[8,2,2,2304]{3,2,1,0:T(2,128)(2,1)}), bf16[8,2,2,2304]{3,2,1,0:T(2,128)(2,1)S(1)}, u32[]{:S(2)}, u32[]{:S(2)}) async-start(bf16[8,2,2,2304]{3,2,1,0:T(2,128)(2,1)} %broadcast_multiply_fusion), calls=%async_computation.16 | async-start | bytes 294912 | tf_op jit(solution)/shard_map/all_to_all | solution.py:223
  641.0 14.2 %collective-permute-start.53 = (bf16[32,3584]{1,0:T(8,128)(2,1)S(1)}, bf16[32,3584]{1,0:T(8,128)(2,1)S(1)}, u32[]{:S(2)}, u32[]{:S(2)}) collective-permute-start(bf16[32,3584]{1,0:T(8,128)(2,1)S(1)} %get-tuple-element.64), channel_id=1, source_target_pairs={{0,2},{1,3},{2,0},{3,1},{32,34},{33,35},{34,32},{35,33},{64,66},{6... | collective-permute-start | bytes 688136 | tf_op jit(solution)/shard_map/ppermute | solution.py:29
  642.3 14.1 %collective-permute-start.54 = (bf16[32,3584]{1,0:T(8,128)(2,1)S(1)}, bf16[32,3584]{1,0:T(8,128)(2,1)S(1)}, u32[]{:S(2)}, u32[]{:S(2)}) collective-permute-start(bf16[32,3584]{1,0:T(8,128)(2,1)S(1)} %get-tuple-element.65), channel_id=1, source_target_pairs={{0,1},{1,2},{2,3},{3,0},{32,33},{33,34},{34,35},{35,32},{64,65},{6... | collective-permute-start | bytes 688136 | tf_op jit(solution)/shard_map/ppermute | solution.py:29
  645.0 22.7 %collective-permute-start.55 = (bf16[2,2,2304]{2,1,0:T(2,128)(2,1)S(1)}, bf16[2,2,2304]{2,1,0:T(2,128)(2,1)S(1)}, u32[]{:S(2)}, u32[]{:S(2)}) collective-permute-start(bf16[2,2,2304]{2,1,0:T(2,128)(2,1)S(1)} %convolution_convert_fusion.10), channel_id=1, source_target_pairs={{0,1},{1,2},{2,3},{3,0},{32,33},{33,34},{34,35},{35,32},{64,65},{6... | collective-permute-start | bytes 55304 | tf_op jit(solution)/shard_map/ppermute | solution.py:29
  645.6 22.1 %collective-permute-start.56 = (bf16[2,2,2304]{2,1,0:T(2,128)(2,1)S(1)}, bf16[2,2,2304]{2,1,0:T(2,128)(2,1)S(1)}, u32[]{:S(2)}, u32[]{:S(2)}) collective-permute-start(bf16[2,2,2304]{2,1,0:T(2,128)(2,1)S(1)} %convolution_convert_fusion.9), channel_id=1, source_target_pairs={{0,2},{1,3},{2,0},{3,1},{32,34},{33,35},{34,32},{35,33},{64,66},{6... | collective-permute-start | bytes 55304 | tf_op jit(solution)/shard_map/ppermute | solution.py:29
  657.2 16.5 %all-to-all-start.15 = ((bf16[8,4,3584]{2,1,0:T(4,128)(2,1)}), bf16[8,4,3584]{2,1,0:T(4,128)(2,1)S(1)}, u32[]{:S(2)}, u32[]{:S(2)}) async-start(bf16[8,4,3584]{2,1,0:T(4,128)(2,1)} %all_to_all.168), calls=%async_computation.15 | async-start | bytes 458752 | tf_op jit(solution)/shard_map/all_to_all | solution.py:272
  (69 other events, 671.7 us)
Sparse Core Ops, SparseCore 0:
  337.2 90.4 all-gather.5
  587.5 72.2 all-gather.3

commit v3 on v1

v3 whole, which is shorter than its diff:
```python
import jax
import jax.numpy as jnp
from jax import lax
from jax.experimental import pallas as pl
from jax.experimental.pallas import tpu as pltpu
from jax.sharding import Mesh, PartitionSpec as P

LAT = 512
EXP_SPLIT = 4
TOPK = 2
KVBLK = 4
EARLY = 7


eps = 1e-06


def shifted(block, axis, distance):
    devices = range(lax.axis_size(axis))
    route = [(i - distance, i) for i in devices if i - distance in devices]
    return lax.ppermute(block, axis, route)


def rms_scale(values, gain_vec):
    values = values.astype(jnp.float32)
    return values * lax.rsqrt(jnp.mean(values * values, axis=-1, keepdims=True) + eps) * gain_vec


def rotate_pairs(rope_part, positions):
    half_dim = rope_part.shape[-1] // 2
    frequency = 10000.0 ** (-jnp.arange(half_dim, dtype=jnp.float32) / half_dim)
    angles = positions.astype(jnp.float32)[:, None] * frequency[None, :]
    cosine = jnp.cos(angles)
    sine_part = jnp.sin(angles)
    first_half = rope_part[:, :half_dim]
    second = rope_part[:, half_dim:]
    return jnp.concatenate(
        [first_half * cosine - second * sine_part, second * cosine + first_half * sine_part], axis=1
    )


def latent_rows(latent, gain_vec, positions):
    compressed = rms_scale(latent[:, :LAT], gain_vec)
    rotated = rotate_pairs(latent[:, LAT:], positions)
    return jnp.concatenate([compressed, rotated], axis=1).astype(jnp.bfloat16)


def packing(route_ids, expert_list, capacity):
    matches = route_ids[:, :, None, :] == expert_list[None, None, :, None]
    picked = jnp.any(matches, axis=3).astype(jnp.int32)
    slot_rank = jnp.cumsum(picked, axis=1) - 1
    slot_ids = jnp.arange(capacity, dtype=jnp.int32)
    slot_table = (slot_rank[..., None] == slot_ids) & (picked[..., None] > 0)
    return jnp.transpose(slot_table, (0, 2, 3, 1))


def one_hot(rows, cols, wanted, kept=None):
    row = lax.broadcasted_iota(jnp.int32, (rows, cols), 0)
    col = lax.broadcasted_iota(jnp.int32, (rows, cols), 1)
    hit = col == wanted(row)
    if kept is not None:
        hit = hit & kept(row)
    return jnp.where(hit, 1.0, 0.0).astype(jnp.bfloat16)


def matmul(left, right):
    return jnp.dot(left, right, preferred_element_type=jnp.float32)


def in_vmem(kernel, out_shape, operands, limit_mib, flops=0, tick=None, tables=()):
    moved = sum(x.size * x.dtype.itemsize for x in operands)
    specs = [pl.BlockSpec(memory_space=pltpu.VMEM)] * len(operands)
    for table in tables:
        specs.append(pl.BlockSpec((1,) + table.shape[1:], lambda i: (tick, 0, 0)))
    return pl.pallas_call(
        kernel,
        grid=(1,),
        out_shape=out_shape,
        in_specs=specs,
        out_specs=pl.BlockSpec(memory_space=pltpu.VMEM),
        compiler_params=pltpu.CompilerParams(vmem_limit_bytes=limit_mib * 1024 * 1024),
        cost_estimate=pl.CostEstimate(flops=flops, bytes_accessed=moved, transcendentals=0),
    )(*operands, *tables)


def choose_kernel(tokens, gain, first, second, out):
    half = out.shape[1]
    normed = rms_scale(tokens[...], gain[...]).astype(jnp.bfloat16).astype(jnp.float32)
    picked = matmul(first[0], normed[:, :half]) + matmul(second[0], normed[:, half:])
    out[...] = picked.astype(jnp.bfloat16)


def expert_kernel(tokens, w_gate, w_up, w_down, out):
    folded, half = tokens.shape
    slots = folded // 2
    place = lambda row: (row // 4) * 8 + row % 4
    first = matmul(one_hot(slots, folded, place), tokens[...]).astype(jnp.bfloat16)
    second = matmul(one_hot(slots, folded, lambda row: place(row) + 4), tokens[...])
    second = second.astype(jnp.bfloat16)
    gate_proj = matmul(first, w_gate[:half, :]) + matmul(second, w_gate[half:, :])
    up_proj = matmul(first, w_up[:half, :]) + matmul(second, w_up[half:, :])
    hidden = (gate_proj / (1.0 + jnp.exp(-gate_proj)) * up_proj).astype(jnp.bfloat16)
    width = 512
    for start in range(0, 2 * half, width):
        cols = slice(start, start + width)
        out[:, cols] = matmul(hidden, w_down[:, cols]).astype(jnp.bfloat16)


def total_kernel(parts, quarters, out):
    folded, half = out.shape
    slots = folded // 2
    total = quarters[:slots, :].astype(jnp.float32)
    for k in range(1, parts):
        total = total + quarters[k * slots : (k + 1) * slots, :].astype(jnp.float32)
    total = total.astype(jnp.bfloat16)
    place = lambda row: (row // 8) * 4 + row % 4
    first = one_hot(folded, slots, place, lambda row: row % 8 < 4)
    second = one_hot(folded, slots, place, lambda row: row % 8 >= 4)
    spread = matmul(first, total[:, :half]) + matmul(second, total[:, half:])
    out[...] = spread.astype(jnp.bfloat16)


def combine_kernel(tokens, returned, first, second, out):
    half = returned.shape[1]
    rows = returned[...].astype(jnp.float32)
    for weights, cols in ((first, slice(0, half)), (second, slice(half, 2 * half))):
        moe_sum = jnp.dot(
            weights[0],
            rows,
            precision=lax.Precision.HIGHEST,
            preferred_element_type=jnp.float32,
        )
        out[:, cols] = (tokens[:, cols].astype(jnp.float32) + moe_sum).astype(jnp.bfloat16)


def body(
    spans,
    attn_gain,
    kv_gain,
    moe_gain,
    w_latent,
    w_gate,
    w_up,
    w_down,
    expert_ids,
    gate_vals,
    owner_map,
    offsets,
):
    section_id = lax.axis_index("section")
    plane = lax.axis_index("z")
    column = lax.axis_index("y")
    n_planes = lax.axis_size("z")
    n_columns = lax.axis_size("y")
    member = plane * n_columns + column
    n_members = n_planes * n_columns
    n_sections = lax.axis_size("section")
    n_spans, span_dev, model_width = spans.shape
    kv_width = w_latent.shape[2]
    experts = n_members // EXP_SPLIT
    capacity = min(span_dev, 2 * span_dev * TOPK // experts)
    per_owner = span_dev // KVBLK
    all_experts = jnp.arange(experts, dtype=jnp.int32)
    local_gate = w_gate[0]
    local_up = w_up[0]
    local_down = w_down[0]
    latent_full = lax.all_gather(w_latent[0], ("z", "y"), axis=0, tiled=True)

    def by_tick(values):
        padded = jnp.concatenate([jnp.zeros_like(values), values], axis=0)
        return lax.dynamic_slice_in_dim(padded, n_spans - section_id, n_sections, 0)

    own_ids = by_tick(lax.dynamic_slice_in_dim(expert_ids[0], member * span_dev, span_dev, 1))
    gate_rows = by_tick(gate_vals[0])
    own_table = packing(own_ids, all_experts, capacity)
    gate_for = jnp.sum(
        jnp.where(
            own_ids[..., None] == all_experts[None, None, None, :], gate_rows[..., None], 0.0
        ),
        axis=2,
    )
    weighting = own_table.astype(jnp.float32) * jnp.transpose(gate_for, (0, 2, 1))[:, :, None, :]
    no_slot = jnp.zeros_like(weighting)

    def folded(first, second):
        return jnp.concatenate([first, second], axis=2).reshape(n_sections, -1, span_dev)

    chooses = own_table.astype(jnp.float32)
    choose_first, choose_second = folded(chooses, no_slot), folded(no_slot, chooses)
    weigh_first = jnp.transpose(folded(weighting, no_slot), (0, 2, 1))
    weigh_second = jnp.transpose(folded(no_slot, weighting), (0, 2, 1))
    positions = (
        by_tick(offsets)[:, None]
        + member * span_dev
        + jnp.arange(span_dev, dtype=jnp.int32)[None, :]
    )
    block_order = by_tick(owner_map[0])

    def project(first, last):
        rows = jnp.concatenate(tick_rows[first:last], axis=0)
        normed = rms_scale(rows, attn_gain[0]).astype(jnp.bfloat16)
        latent = jnp.dot(normed, latent_full, preferred_element_type=jnp.float32)
        return latent_rows(latent, kv_gain[0], positions[first:last].reshape(-1))

    def owned_rows(order):
        block = jnp.repeat(order, KVBLK, axis=-1)
        return block * KVBLK + jnp.arange(block.shape[-1], dtype=jnp.int32) % KVBLK

    def deliver_whole(kv_rows, first, last):
        count = last - first
        gathered = lax.all_gather(kv_rows, ("z", "y"), axis=0)
        gathered = gathered.reshape(n_members, count, span_dev, kv_width)
        order = lax.dynamic_slice_in_dim(
            block_order[first:last], member * per_owner, per_owner, 1
        )
        every = jnp.arange(n_members * span_dev, dtype=jnp.int32)
        pick = (owned_rows(order)[..., None] == every).astype(jnp.bfloat16)
        pick = pick.reshape(count, span_dev, n_members, span_dev)
        return jnp.einsum(
            "tdmr,mtrk->tdk", pick, gathered, preferred_element_type=jnp.float32
        ).astype(jnp.bfloat16)

    def side_by_side(rows):
        wide = [rows[..., i : i + 8, :] for i in range(0, rows.shape[-2], 8)]
        wide = jnp.concatenate(wide, axis=-1)
        spare = model_width // 2 - wide.shape[-1]
        return jnp.pad(wide, [(0, 0)] * (wide.ndim - 1) + [(0, spare)])

    def apart(wide, count):
        pieces = [wide[..., i * kv_width : (i + 1) * kv_width] for i in range(count)]
        return jnp.concatenate(pieces, axis=-2)

    def pack_late(column_rows, first, last):
        count = last - first
        order = block_order[first:last].reshape(count, n_planes, n_columns, per_owner)
        order = lax.dynamic_index_in_dim(order, column, 2, keepdims=False)
        wanted = jnp.transpose(owned_rows(order), (1, 0, 2))
        col = jnp.arange(n_columns, dtype=jnp.int32)[:, None, None]
        tick = jnp.arange(count, dtype=jnp.int32)[None, :, None]
        row = jnp.arange(span_dev, dtype=jnp.int32)[None, None, :]
        held = (plane * n_columns + col) * span_dev + row + 0 * tick
        same = tick + 0 * held == jnp.arange(count, dtype=jnp.int32)[:, None, None, None]
        hit = (wanted[..., None, None, None] == held) & same[:, None]
        hit = hit.reshape(n_planes * count * span_dev, -1).astype(jnp.bfloat16)
        source = column_rows.reshape(-1, kv_width)
        packed = matmul(hit, source).astype(jnp.bfloat16)
        return side_by_side(packed.reshape(n_planes, count * span_dev, kv_width))

    def unpack_late(arrived, first, last):
        count = last - first
        rows = jnp.sum(arrived.astype(jnp.float32), axis=0).astype(jnp.bfloat16)
        return apart(rows, count).reshape(count, span_dev, kv_width)

    half = model_width // 2
    slots = experts * capacity
    tick_rows = []
    layer_in = jnp.zeros((span_dev, model_width), jnp.bfloat16)
    early = None
    flops = 2 * 3 * n_columns * slots * model_width * local_gate.shape[1]
    for tick in range(n_sections):
        last_tick = tick + 1 == n_sections
        tokens = jnp.where(section_id == 0, spans[tick], layer_in)
        tick_rows.append(tokens)
        if tick == 0:
            held = (tokens, choose_first, choose_second, weigh_first, weigh_second)
            held = lax.optimization_barrier(held)
            tokens, choose_first, choose_second, weigh_first, weigh_second = held
        if tick == 2:
            tokens, latent_full = lax.optimization_barrier((tokens, latent_full))
        if tick == EARLY - 1:
            early_rows = project(0, EARLY)
            tokens, early_rows = lax.optimization_barrier((tokens, early_rows))
            early = deliver_whole(early_rows, 0, EARLY)
        chosen = in_vmem(
            choose_kernel,
            jax.ShapeDtypeStruct((2 * slots, half), jnp.bfloat16),
            (tokens, moe_gain),
            8,
            tick=tick,
            tables=(choose_first, choose_second),
        )
        arrived = lax.all_to_all(chosen, "z", split_axis=0, concat_axis=0, tiled=True)
        if last_tick:
            late_rows = side_by_side(project(EARLY, n_sections))
            arrived = jnp.concatenate([arrived, late_rows], axis=0)
        token_rows = lax.all_gather(arrived, "y", axis=0, tiled=True)
        if last_tick:
            token_rows = token_rows.reshape(n_columns, -1, half)
            late_rows = apart(token_rows[:, 2 * slots :], n_sections - EARLY)
            token_rows = token_rows[:, : 2 * slots].reshape(-1, half)
        parts = in_vmem(
            expert_kernel,
            jax.ShapeDtypeStruct((n_columns * slots, model_width), jnp.bfloat16),
            (token_rows, local_gate, local_up, local_down),
            24,
            flops,
        )
        quarters = lax.all_to_all(parts, "y", split_axis=0, concat_axis=0, tiled=True)
        summed = in_vmem(
            lambda *refs: total_kernel(n_columns, *refs),
            jax.ShapeDtypeStruct((2 * slots, half), jnp.bfloat16),
            (quarters,),
            12,
        )
        if last_tick:
            late = pack_late(late_rows, EARLY, n_sections)
            summed = jnp.concatenate([summed.reshape(n_planes, -1, half), late], axis=1)
            summed = summed.reshape(-1, half)
        returned = lax.all_to_all(summed, "z", split_axis=0, concat_axis=0, tiled=True)
        if last_tick:
            returned = returned.reshape(n_planes, -1, half)
            late = unpack_late(returned[:, -8:], EARLY, n_sections)
            returned = returned[:, :-8].reshape(-1, half)
        layer_out = in_vmem(
            combine_kernel,
            jax.ShapeDtypeStruct((span_dev, model_width), jnp.bfloat16),
            (tokens, returned),
            8,
            tick=tick,
            tables=(weigh_first, weigh_second),
        )
        if not last_tick:
            layer_in = shifted(layer_out, "section", 1)
    delivered = [early, late]
    blank = jnp.zeros((n_spans, span_dev, kv_width), jnp.bfloat16)
    kv_ticks = jnp.concatenate(delivered + [blank], axis=0)
    kv_store = lax.dynamic_slice_in_dim(kv_ticks, section_id, n_spans, 0)
    return (layer_out[None], kv_store[None])


def solution(mesh):
    n_members = mesh.shape["ep"]
    grid = Mesh(
        mesh.devices.reshape(mesh.shape["section"], n_members // EXP_SPLIT, EXP_SPLIT),
        ("section", "z", "y"),
    )
    ep = ("z", "y")
    in_specs = (
        P(None, ep, None),
        P("section", None),
        P("section", None),
        P("section", None),
        P("section", ep, None),
        P("section", None, ep),
        P("section", None, ep),
        P("section", ep, None),
        P("section", None, None, None),
        P("section", None, ep, None),
        P("section", None, None),
        P(),
    )
    out_specs = (P("section", ep, None), P("section", None, ep, None))
    return jax.shard_map(body, mesh=grid, in_specs=in_specs, out_specs=out_specs, check_vma=False)
```

time: 608 us -> 573 us (0.942)
  blocking collectives: 301 us -> 387 us
  matrix products: 74.6 us -> 8.86 us
  waiting for transfers between devices: 113 us -> 66.8 us
  starting transfers between devices: 68 us -> 32.2 us
  Pallas kernels: 0 us -> 28.8 us
    dot_general x33 -> x2, matrix products: 68.3 us -> 2.59 us  [the longest x1 2.38 us: deliver_whole(): jnp.einsum('tdmr,mtrk->tdk', pick, gathered, preferred_element_type=jnp.f...]
    all_to_all x3 -> x6, blocking collectives: 46.1 us -> 93.7 us  [body(): lax.all_to_all(parts, 'y', split_axis=0, concat_axis=0, tiled=True)]
    pallas_call x0 -> x32, Pallas kernels: none -> 28.8 us  [in_vmem(): pl.pallas_call(kernel, grid=(1,), out_shape=out_shape, in_specs=specs, ou...]
    all_to_all x5 -> x7, blocking collectives: 77 us -> 103 us  [body(): lax.all_to_all(chosen, 'z', split_axis=0, concat_axis=0, tiled=True)]
    all_to_all x4 -> x6, blocking collectives: 52.3 us -> 78.7 us  [body(): lax.all_to_all(summed, 'z', split_axis=0, concat_axis=0, tiled=True)]
    unnamed x19 -> x48, local copies, waits for them, and re-layouts: 0.7 us -> 25.8 us
    all_to_all x4 -> x2, waiting for transfers between devices: 37.8 us -> 23.5 us  [body(): lax.all_to_all(summed, 'z', split_axis=0, concat_axis=0, tiled=True)]
    all_to_all x5 -> x2, starting transfers between devices: 26.5 us -> 12.3 us  [body(): lax.all_to_all(parts, 'y', split_axis=0, concat_axis=0, tiled=True)]
  transfers between devices with their start and end apart: 22 -> 14, of which waited for: 18 -> 12; matrix products, arithmetic and copies ran while one was open for 9% -> 2% of each run, Pallas kernels for 0% -> 2%
where the time goes in v3:
time: 573 us; the launch traced here: 571 us
  blocking collectives  387 us (68%)
  waiting for transfers between devices  66.8 us (12%)
  starting transfers between devices  32.2 us (6%)
  Pallas kernels  28.8 us (5%)
  local copies, waits for them, and re-layouts  27.5 us (5%)
  between operations  14.6 us (3%)
  matrix products  8.86 us (2%)
    all_gather x8, blocking collectives, body(): token_rows = lax.all_gather(arrived, 'y', axis=0, tiled=True)  111 us
    all_to_all x7, blocking collectives, body(): lax.all_to_all(chosen, 'z', split_axis=0, concat_axis=0, tiled=True)  103 us
    all_to_all x6, blocking collectives, body(): lax.all_to_all(parts, 'y', split_axis=0, concat_axis=0, tiled=True)  93.7 us
    all_to_all x6, blocking collectives, body(): lax.all_to_all(summed, 'z', split_axis=0, concat_axis=0, tiled=True)  78.7 us
    pallas_call x32, Pallas kernels, in_vmem(): pl.pallas_call(kernel, grid=(1,), out_shape=out_shape, in_specs=specs, ou...  28.8 us
    unnamed x48, local copies, waits for them, and re-layouts  25.8 us
    all_to_all x2, waiting for transfers between devices, body(): lax.all_to_all(parts, 'y', split_axis=0, concat_axis=0, tiled=True)  24.4 us
    all_to_all x2, waiting for transfers between devices, body(): lax.all_to_all(summed, 'z', split_axis=0, concat_axis=0, tiled=True)  23.5 us
  transfers between devices with their start and end apart: 14, of which 12 were waited for; matrix products, arithmetic and copies ran while one was open for 2% of the time, Pallas kernels for 2%

profile of v3, /device:TPU:8, one launch (start us, length us, event | category | flops | bytes accessed | tf_op | source)
XLA Modules:
  0.0 571.1 jit_solution(17579037725415518678)
XLA Ops:
  11.7 19.5 %all_to_all.267 = bf16[8,8,1792]{2,1,0:T(8,128)(2,1)S(1)} all-to-all(bf16[8,8,1792]{2,1,0:T(8,128)(2,1)S(1)} %bitcast.200), channel_id=1, replica_groups=mesh['section'=8,'z'=8,'y'=4] {'z'}, dimensions={0} | all-to-all | bytes 458752 | tf_op jit(solution)/shard_map/all_to_all | solution.py:282
  31.2 14.5 %all_gather.33.tokens = bf16[256,1792]{1,0:T(8,128)(2,1)S(1)} all-gather(bf16[64,1792]{1,0:T(8,128)(2,1)S(1)} %bitcast.219), channel_id=1, replica_groups=mesh['section'=8,'z'=8,'y'=4] {'y'}, dimensions={0}, use_global_device_ids=true | all-gather | bytes 1146880 | tf_op jit(solution)/shard_map/all_gather | solution.py:286
  53.8 16.8 %all_to_all.268 = bf16[4,32,3584]{2,1,0:T(8,128)(2,1)S(1)} all-to-all(bf16[4,32,3584]{2,1,0:T(8,128)(2,1)S(1)} %bitcast.162), channel_id=1, replica_groups=mesh['section'=8,'z'=8,'y'=4] {'y'}, dimensions={0} | all-to-all | bytes 1835008 | tf_op jit(solution)/shard_map/all_to_all | solution.py:298
  70.8 15.0 %all_to_all.269 = bf16[8,8,1792]{2,1,0:T(8,128)(2,1)S(1)} all-to-all(bf16[8,8,1792]{2,1,0:T(8,128)(2,1)S(1)} %bitcast.207), channel_id=1, replica_groups=mesh['section'=8,'z'=8,'y'=4] {'z'}, dimensions={0} | all-to-all | bytes 458752 | tf_op jit(solution)/shard_map/all_to_all | solution.py:309
  88.8 12.9 %all_to_all.270 = bf16[8,8,1792]{2,1,0:T(8,128)(2,1)S(1)} all-to-all(bf16[8,8,1792]{2,1,0:T(8,128)(2,1)S(1)} %bitcast.201), channel_id=1, replica_groups=mesh['section'=8,'z'=8,'y'=4] {'z'}, dimensions={0} | all-to-all | bytes 458752 | tf_op jit(solution)/shard_map/all_to_all | solution.py:282
  101.8 14.1 %all_gather.34.tokens = bf16[256,1792]{1,0:T(8,128)(2,1)S(1)} all-gather(bf16[64,1792]{1,0:T(8,128)(2,1)S(1)} %bitcast.220), channel_id=1, replica_groups=mesh['section'=8,'z'=8,'y'=4] {'y'}, dimensions={0}, use_global_device_ids=true | all-gather | bytes 1146880 | tf_op jit(solution)/shard_map/all_gather | solution.py:286
  117.9 16.4 %all_to_all.271 = bf16[4,32,3584]{2,1,0:T(8,128)(2,1)S(1)} all-to-all(bf16[4,32,3584]{2,1,0:T(8,128)(2,1)S(1)} %bitcast.163), channel_id=1, replica_groups=mesh['section'=8,'z'=8,'y'=4] {'y'}, dimensions={0} | all-to-all | bytes 1835008 | tf_op jit(solution)/shard_map/all_to_all | solution.py:298
  134.7 13.0 %all_to_all.272 = bf16[8,8,1792]{2,1,0:T(8,128)(2,1)S(1)} all-to-all(bf16[8,8,1792]{2,1,0:T(8,128)(2,1)S(1)} %bitcast.208), channel_id=1, replica_groups=mesh['section'=8,'z'=8,'y'=4] {'z'}, dimensions={0} | all-to-all | bytes 458752 | tf_op jit(solution)/shard_map/all_to_all | solution.py:309
  150.7 13.2 %all_to_all.273 = bf16[8,8,1792]{2,1,0:T(8,128)(2,1)S(1)} all-to-all(bf16[8,8,1792]{2,1,0:T(8,128)(2,1)S(1)} %bitcast.202), channel_id=1, replica_groups=mesh['section'=8,'z'=8,'y'=4] {'z'}, dimensions={0} | all-to-all | bytes 458752 | tf_op jit(solution)/shard_map/all_to_all | solution.py:282
  163.9 14.2 %all_gather.36.tokens = bf16[256,1792]{1,0:T(8,128)(2,1)S(1)} all-gather(bf16[64,1792]{1,0:T(8,128)(2,1)S(1)} %bitcast.221), channel_id=1, replica_groups=mesh['section'=8,'z'=8,'y'=4] {'y'}, dimensions={0}, use_global_device_ids=true | all-gather | bytes 1146880 | tf_op jit(solution)/shard_map/all_gather | solution.py:286
  186.2 17.2 %all_to_all.274 = bf16[4,32,3584]{2,1,0:T(8,128)(2,1)S(1)} all-to-all(bf16[4,32,3584]{2,1,0:T(8,128)(2,1)S(1)} %bitcast.164), channel_id=1, replica_groups=mesh['section'=8,'z'=8,'y'=4] {'y'}, dimensions={0} | all-to-all | bytes 1835008 | tf_op jit(solution)/shard_map/all_to_all | solution.py:298
  203.7 13.2 %all_to_all.275 = bf16[8,8,1792]{2,1,0:T(8,128)(2,1)S(1)} all-to-all(bf16[8,8,1792]{2,1,0:T(8,128)(2,1)S(1)} %bitcast.209), channel_id=1, replica_groups=mesh['section'=8,'z'=8,'y'=4] {'z'}, dimensions={0} | all-to-all | bytes 458752 | tf_op jit(solution)/shard_map/all_to_all | solution.py:309
  219.9 14.4 %all_to_all.276 = bf16[8,8,1792]{2,1,0:T(8,128)(2,1)S(1)} all-to-all(bf16[8,8,1792]{2,1,0:T(8,128)(2,1)S(1)} %bitcast.203), channel_id=1, replica_groups=mesh['section'=8,'z'=8,'y'=4] {'z'}, dimensions={0} | all-to-all | bytes 458752 | tf_op jit(solution)/shard_map/all_to_all | solution.py:282
  234.3 13.8 %all_gather.37.tokens = bf16[256,1792]{1,0:T(8,128)(2,1)S(1)} all-gather(bf16[64,1792]{1,0:T(8,128)(2,1)S(1)} %bitcast.222), channel_id=1, replica_groups=mesh['section'=8,'z'=8,'y'=4] {'y'}, dimensions={0}, use_global_device_ids=true | all-gather | bytes 1146880 | tf_op jit(solution)/shard_map/all_gather | solution.py:286
  250.0 14.4 %all_to_all.277 = bf16[4,32,3584]{2,1,0:T(8,128)(2,1)S(1)} all-to-all(bf16[4,32,3584]{2,1,0:T(8,128)(2,1)S(1)} %bitcast.165), channel_id=1, replica_groups=mesh['section'=8,'z'=8,'y'=4] {'y'}, dimensions={0} | all-to-all | bytes 1835008 | tf_op jit(solution)/shard_map/all_to_all | solution.py:298
  264.8 12.5 %all_to_all.278 = bf16[8,8,1792]{2,1,0:T(8,128)(2,1)S(1)} all-to-all(bf16[8,8,1792]{2,1,0:T(8,128)(2,1)S(1)} %bitcast.210), channel_id=1, replica_groups=mesh['section'=8,'z'=8,'y'=4] {'z'}, dimensions={0} | all-to-all | bytes 458752 | tf_op jit(solution)/shard_map/all_to_all | solution.py:309
  280.3 14.5 %all_to_all.279 = bf16[8,8,1792]{2,1,0:T(8,128)(2,1)S(1)} all-to-all(bf16[8,8,1792]{2,1,0:T(8,128)(2,1)S(1)} %bitcast.204), channel_id=1, replica_groups=mesh['section'=8,'z'=8,'y'=4] {'z'}, dimensions={0} | all-to-all | bytes 458752 | tf_op jit(solution)/shard_map/all_to_all | solution.py:282
  294.8 13.6 %all_gather.38.tokens = bf16[256,1792]{1,0:T(8,128)(2,1)S(1)} all-gather(bf16[64,1792]{1,0:T(8,128)(2,1)S(1)} %bitcast.223), channel_id=1, replica_groups=mesh['section'=8,'z'=8,'y'=4] {'y'}, dimensions={0}, use_global_device_ids=true | all-gather | bytes 1146880 | tf_op jit(solution)/shard_map/all_gather | solution.py:286
  310.4 14.4 %all_to_all.280 = bf16[4,32,3584]{2,1,0:T(8,128)(2,1)S(1)} all-to-all(bf16[4,32,3584]{2,1,0:T(8,128)(2,1)S(1)} %bitcast.166), channel_id=1, replica_groups=mesh['section'=8,'z'=8,'y'=4] {'y'}, dimensions={0} | all-to-all | bytes 1835008 | tf_op jit(solution)/shard_map/all_to_all | solution.py:298
  325.1 12.5 %all_to_all.281 = bf16[8,8,1792]{2,1,0:T(8,128)(2,1)S(1)} all-to-all(bf16[8,8,1792]{2,1,0:T(8,128)(2,1)S(1)} %bitcast.211), channel_id=1, replica_groups=mesh['section'=8,'z'=8,'y'=4] {'z'}, dimensions={0} | all-to-all | bytes 458752 | tf_op jit(solution)/shard_map/all_to_all | solution.py:309
  340.7 14.6 %all_to_all.282 = bf16[8,8,1792]{2,1,0:T(8,128)(2,1)S(1)} all-to-all(bf16[8,8,1792]{2,1,0:T(8,128)(2,1)S(1)} %bitcast.205), channel_id=1, replica_groups=mesh['section'=8,'z'=8,'y'=4] {'z'}, dimensions={0} | all-to-all | bytes 458752 | tf_op jit(solution)/shard_map/all_to_all | solution.py:282
  355.3 13.6 %all_gather.39.tokens = bf16[256,1792]{1,0:T(8,128)(2,1)S(1)} all-gather(bf16[64,1792]{1,0:T(8,128)(2,1)S(1)} %bitcast.224), channel_id=1, replica_groups=mesh['section'=8,'z'=8,'y'=4] {'y'}, dimensions={0}, use_global_device_ids=true | all-gather | bytes 1146880 | tf_op jit(solution)/shard_map/all_gather | solution.py:286
  377.8 9.5 %all-to-all-done.16 = bf16[4,32,3584]{2,1,0:T(8,128)(2,1)S(1)} async-done(((bf16[4,32,3584]{2,1,0:T(8,128)(2,1)}), bf16[4,32,3584]{2,1,0:T(8,128)(2,1)S(1)}, u32[]{:S(2)}, u32[]{:S(2)}) %all-to-all-start.16) | async-done | bytes 917536 | tf_op jit(solution)/shard_map/all_to_all | solution.py:298
  392.1 9.8 %all-to-all-done.17 = bf16[8,8,1792]{2,1,0:T(8,128)(2,1)S(1)} async-done(((bf16[8,8,1792]{2,1,0:T(8,128)(2,1)}), bf16[8,8,1792]{2,1,0:T(8,128)(2,1)S(1)}, u32[]{:S(2)}, u32[]{:S(2)}) %all-to-all-start.17) | async-done | bytes 229408 | tf_op jit(solution)/shard_map/all_to_all | solution.py:309
  409.5 14.4 %all_to_all.283 = bf16[8,8,1792]{2,1,0:T(8,128)(2,1)S(1)} all-to-all(bf16[8,8,1792]{2,1,0:T(8,128)(2,1)S(1)} %bitcast.206), channel_id=1, replica_groups=mesh['section'=8,'z'=8,'y'=4] {'z'}, dimensions={0} | all-to-all | bytes 458752 | tf_op jit(solution)/shard_map/all_to_all | solution.py:282
  423.8 13.8 %all_gather.40.tokens = bf16[256,1792]{1,0:T(8,128)(2,1)S(1)} all-gather(bf16[64,1792]{1,0:T(8,128)(2,1)S(1)} %bitcast.225), channel_id=1, replica_groups=mesh['section'=8,'z'=8,'y'=4] {'y'}, dimensions={0}, use_global_device_ids=true | all-gather | bytes 1146880 | tf_op jit(solution)/shard_map/all_gather | solution.py:286
  445.7 14.4 %all_to_all.284 = bf16[4,32,3584]{2,1,0:T(8,128)(2,1)S(1)} all-to-all(bf16[4,32,3584]{2,1,0:T(8,128)(2,1)S(1)} %bitcast.167), channel_id=1, replica_groups=mesh['section'=8,'z'=8,'y'=4] {'y'}, dimensions={0} | all-to-all | bytes 1835008 | tf_op jit(solution)/shard_map/all_to_all | solution.py:298
  460.4 12.5 %all_to_all.285 = bf16[8,8,1792]{2,1,0:T(8,128)(2,1)S(1)} all-to-all(bf16[8,8,1792]{2,1,0:T(8,128)(2,1)S(1)} %bitcast.212), channel_id=1, replica_groups=mesh['section'=8,'z'=8,'y'=4] {'z'}, dimensions={0} | all-to-all | bytes 458752 | tf_op jit(solution)/shard_map/all_to_all | solution.py:309
  483.7 12.1 %all-to-all-done.21 = bf16[8,8,1792]{2,1,0:T(8,128)(2,1)S(1)} async-done(((bf16[8,8,1792]{2,1,0:T(8,128)(2,1)}), bf16[8,8,1792]{2,1,0:T(8,128)(2,1)S(1)}, u32[]{:S(2)}, u32[]{:S(2)}) %all-to-all-start.21) | async-done | bytes 229408 | tf_op jit(solution)/shard_map/all_to_all | solution.py:282
  495.8 13.5 %all_gather.41 = bf16[288,1792]{1,0:T(8,128)(2,1)S(1)} all-gather(bf16[72,1792]{1,0:T(8,128)(2,1)S(1)} %pad_maximum_fusion), channel_id=1, replica_groups=mesh['section'=8,'z'=8,'y'=4] {'y'}, dimensions={0}, use_global_device_ids=true | all-gather | bytes 1290240 | tf_op jit(solution)/shard_map/all_gather | solution.py:286
  526.0 14.9 %all-to-all-done.22 = bf16[4,32,3584]{2,1,0:T(8,128)(2,1)S(1)} async-done(((bf16[4,32,3584]{2,1,0:T(8,128)(2,1)}), bf16[4,32,3584]{2,1,0:T(8,128)(2,1)S(1)}, u32[]{:S(2)}, u32[]{:S(2)}) %all-to-all-start.22) | async-done | bytes 917536 | tf_op jit(solution)/shard_map/all_to_all | solution.py:298
  546.3 13.7 %all-to-all-done.23 = bf16[8,16,1792]{2,1,0:T(8,128)(2,1)S(1)} async-done(((bf16[8,16,1792]{2,1,0:T(8,128)(2,1)}), bf16[8,16,1792]{2,1,0:T(8,128)(2,1)S(1)}, u32[]{:S(2)}, u32[]{:S(2)}) %all-to-all-start.23) | async-done | bytes 458784 | tf_op jit(solution)/shard_map/all_to_all | solution.py:309
  (184 shorter events, 109.6 us)
Async XLA Ops:
  7.2 4.1 copy-start.16
  7.2 143.1 %all-gather.5.cloned.1.call-start = ((), (), s32[]{:S(2)}) async-start(), calls=%async_computation.24 | async-start | bytes 4730880 | tf_op jit(solution)/shard_map/all_gather | solution.py:167
  45.6 2.1 copy-start.1
  47.7 2.0 copy-start.6
  49.7 2.0 copy-start.11
  51.8 36.7 %copy-start.17 = (bf16[8,8,3584]{2,1,0:T(8,128)(2,1)S(1)}, bf16[8,8,3584]{2,1,0:T(8,128)(2,1)}, u32[]{:S(2)}) copy-start(bf16[8,8,3584]{2,1,0:T(8,128)(2,1)} %param.12) | copy-start | bytes 1376260
  51.8 64.2 %copy-start.7 = (bf16[1,3584,512]{2,1,0:T(8,128)(2,1)S(1)}, bf16[1,3584,512]{2,1,0:T(8,128)(2,1)}, u32[]{:S(2)}) copy-start(bf16[1,3584,512]{2,1,0:T(8,128)(2,1)} %param.18) | copy-start | bytes 11010052
  51.8 64.2 %copy-start.12 = (bf16[1,512,3584]{2,1,0:T(8,128)(2,1)S(1)}, bf16[1,512,3584]{2,1,0:T(8,128)(2,1)}, u32[]{:S(2)}) copy-start(bf16[1,512,3584]{2,1,0:T(8,128)(2,1)} %param.19) | copy-start | bytes 11010052
  53.8 62.2 %copy-start.2 = (bf16[1,3584,512]{2,1,0:T(8,128)(2,1)S(1)}, bf16[1,3584,512]{2,1,0:T(8,128)(2,1)}, u32[]{:S(2)}) copy-start(bf16[1,3584,512]{2,1,0:T(8,128)(2,1)} %param.17) | copy-start | bytes 11010052
  86.3 2.2 collective-permute-start
  148.1 2.2 collective-permute-start.1
  178.1 2.0 copy-start.3
  180.2 2.0 copy-start.8
  182.2 2.0 copy-start.13
  217.4 2.2 collective-permute-start.2
  277.8 2.2 collective-permute-start.3
  338.1 2.2 collective-permute-start.4
  368.9 8.7 %copy-start.21 = (s32[8]{0:T(128)S(1)}, s32[8]{0:T(128)}, u32[]{:S(2)}) copy-start(s32[8]{0:T(128)} %param.23) | copy-start | bytes 100
  368.9 23.1 %copy-start.18 = (f32[1,3584]{1,0:T(1,128)S(1)}, f32[1,3584]{1,0:T(1,128)}, u32[]{:S(2)}) copy-start(f32[1,3584]{1,0:T(1,128)} %param.13) | copy-start | bytes 43012
  371.9 15.4 %all-to-all-start.16 = ((bf16[4,32,3584]{2,1,0:T(8,128)(2,1)}), bf16[4,32,3584]{2,1,0:T(8,128)(2,1)S(1)}, u32[]{:S(2)}, u32[]{:S(2)}) async-start(bf16[4,32,3584]{2,1,0:T(8,128)(2,1)} %bitcast.53), calls=%async_computation.16 | async-start | bytes 1835008 | tf_op jit(solution)/shard_map/all_to_all | solution.py:298
  388.3 20.0 %copy-start.19 = (f32[1,512]{1,0:T(1,128)S(1)}, f32[1,512]{1,0:T(1,128)}, u32[]{:S(2)}) copy-start(f32[1,512]{1,0:T(1,128)} %param.14) | copy-start | bytes 6148
  388.3 13.6 %all-to-all-start.17 = ((bf16[8,8,1792]{2,1,0:T(8,128)(2,1)}), bf16[8,8,1792]{2,1,0:T(8,128)(2,1)S(1)}, u32[]{:S(2)}, u32[]{:S(2)}) async-start(bf16[8,8,1792]{2,1,0:T(8,128)(2,1)} %bitcast.55), calls=%async_computation.17 | async-start | bytes 458752 | tf_op jit(solution)/shard_map/all_to_all | solution.py:309
  391.8 169.4 %all-gather.7.cloned.1.call-start = ((), (), s32[]{:S(2)}) async-start(), calls=%async_computation.25 | async-start | bytes 2365440 | tf_op jit(solution)/shard_map/all_gather | solution.py:211
  402.3 2.2 collective-permute-start.5
  437.7 2.0 copy-start.4
  439.7 2.0 copy-start.9
  473.5 2.2 collective-permute-start.6
  479.9 15.9 %all-to-all-start.21 = ((bf16[8,8,1792]{2,1,0:T(8,128)(2,1)}), bf16[8,8,1792]{2,1,0:T(8,128)(2,1)S(1)}, u32[]{:S(2)}, u32[]{:S(2)}) async-start(bf16[8,8,1792]{2,1,0:T(8,128)(2,1)} %bitcast.64), calls=%async_computation.21 | async-start | bytes 458752 | tf_op jit(solution)/shard_map/all_to_all | solution.py:282
  509.4 2.0 copy-start.5
  515.5 9.7 %copy-start.20 = (s32[1,8,64]{2,1,0:T(8,128)S(1)}, s32[1,8,64]{2,1,0:T(8,128)}, u32[]{:S(2)}) copy-start(s32[1,8,64]{2,1,0:T(8,128)} %param.22) | copy-start | bytes 6148
  518.4 22.5 %all-to-all-start.22 = ((bf16[4,32,3584]{2,1,0:T(8,128)(2,1)}), bf16[4,32,3584]{2,1,0:T(8,128)(2,1)S(1)}, u32[]{:S(2)}, u32[]{:S(2)}) async-start(bf16[4,32,3584]{2,1,0:T(8,128)(2,1)} %bitcast.69), calls=%async_computation.22 | async-start | bytes 1835008 | tf_op jit(solution)/shard_map/all_to_all | solution.py:298
  542.0 18.0 %all-to-all-start.23 = ((bf16[8,16,1792]{2,1,0:T(8,128)(2,1)}), bf16[8,16,1792]{2,1,0:T(8,128)(2,1)S(1)}, u32[]{:S(2)}, u32[]{:S(2)}) async-start(bf16[8,16,1792]{2,1,0:T(8,128)(2,1)} %fusion.13), calls=%async_computation.23 | async-start | bytes 917504 | tf_op jit(solution)/shard_map/all_to_all | solution.py:309
  (4 other events, 6.9 us)
Sparse Core Ops, SparseCore 0:
  10.6 89.2 all-gather.4
  474.9 71.7 all-gather.6

commit v4 on v3

--- a/solution.py
+++ b/solution.py
@@ -26,32 +26,11 @@
     return values * lax.rsqrt(jnp.mean(values * values, axis=-1, keepdims=True) + eps) * gain_vec
 
 
-def rotate_pairs(rope_part, positions):
-    half_dim = rope_part.shape[-1] // 2
+def rotation(width, positions):
+    half_dim = width // 2
     frequency = 10000.0 ** (-jnp.arange(half_dim, dtype=jnp.float32) / half_dim)
     angles = positions.astype(jnp.float32)[:, None] * frequency[None, :]
-    cosine = jnp.cos(angles)
-    sine_part = jnp.sin(angles)
-    first_half = rope_part[:, :half_dim]
-    second = rope_part[:, half_dim:]
-    return jnp.concatenate(
-        [first_half * cosine - second * sine_part, second * cosine + first_half * sine_part], axis=1
-    )
-
-
-def latent_rows(latent, gain_vec, positions):
-    compressed = rms_scale(latent[:, :LAT], gain_vec)
-    rotated = rotate_pairs(latent[:, LAT:], positions)
-    return jnp.concatenate([compressed, rotated], axis=1).astype(jnp.bfloat16)
-
-
-def packing(route_ids, expert_list, capacity):
-    matches = route_ids[:, :, None, :] == expert_list[None, None, :, None]
-    picked = jnp.any(matches, axis=3).astype(jnp.int32)
-    slot_rank = jnp.cumsum(picked, axis=1) - 1
-    slot_ids = jnp.arange(capacity, dtype=jnp.int32)
-    slot_table = (slot_rank[..., None] == slot_ids) & (picked[..., None] > 0)
-    return jnp.transpose(slot_table, (0, 2, 3, 1))
+    return jnp.tile(jnp.cos(angles), (1, 2)), jnp.tile(jnp.sin(angles), (1, 2))
 
 
 def one_hot(rows, cols, wanted, kept=None):
@@ -83,19 +62,63 @@
     )(*operands, *tables)
 
 
-def choose_kernel(tokens, gain, first, second, out):
-    half = out.shape[1]
+def slot_hits(routes, folded, offset):
+    rows = routes.shape[0]
+    line = lax.broadcasted_iota(jnp.int32, (rows, folded), 1)
+    expert = (line // 8).astype(jnp.float32)
+    slot = (line % 8 - offset).astype(jnp.float32)
+    picked = jnp.zeros((rows, folded), jnp.float32)
+    weight = jnp.zeros((rows, folded), jnp.float32)
+    for k in range(TOPK):
+        same = routes[:, k : k + 1] == expert
+        picked = jnp.where(same, 1.0, picked)
+        weight = jnp.where(same, routes[:, TOPK + k : TOPK + k + 1], weight)
+    row = lax.broadcasted_iota(jnp.int32, (rows, rows), 0)
+    col = lax.broadcasted_iota(jnp.int32, (rows, rows), 1)
+    earlier = jnp.where(col < row, 1.0, 0.0)
+    rank = matmul(earlier, picked)
+    hit = (picked > 0.5) & (rank == slot) & (slot >= 0.0) & (slot < 4.0)
+    return jnp.where(hit, 1.0, 0.0), jnp.where(hit, weight, 0.0)
+
+
+def choose_kernel(tokens, gain, routes, out):
+    folded, half = out.shape
     normed = rms_scale(tokens[...], gain[...]).astype(jnp.bfloat16).astype(jnp.float32)
-    picked = matmul(first[0], normed[:, :half]) + matmul(second[0], normed[:, half:])
+    picked = 0.0
+    for offset, part in ((0, normed[:, :half]), (4, normed[:, half:])):
+        hits, _ = slot_hits(routes[0], folded, offset)
+        picked = picked + lax.dot_general(
+            hits, part, (((0,), (0,)), ((), ())), preferred_element_type=jnp.float32
+        )
     out[...] = picked.astype(jnp.bfloat16)
 
 
-def expert_kernel(tokens, w_gate, w_up, w_down, out):
-    folded, half = tokens.shape
-    slots = folded // 2
-    place = lambda row: (row // 4) * 8 + row % 4
-    first = matmul(one_hot(slots, folded, place), tokens[...]).astype(jnp.bfloat16)
-    second = matmul(one_hot(slots, folded, lambda row: place(row) + 4), tokens[...])
+def latent_kernel(rows, attn_gain, kv_gain, w_latent, cosine, sine, out):
+    normed = rms_scale(rows[...], attn_gain[...]).astype(jnp.bfloat16)
+    latent = matmul(normed, w_latent[...])
+    out[:, :LAT] = rms_scale(latent[:, :LAT], kv_gain[...]).astype(jnp.bfloat16)
+    tail = latent[:, LAT:]
+    width = tail.shape[1]
+    row = lax.broadcasted_iota(jnp.int32, (width, width), 0)
+    col = lax.broadcasted_iota(jnp.int32, (width, width), 1)
+    turn = jnp.where(row == col + width // 2, -1.0, jnp.where(row + width // 2 == col, 1.0, 0.0))
+    turned = jnp.dot(
+        tail, turn, precision=lax.Precision.HIGHEST, preferred_element_type=jnp.float32
+    )
+    out[:, LAT:] = (tail * cosine[...] + turned * sine[...]).astype(jnp.bfloat16)
+
+
+def expert_kernel(columns, tokens, w_gate, w_up, w_down, out):
+    height, half = tokens.shape
+    slots = out.shape[0]
+    each, stride = slots // columns, height // columns
+
+    def place(row):
+        within = row % each
+        return (row // each) * stride + (within // 4) * 8 + within % 4
+
+    first = matmul(one_hot(slots, height, place), tokens[...]).astype(jnp.bfloat16)
+    second = matmul(one_hot(slots, height, lambda row: place(row) + 4), tokens[...])
     second = second.astype(jnp.bfloat16)
     gate_proj = matmul(first, w_gate[:half, :]) + matmul(second, w_gate[half:, :])
     up_proj = matmul(first, w_up[:half, :]) + matmul(second, w_up[half:, :])
@@ -120,15 +143,13 @@
     out[...] = spread.astype(jnp.bfloat16)
 
 
-def combine_kernel(tokens, returned, first, second, out):
-    half = returned.shape[1]
+def combine_kernel(tokens, returned, routes, out):
+    folded, half = returned.shape
     rows = returned[...].astype(jnp.float32)
-    for weights, cols in ((first, slice(0, half)), (second, slice(half, 2 * half))):
+    for offset, cols in ((0, slice(0, half)), (4, slice(half, 2 * half))):
+        _, weights = slot_hits(routes[0], folded, offset)
         moe_sum = jnp.dot(
-            weights[0],
-            rows,
-            precision=lax.Precision.HIGHEST,
-            preferred_element_type=jnp.float32,
+            weights, rows, precision=lax.Precision.HIGHEST, preferred_element_type=jnp.float32
         )
         out[:, cols] = (tokens[:, cols].astype(jnp.float32) + moe_sum).astype(jnp.bfloat16)
 
@@ -160,7 +181,6 @@
     experts = n_members // EXP_SPLIT
     capacity = min(span_dev, 2 * span_dev * TOPK // experts)
     per_owner = span_dev // KVBLK
-    all_experts = jnp.arange(experts, dtype=jnp.int32)
     local_gate = w_gate[0]
     local_up = w_up[0]
     local_down = w_down[0]
@@ -171,44 +191,24 @@
         return lax.dynamic_slice_in_dim(padded, n_spans - section_id, n_sections, 0)
 
     own_ids = by_tick(lax.dynamic_slice_in_dim(expert_ids[0], member * span_dev, span_dev, 1))
-    gate_rows = by_tick(gate_vals[0])
-    own_table = packing(own_ids, all_experts, capacity)
-    gate_for = jnp.sum(
-        jnp.where(
-            own_ids[..., None] == all_experts[None, None, None, :], gate_rows[..., None], 0.0
-        ),
-        axis=2,
-    )
-    weighting = own_table.astype(jnp.float32) * jnp.transpose(gate_for, (0, 2, 1))[:, :, None, :]
-    no_slot = jnp.zeros_like(weighting)
-
-    def folded(first, second):
-        return jnp.concatenate([first, second], axis=2).reshape(n_sections, -1, span_dev)
-
-    chooses = own_table.astype(jnp.float32)
-    choose_first, choose_second = folded(chooses, no_slot), folded(no_slot, chooses)
-    weigh_first = jnp.transpose(folded(weighting, no_slot), (0, 2, 1))
-    weigh_second = jnp.transpose(folded(no_slot, weighting), (0, 2, 1))
-    positions = (
-        by_tick(offsets)[:, None]
-        + member * span_dev
-        + jnp.arange(span_dev, dtype=jnp.int32)[None, :]
-    )
-    block_order = by_tick(owner_map[0])
-
-    def project(first, last):
+    routes = jnp.concatenate([own_ids.astype(jnp.float32), by_tick(gate_vals[0])], axis=2)
+
+    def project(first, last, gains, weights, turns):
         rows = jnp.concatenate(tick_rows[first:last], axis=0)
-        normed = rms_scale(rows, attn_gain[0]).astype(jnp.bfloat16)
-        latent = jnp.dot(normed, latent_full, preferred_element_type=jnp.float32)
-        return latent_rows(latent, kv_gain[0], positions[first:last].reshape(-1))
+        part = slice(first * span_dev, last * span_dev)
+        return in_vmem(
+            latent_kernel,
+            jax.ShapeDtypeStruct((rows.shape[0], kv_width), jnp.bfloat16),
+            (rows, *gains, weights, turns[0][part], turns[1][part]),
+            16,
+        )
 
     def owned_rows(order):
         block = jnp.repeat(order, KVBLK, axis=-1)
         return block * KVBLK + jnp.arange(block.shape[-1], dtype=jnp.int32) % KVBLK
 
-    def deliver_whole(kv_rows, first, last):
+    def deliver_whole(gathered, block_order, first, last):
         count = last - first
-        gathered = lax.all_gather(kv_rows, ("z", "y"), axis=0)
         gathered = gathered.reshape(n_members, count, span_dev, kv_width)
         order = lax.dynamic_slice_in_dim(
             block_order[first:last], member * per_owner, per_owner, 1
@@ -230,7 +230,7 @@
         pieces = [wide[..., i * kv_width : (i + 1) * kv_width] for i in range(count)]
         return jnp.concatenate(pieces, axis=-2)
 
-    def pack_late(column_rows, first, last):
+    def pack_late(column_rows, block_order, first, last):
         count = last - first
         order = block_order[first:last].reshape(count, n_planes, n_columns, per_owner)
         order = lax.dynamic_index_in_dim(order, column, 2, keepdims=False)
@@ -255,46 +255,53 @@
     slots = experts * capacity
     tick_rows = []
     layer_in = jnp.zeros((span_dev, model_width), jnp.bfloat16)
-    early = None
+    gains = (attn_gain, kv_gain)
     flops = 2 * 3 * n_columns * slots * model_width * local_gate.shape[1]
     for tick in range(n_sections):
         last_tick = tick + 1 == n_sections
         tokens = jnp.where(section_id == 0, spans[tick], layer_in)
         tick_rows.append(tokens)
-        if tick == 0:
-            held = (tokens, choose_first, choose_second, weigh_first, weigh_second)
-            held = lax.optimization_barrier(held)
-            tokens, choose_first, choose_second, weigh_first, weigh_second = held
-        if tick == 2:
-            tokens, latent_full = lax.optimization_barrier((tokens, latent_full))
-        if tick == EARLY - 1:
-            early_rows = project(0, EARLY)
-            tokens, early_rows = lax.optimization_barrier((tokens, early_rows))
-            early = deliver_whole(early_rows, 0, EARLY)
+        if last_tick:
+            late_rows = project(EARLY, n_sections, gains, latent_full, turns)
+            tokens, late_rows = lax.optimization_barrier((tokens, late_rows))
         chosen = in_vmem(
             choose_kernel,
             jax.ShapeDtypeStruct((2 * slots, half), jnp.bfloat16),
             (tokens, moe_gain),
             8,
             tick=tick,
-            tables=(choose_first, choose_second),
-        )
+            tables=(routes,),
+        )
+        if tick == 0:
+            chosen, offsets = lax.optimization_barrier((chosen, offsets))
+            positions = by_tick(offsets)[:, None] + member * span_dev
+            positions = positions + jnp.arange(span_dev, dtype=jnp.int32)[None, :]
+            turns = rotation(kv_width - LAT, positions.reshape(-1))
         arrived = lax.all_to_all(chosen, "z", split_axis=0, concat_axis=0, tiled=True)
-        if last_tick:
-            late_rows = side_by_side(project(EARLY, n_sections))
-            arrived = jnp.concatenate([arrived, late_rows], axis=0)
+        if tick == 0:
+            arrived, turns = lax.optimization_barrier((arrived, turns))
+        if last_tick:
+            arrived = jnp.concatenate([arrived, side_by_side(late_rows)], axis=0)
         token_rows = lax.all_gather(arrived, "y", axis=0, tiled=True)
-        if last_tick:
-            token_rows = token_rows.reshape(n_columns, -1, half)
-            late_rows = apart(token_rows[:, 2 * slots :], n_sections - EARLY)
-            token_rows = token_rows[:, : 2 * slots].reshape(-1, half)
         parts = in_vmem(
-            expert_kernel,
+            lambda *refs: expert_kernel(n_columns, *refs),
             jax.ShapeDtypeStruct((n_columns * slots, model_width), jnp.bfloat16),
             (token_rows, local_gate, local_up, local_down),
             24,
             flops,
         )
+        if tick == 1:
+            parts, latent_full = lax.optimization_barrier((parts, latent_full))
+        if tick == EARLY - 1:
+            held = lax.optimization_barrier((parts, tick_rows, gains, latent_full, turns))
+            parts, tick_rows, gains, latent_full, turns = held
+            early_rows = project(0, EARLY, gains, latent_full, turns)
+            parts, early_rows = lax.optimization_barrier((parts, early_rows))
+            early = lax.all_gather(early_rows, ("z", "y"), axis=0)
+        if last_tick:
+            held = (parts, token_rows, owner_map)
+            parts, token_rows, owner_map = lax.optimization_barrier(held)
+            block_order = by_tick(owner_map[0])
         quarters = lax.all_to_all(parts, "y", split_axis=0, concat_axis=0, tiled=True)
         summed = in_vmem(
             lambda *refs: total_kernel(n_columns, *refs),
@@ -303,7 +310,9 @@
             12,
         )
         if last_tick:
-            late = pack_late(late_rows, EARLY, n_sections)
+            late_rows = token_rows.reshape(n_columns, -1, half)[:, 2 * slots :]
+            late_rows = apart(late_rows, n_sections - EARLY)
+            late = pack_late(late_rows, block_order, EARLY, n_sections)
             summed = jnp.concatenate([summed.reshape(n_planes, -1, half), late], axis=1)
             summed = summed.reshape(-1, half)
         returned = lax.all_to_all(summed, "z", split_axis=0, concat_axis=0, tiled=True)
@@ -317,10 +326,11 @@
             (tokens, returned),
             8,
             tick=tick,
-            tables=(weigh_first, weigh_second),
+            tables=(routes,),
         )
         if not last_tick:
             layer_in = shifted(layer_out, "section", 1)
+    early = deliver_whole(early, block_order, 0, EARLY)
     delivered = [early, late]
     blank = jnp.zeros((n_spans, span_dev, kv_width), jnp.bfloat16)
     kv_ticks = jnp.concatenate(delivered + [blank], axis=0)

time: 573 us -> 567 us (0.990)
  blocking collectives: 387 us -> 396 us
  waiting for transfers between devices: 66.8 us -> 57.8 us
  matrix products: 8.86 us -> 2.59 us
    all_to_all x7 -> x6, blocking collectives: 103 us -> 85.7 us  [body(): lax.all_to_all(chosen, 'z', split_axis=0, concat_axis=0, tiled=True)]
    all_to_all x6 -> x7, blocking collectives: 93.7 us -> 107 us  [body(): lax.all_to_all(parts, 'y', split_axis=0, concat_axis=0, tiled=True)]
    all_to_all x6 -> x7, blocking collectives: 78.7 us -> 91.3 us  [body(): lax.all_to_all(summed, 'z', split_axis=0, concat_axis=0, tiled=True)]
    all_to_all x1 -> x2, waiting for transfers between devices: 12.1 us -> 22.7 us  [body(): lax.all_to_all(chosen, 'z', split_axis=0, concat_axis=0, tiled=True)]
    all_to_all x2 -> x1, waiting for transfers between devices: 24.4 us -> 14 us  [body(): lax.all_to_all(parts, 'y', split_axis=0, concat_axis=0, tiled=True)]
    all_to_all x2 -> x1, waiting for transfers between devices: 23.5 us -> 14.3 us  [body(): lax.all_to_all(summed, 'z', split_axis=0, concat_axis=0, tiled=True)]
    all_to_all x1 -> x2, starting transfers between devices: 3.4 us -> 11.9 us  [body(): lax.all_to_all(chosen, 'z', split_axis=0, concat_axis=0, tiled=True)]
    dot_general x2 -> x0, matrix products: 6.27 us -> none  [project(): latent = jnp.dot(normed, latent_full, preferred_element_type=jnp.float32)]
  transfers between devices with their start and end apart: 14 -> 13, of which waited for: 12 -> 11; matrix products, arithmetic and copies ran while one was open for 2% -> 1% of each run, Pallas kernels for 2% -> 2%
where the time goes in v4:
time: 567 us; the launch traced here: 565 us
  blocking collectives  396 us (70%)
  waiting for transfers between devices  57.8 us (10%)
  Pallas kernels  34.1 us (6%)
  starting transfers between devices  32.2 us (6%)
  local copies, waits for them, and re-layouts  24.1 us (4%)
  between operations  14.6 us (3%)
    all_gather x8, blocking collectives, body(): token_rows = lax.all_gather(arrived, 'y', axis=0, tiled=True)  112 us
    all_to_all x7, blocking collectives, body(): lax.all_to_all(parts, 'y', split_axis=0, concat_axis=0, tiled=True)  107 us
    all_to_all x7, blocking collectives, body(): lax.all_to_all(summed, 'z', split_axis=0, concat_axis=0, tiled=True)  91.3 us
    all_to_all x6, blocking collectives, body(): lax.all_to_all(chosen, 'z', split_axis=0, concat_axis=0, tiled=True)  85.7 us
    pallas_call x34, Pallas kernels, in_vmem(): pl.pallas_call(kernel, grid=(1,), out_shape=out_shape, in_specs=specs, ou...  34.1 us
    all_to_all x2, waiting for transfers between devices, body(): lax.all_to_all(chosen, 'z', split_axis=0, concat_axis=0, tiled=True)  22.7 us
    unnamed x49, local copies, waits for them, and re-layouts  21.8 us
    all_to_all x1, waiting for transfers between devices, body(): lax.all_to_all(summed, 'z', split_axis=0, concat_axis=0, tiled=True)  14.3 us
  transfers between devices with their start and end apart: 13, of which 11 were waited for; matrix products, arithmetic and copies ran while one was open for 1% of the time, Pallas kernels for 2%

profile of v4, /device:TPU:8, one launch (start us, length us, event | category | flops | bytes accessed | tf_op | source)
XLA Modules:
  0.0 565.4 jit_solution(10921379377675797971)
XLA Ops:
  21.4 10.1 %all-to-all-done = bf16[8,8,1792]{2,1,0:T(8,128)(2,1)S(1)} async-done(((bf16[8,8,1792]{2,1,0:T(8,128)(2,1)}), bf16[8,8,1792]{2,1,0:T(8,128)(2,1)S(1)}, u32[]{:S(2)}, u32[]{:S(2)}) %all-to-all-start) | async-done | bytes 229408 | tf_op jit(solution)/shard_map/all_to_all | solution.py:280
  31.5 14.9 %all_gather.33.refs_0_ = bf16[256,1792]{1,0:T(8,128)(2,1)S(1)} all-gather(bf16[64,1792]{1,0:T(8,128)(2,1)S(1)} %bitcast.168), channel_id=1, replica_groups=mesh['section'=8,'z'=8,'y'=4] {'y'}, dimensions={0}, use_global_device_ids=true | all-gather | bytes 1146880 | tf_op jit(solution)/shard_map/all_gather | solution.py:285
  54.5 16.6 %all_to_all.267 = bf16[4,32,3584]{2,1,0:T(8,128)(2,1)S(1)} all-to-all(bf16[4,32,3584]{2,1,0:T(8,128)(2,1)S(1)} %bitcast.133), channel_id=1, replica_groups=mesh['section'=8,'z'=8,'y'=4] {'y'}, dimensions={0} | all-to-all | bytes 1835008 | tf_op jit(solution)/shard_map/all_to_all | solution.py:305
  71.4 15.2 %all_to_all.268 = bf16[8,8,1792]{2,1,0:T(8,128)(2,1)S(1)} all-to-all(bf16[8,8,1792]{2,1,0:T(8,128)(2,1)S(1)} %bitcast.159), channel_id=1, replica_groups=mesh['section'=8,'z'=8,'y'=4] {'z'}, dimensions={0} | all-to-all | bytes 458752 | tf_op jit(solution)/shard_map/all_to_all | solution.py:318
  90.1 13.0 %all_to_all.269 = bf16[8,8,1792]{2,1,0:T(8,128)(2,1)S(1)} all-to-all(bf16[8,8,1792]{2,1,0:T(8,128)(2,1)S(1)} %bitcast.153), channel_id=1, replica_groups=mesh['section'=8,'z'=8,'y'=4] {'z'}, dimensions={0} | all-to-all | bytes 458752 | tf_op jit(solution)/shard_map/all_to_all | solution.py:280
  103.1 14.4 %all_gather.34.refs_0_ = bf16[256,1792]{1,0:T(8,128)(2,1)S(1)} all-gather(bf16[64,1792]{1,0:T(8,128)(2,1)S(1)} %bitcast.169), channel_id=1, replica_groups=mesh['section'=8,'z'=8,'y'=4] {'y'}, dimensions={0}, use_global_device_ids=true | all-gather | bytes 1146880 | tf_op jit(solution)/shard_map/all_gather | solution.py:285
  119.5 17.1 %all_to_all.270 = bf16[4,32,3584]{2,1,0:T(8,128)(2,1)S(1)} all-to-all(bf16[4,32,3584]{2,1,0:T(8,128)(2,1)S(1)} %bitcast.132), channel_id=1, replica_groups=mesh['section'=8,'z'=8,'y'=4] {'y'}, dimensions={0} | all-to-all | bytes 1835008 | tf_op jit(solution)/shard_map/all_to_all | solution.py:305
  137.0 13.4 %all_to_all.271 = bf16[8,8,1792]{2,1,0:T(8,128)(2,1)S(1)} all-to-all(bf16[8,8,1792]{2,1,0:T(8,128)(2,1)S(1)} %bitcast.160), channel_id=1, replica_groups=mesh['section'=8,'z'=8,'y'=4] {'z'}, dimensions={0} | all-to-all | bytes 458752 | tf_op jit(solution)/shard_map/all_to_all | solution.py:318
  153.8 14.2 %all_to_all.272 = bf16[8,8,1792]{2,1,0:T(8,128)(2,1)S(1)} all-to-all(bf16[8,8,1792]{2,1,0:T(8,128)(2,1)S(1)} %bitcast.154), channel_id=1, replica_groups=mesh['section'=8,'z'=8,'y'=4] {'z'}, dimensions={0} | all-to-all | bytes 458752 | tf_op jit(solution)/shard_map/all_to_all | solution.py:280
  168.1 14.1 %all_gather.36.refs_0_ = bf16[256,1792]{1,0:T(8,128)(2,1)S(1)} all-gather(bf16[64,1792]{1,0:T(8,128)(2,1)S(1)} %bitcast.170), channel_id=1, replica_groups=mesh['section'=8,'z'=8,'y'=4] {'y'}, dimensions={0}, use_global_device_ids=true | all-gather | bytes 1146880 | tf_op jit(solution)/shard_map/all_gather | solution.py:285
  188.2 16.0 %all_to_all.273 = bf16[4,32,3584]{2,1,0:T(8,128)(2,1)S(1)} all-to-all(bf16[4,32,3584]{2,1,0:T(8,128)(2,1)S(1)} %bitcast.134), channel_id=1, replica_groups=mesh['section'=8,'z'=8,'y'=4] {'y'}, dimensions={0} | all-to-all | bytes 1835008 | tf_op jit(solution)/shard_map/all_to_all | solution.py:305
  204.5 12.5 %all_to_all.274 = bf16[8,8,1792]{2,1,0:T(8,128)(2,1)S(1)} all-to-all(bf16[8,8,1792]{2,1,0:T(8,128)(2,1)S(1)} %bitcast.161), channel_id=1, replica_groups=mesh['section'=8,'z'=8,'y'=4] {'z'}, dimensions={0} | all-to-all | bytes 458752 | tf_op jit(solution)/shard_map/all_to_all | solution.py:318
  220.5 15.0 %all_to_all.275 = bf16[8,8,1792]{2,1,0:T(8,128)(2,1)S(1)} all-to-all(bf16[8,8,1792]{2,1,0:T(8,128)(2,1)S(1)} %bitcast.155), channel_id=1, replica_groups=mesh['section'=8,'z'=8,'y'=4] {'z'}, dimensions={0} | all-to-all | bytes 458752 | tf_op jit(solution)/shard_map/all_to_all | solution.py:280
  235.5 13.8 %all_gather.37.refs_0_ = bf16[256,1792]{1,0:T(8,128)(2,1)S(1)} all-gather(bf16[64,1792]{1,0:T(8,128)(2,1)S(1)} %bitcast.171), channel_id=1, replica_groups=mesh['section'=8,'z'=8,'y'=4] {'y'}, dimensions={0}, use_global_device_ids=true | all-gather | bytes 1146880 | tf_op jit(solution)/shard_map/all_gather | solution.py:285
  251.3 14.4 %all_to_all.276 = bf16[4,32,3584]{2,1,0:T(8,128)(2,1)S(1)} all-to-all(bf16[4,32,3584]{2,1,0:T(8,128)(2,1)S(1)} %bitcast.135), channel_id=1, replica_groups=mesh['section'=8,'z'=8,'y'=4] {'y'}, dimensions={0} | all-to-all | bytes 1835008 | tf_op jit(solution)/shard_map/all_to_all | solution.py:305
  266.0 12.5 %all_to_all.277 = bf16[8,8,1792]{2,1,0:T(8,128)(2,1)S(1)} all-to-all(bf16[8,8,1792]{2,1,0:T(8,128)(2,1)S(1)} %bitcast.162), channel_id=1, replica_groups=mesh['section'=8,'z'=8,'y'=4] {'z'}, dimensions={0} | all-to-all | bytes 458752 | tf_op jit(solution)/shard_map/all_to_all | solution.py:318
  282.0 14.4 %all_to_all.278 = bf16[8,8,1792]{2,1,0:T(8,128)(2,1)S(1)} all-to-all(bf16[8,8,1792]{2,1,0:T(8,128)(2,1)S(1)} %bitcast.156), channel_id=1, replica_groups=mesh['section'=8,'z'=8,'y'=4] {'z'}, dimensions={0} | all-to-all | bytes 458752 | tf_op jit(solution)/shard_map/all_to_all | solution.py:280
  296.3 13.6 %all_gather.38.refs_0_ = bf16[256,1792]{1,0:T(8,128)(2,1)S(1)} all-gather(bf16[64,1792]{1,0:T(8,128)(2,1)S(1)} %bitcast.172), channel_id=1, replica_groups=mesh['section'=8,'z'=8,'y'=4] {'y'}, dimensions={0}, use_global_device_ids=true | all-gather | bytes 1146880 | tf_op jit(solution)/shard_map/all_gather | solution.py:285
  311.9 14.4 %all_to_all.279 = bf16[4,32,3584]{2,1,0:T(8,128)(2,1)S(1)} all-to-all(bf16[4,32,3584]{2,1,0:T(8,128)(2,1)S(1)} %bitcast.136), channel_id=1, replica_groups=mesh['section'=8,'z'=8,'y'=4] {'y'}, dimensions={0} | all-to-all | bytes 1835008 | tf_op jit(solution)/shard_map/all_to_all | solution.py:305
  326.6 12.5 %all_to_all.280 = bf16[8,8,1792]{2,1,0:T(8,128)(2,1)S(1)} all-to-all(bf16[8,8,1792]{2,1,0:T(8,128)(2,1)S(1)} %bitcast.163), channel_id=1, replica_groups=mesh['section'=8,'z'=8,'y'=4] {'z'}, dimensions={0} | all-to-all | bytes 458752 | tf_op jit(solution)/shard_map/all_to_all | solution.py:318
  342.6 14.5 %all_to_all.281 = bf16[8,8,1792]{2,1,0:T(8,128)(2,1)S(1)} all-to-all(bf16[8,8,1792]{2,1,0:T(8,128)(2,1)S(1)} %bitcast.157), channel_id=1, replica_groups=mesh['section'=8,'z'=8,'y'=4] {'z'}, dimensions={0} | all-to-all | bytes 458752 | tf_op jit(solution)/shard_map/all_to_all | solution.py:280
  357.1 13.6 %all_gather.39.refs_0_ = bf16[256,1792]{1,0:T(8,128)(2,1)S(1)} all-gather(bf16[64,1792]{1,0:T(8,128)(2,1)S(1)} %bitcast.173), channel_id=1, replica_groups=mesh['section'=8,'z'=8,'y'=4] {'y'}, dimensions={0}, use_global_device_ids=true | all-gather | bytes 1146880 | tf_op jit(solution)/shard_map/all_gather | solution.py:285
  372.7 14.4 %all_to_all.282 = bf16[4,32,3584]{2,1,0:T(8,128)(2,1)S(1)} all-to-all(bf16[4,32,3584]{2,1,0:T(8,128)(2,1)S(1)} %bitcast.137), channel_id=1, replica_groups=mesh['section'=8,'z'=8,'y'=4] {'y'}, dimensions={0} | all-to-all | bytes 1835008 | tf_op jit(solution)/shard_map/all_to_all | solution.py:305
  387.4 12.5 %all_to_all.283 = bf16[8,8,1792]{2,1,0:T(8,128)(2,1)S(1)} all-to-all(bf16[8,8,1792]{2,1,0:T(8,128)(2,1)S(1)} %bitcast.164), channel_id=1, replica_groups=mesh['section'=8,'z'=8,'y'=4] {'z'}, dimensions={0} | all-to-all | bytes 458752 | tf_op jit(solution)/shard_map/all_to_all | solution.py:318
  403.3 14.7 %all_to_all.284 = bf16[8,8,1792]{2,1,0:T(8,128)(2,1)S(1)} all-to-all(bf16[8,8,1792]{2,1,0:T(8,128)(2,1)S(1)} %bitcast.158), channel_id=1, replica_groups=mesh['section'=8,'z'=8,'y'=4] {'z'}, dimensions={0} | all-to-all | bytes 458752 | tf_op jit(solution)/shard_map/all_to_all | solution.py:280
  418.0 13.9 %all_gather.40.refs_0_ = bf16[256,1792]{1,0:T(8,128)(2,1)S(1)} all-gather(bf16[64,1792]{1,0:T(8,128)(2,1)S(1)} %bitcast.174), channel_id=1, replica_groups=mesh['section'=8,'z'=8,'y'=4] {'y'}, dimensions={0}, use_global_device_ids=true | all-gather | bytes 1146880 | tf_op jit(solution)/shard_map/all_gather | solution.py:285
  438.3 14.4 %all_to_all.285 = bf16[4,32,3584]{2,1,0:T(8,128)(2,1)S(1)} all-to-all(bf16[4,32,3584]{2,1,0:T(8,128)(2,1)S(1)} %bitcast.131), channel_id=1, replica_groups=mesh['section'=8,'z'=8,'y'=4] {'y'}, dimensions={0} | all-to-all | bytes 1835008 | tf_op jit(solution)/shard_map/all_to_all | solution.py:305
  453.0 12.5 %all_to_all.286 = bf16[8,8,1792]{2,1,0:T(8,128)(2,1)S(1)} all-to-all(bf16[8,8,1792]{2,1,0:T(8,128)(2,1)S(1)} %bitcast.165), channel_id=1, replica_groups=mesh['section'=8,'z'=8,'y'=4] {'z'}, dimensions={0} | all-to-all | bytes 458752 | tf_op jit(solution)/shard_map/all_to_all | solution.py:318
  476.3 12.6 %all-to-all-done.21 = bf16[8,8,1792]{2,1,0:T(8,128)(2,1)S(1)} async-done(((bf16[8,8,1792]{2,1,0:T(8,128)(2,1)}), bf16[8,8,1792]{2,1,0:T(8,128)(2,1)S(1)}, u32[]{:S(2)}, u32[]{:S(2)}) %all-to-all-start.21) | async-done | bytes 229408 | tf_op jit(solution)/shard_map/all_to_all | solution.py:280
  489.0 13.6 %all_gather.41.refs_0_ = bf16[288,1792]{1,0:T(8,128)(2,1)S(1)} all-gather(bf16[72,1792]{1,0:T(8,128)(2,1)S(1)} %fusion.12), channel_id=1, replica_groups=mesh['section'=8,'z'=8,'y'=4] {'y'}, dimensions={0}, use_global_device_ids=true | all-gather | bytes 1290240 | tf_op jit(solution)/shard_map/all_gather | solution.py:285
  519.9 14.0 %all-to-all-done.22 = bf16[4,32,3584]{2,1,0:T(8,128)(2,1)S(1)} async-done(((bf16[4,32,3584]{2,1,0:T(8,128)(2,1)}), bf16[4,32,3584]{2,1,0:T(8,128)(2,1)S(1)}, u32[]{:S(2)}, u32[]{:S(2)}) %all-to-all-start.22) | async-done | bytes 917536 | tf_op jit(solution)/shard_map/all_to_all | solution.py:305
  539.7 14.3 %all-to-all-done.23 = bf16[8,16,1792]{2,1,0:T(8,128)(2,1)S(1)} async-done(((bf16[8,16,1792]{2,1,0:T(8,128)(2,1)}), bf16[8,16,1792]{2,1,0:T(8,128)(2,1)S(1)}, u32[]{:S(2)}, u32[]{:S(2)}) %all-to-all-start.23) | async-done | bytes 458784 | tf_op jit(solution)/shard_map/all_to_all | solution.py:318
  (168 shorter events, 103.6 us)
Async XLA Ops:
  7.2 112.4 %all-gather.5.cloned.1.call-start = ((), (), s32[]{:S(2)}) async-start(), calls=%async_computation.24 | async-start | bytes 4730880 | tf_op jit(solution)/shard_map/all_gather | solution.py:187
  11.8 19.7 %all-to-all-start = ((bf16[8,8,1792]{2,1,0:T(8,128)(2,1)}), bf16[8,8,1792]{2,1,0:T(8,128)(2,1)S(1)}, u32[]{:S(2)}, u32[]{:S(2)}) async-start(bf16[8,8,1792]{2,1,0:T(8,128)(2,1)} %bitcast.10), calls=%async_computation | async-start | bytes 458752 | tf_op jit(solution)/shard_map/all_to_all | solution.py:280
  20.3 535.1 %all-gather.7.cloned.1.call-start = ((), (), s32[]{:S(2)}) async-start(), calls=%async_computation.25 | async-start | bytes 2365440 | tf_op jit(solution)/shard_map/all_gather | solution.py:300
  46.4 2.0 copy-start.1
  48.4 2.0 copy-start.5
  50.5 2.0 copy-start.9
  52.5 65.0 %copy-start.6 = (bf16[1,3584,512]{2,1,0:T(8,128)(2,1)S(1)}, bf16[1,3584,512]{2,1,0:T(8,128)(2,1)}, u32[]{:S(2)}) copy-start(bf16[1,3584,512]{2,1,0:T(8,128)(2,1)} %param.18) | copy-start | bytes 11010052
  52.5 65.0 %copy-start.10 = (bf16[1,512,3584]{2,1,0:T(8,128)(2,1)S(1)}, bf16[1,512,3584]{2,1,0:T(8,128)(2,1)}, u32[]{:S(2)}) copy-start(bf16[1,512,3584]{2,1,0:T(8,128)(2,1)} %param.19) | copy-start | bytes 11010052
  54.5 35.1 %copy-start.19 = (bf16[8,8,3584]{2,1,0:T(8,128)(2,1)S(1)}, bf16[8,8,3584]{2,1,0:T(8,128)(2,1)}, u32[]{:S(2)}) copy-start(bf16[8,8,3584]{2,1,0:T(8,128)(2,1)} %param.12) | copy-start | bytes 1376260
  54.5 35.1 %copy-start.16 = (f32[1,3584]{1,0:T(1,128)S(1)}, f32[1,3584]{1,0:T(1,128)}, u32[]{:S(2)}) copy-start(f32[1,3584]{1,0:T(1,128)} %gain.15) | copy-start | bytes 43012
  71.1 46.4 %copy-start.2 = (bf16[1,3584,512]{2,1,0:T(8,128)(2,1)S(1)}, bf16[1,3584,512]{2,1,0:T(8,128)(2,1)}, u32[]{:S(2)}) copy-start(bf16[1,3584,512]{2,1,0:T(8,128)(2,1)} %param.17) | copy-start | bytes 11010052
  87.4 2.2 collective-permute-start
  136.7 45.4 %copy-start.3 = (bf16[1,3584,512]{2,1,0:T(8,128)(2,1)S(1)}, bf16[1,3584,512]{2,1,0:T(8,128)(2,1)}, u32[]{:S(2)}) copy-start(bf16[1,3584,512]{2,1,0:T(8,128)(2,1)} %param.17) | copy-start | bytes 11010052
  151.1 2.2 collective-permute-start.1
  182.1 2.0 copy-start.7
  184.2 2.0 copy-start.11
  217.8 2.2 collective-permute-start.2
  279.3 2.2 collective-permute-start.3
  339.9 2.2 collective-permute-start.4
  400.6 2.2 collective-permute-start.5
  431.9 2.3 copy-start.17
  431.9 2.3 copy-start.18
  434.1 2.3 copy-start.13
  466.3 2.2 collective-permute-start.6
  468.5 2.3 copy-start.14
  472.9 16.0 %all-to-all-start.21 = ((bf16[8,8,1792]{2,1,0:T(8,128)(2,1)}), bf16[8,8,1792]{2,1,0:T(8,128)(2,1)S(1)}, u32[]{:S(2)}, u32[]{:S(2)}) async-start(bf16[8,8,1792]{2,1,0:T(8,128)(2,1)} %bitcast.58), calls=%async_computation.21 | async-start | bytes 458752 | tf_op jit(solution)/shard_map/all_to_all | solution.py:280
  502.6 2.0 copy-start.4
  504.6 2.0 copy-start.8
  506.6 2.0 copy-start.12
  508.7 10.5 %copy-start.20 = (s32[1,8,64]{2,1,0:T(8,128)S(1)}, s32[1,8,64]{2,1,0:T(8,128)}, u32[]{:S(2)}) copy-start(s32[1,8,64]{2,1,0:T(8,128)} %param.22) | copy-start | bytes 6148
  511.8 22.1 %all-to-all-start.22 = ((bf16[4,32,3584]{2,1,0:T(8,128)(2,1)}), bf16[4,32,3584]{2,1,0:T(8,128)(2,1)S(1)}, u32[]{:S(2)}, u32[]{:S(2)}) async-start(bf16[4,32,3584]{2,1,0:T(8,128)(2,1)} %bitcast.60), calls=%async_computation.22 | async-start | bytes 1835008 | tf_op jit(solution)/shard_map/all_to_all | solution.py:305
  535.0 18.9 %all-to-all-start.23 = ((bf16[8,16,1792]{2,1,0:T(8,128)(2,1)}), bf16[8,16,1792]{2,1,0:T(8,128)(2,1)S(1)}, u32[]{:S(2)}, u32[]{:S(2)}) async-start(bf16[8,16,1792]{2,1,0:T(8,128)(2,1)} %fusion.11), calls=%async_computation.23 | async-start | bytes 917504 | tf_op jit(solution)/shard_map/all_to_all | solution.py:318
  (2 other events, 1.5 us)
Sparse Core Ops, SparseCore 0:
  10.6 87.4 all-gather.4
  467.7 71.4 all-gather.6

commit v5 on v4

--- a/solution.py
+++ b/solution.py
@@ -1,5 +1,6 @@
 import jax
 import jax.numpy as jnp
+import numpy as np
 from jax import lax
 from jax.experimental import pallas as pl
 from jax.experimental.pallas import tpu as pltpu
@@ -205,7 +206,7 @@
 
     def owned_rows(order):
         block = jnp.repeat(order, KVBLK, axis=-1)
-        return block * KVBLK + jnp.arange(block.shape[-1], dtype=jnp.int32) % KVBLK
+        return block * KVBLK + np.arange(block.shape[-1], dtype=np.int32) % KVBLK
 
     def deliver_whole(gathered, block_order, first, last):
         count = last - first
@@ -213,7 +214,7 @@
         order = lax.dynamic_slice_in_dim(
             block_order[first:last], member * per_owner, per_owner, 1
         )
-        every = jnp.arange(n_members * span_dev, dtype=jnp.int32)
+        every = np.arange(n_members * span_dev, dtype=np.int32)
         pick = (owned_rows(order)[..., None] == every).astype(jnp.bfloat16)
         pick = pick.reshape(count, span_dev, n_members, span_dev)
         return jnp.einsum(
@@ -235,11 +236,11 @@
         order = block_order[first:last].reshape(count, n_planes, n_columns, per_owner)
         order = lax.dynamic_index_in_dim(order, column, 2, keepdims=False)
         wanted = jnp.transpose(owned_rows(order), (1, 0, 2))
-        col = jnp.arange(n_columns, dtype=jnp.int32)[:, None, None]
-        tick = jnp.arange(count, dtype=jnp.int32)[None, :, None]
-        row = jnp.arange(span_dev, dtype=jnp.int32)[None, None, :]
+        col = np.arange(n_columns, dtype=np.int32)[:, None, None]
+        tick = np.arange(count, dtype=np.int32)[None, :, None]
+        row = np.arange(span_dev, dtype=np.int32)[None, None, :]
         held = (plane * n_columns + col) * span_dev + row + 0 * tick
-        same = tick + 0 * held == jnp.arange(count, dtype=jnp.int32)[:, None, None, None]
+        same = tick + 0 * held == np.arange(count, dtype=np.int32)[:, None, None, None]
         hit = (wanted[..., None, None, None] == held) & same[:, None]
         hit = hit.reshape(n_planes * count * span_dev, -1).astype(jnp.bfloat16)
         source = column_rows.reshape(-1, kv_width)
@@ -262,7 +263,7 @@
         tokens = jnp.where(section_id == 0, spans[tick], layer_in)
         tick_rows.append(tokens)
         if last_tick:
-            late_rows = project(EARLY, n_sections, gains, latent_full, turns)
+            late_rows = side_by_side(project(EARLY, n_sections, gains, latent_full, turns))
             tokens, late_rows = lax.optimization_barrier((tokens, late_rows))
         chosen = in_vmem(
             choose_kernel,
@@ -278,10 +279,10 @@
             positions = positions + jnp.arange(span_dev, dtype=jnp.int32)[None, :]
             turns = rotation(kv_width - LAT, positions.reshape(-1))
         arrived = lax.all_to_all(chosen, "z", split_axis=0, concat_axis=0, tiled=True)
+        if last_tick:
+            arrived = jnp.concatenate([arrived, late_rows], axis=0)
         if tick == 0:
             arrived, turns = lax.optimization_barrier((arrived, turns))
-        if last_tick:
-            arrived = jnp.concatenate([arrived, side_by_side(late_rows)], axis=0)
         token_rows = lax.all_gather(arrived, "y", axis=0, tiled=True)
         parts = in_vmem(
             lambda *refs: expert_kernel(n_columns, *refs),
@@ -303,6 +304,8 @@
             parts, token_rows, owner_map = lax.optimization_barrier(held)
             block_order = by_tick(owner_map[0])
         quarters = lax.all_to_all(parts, "y", split_axis=0, concat_axis=0, tiled=True)
+        if last_tick:
+            quarters, early = lax.optimization_barrier((quarters, early))
         summed = in_vmem(
             lambda *refs: total_kernel(n_columns, *refs),
             jax.ShapeDtypeStruct((2 * slots, half), jnp.bfloat16),

time: 567 us -> 558 us (0.984)
  waiting for transfers between devices: 57.8 us -> 45.9 us
  blocking collectives: 396 us -> 403 us
    all_to_all x6 -> x7, blocking collectives: 85.7 us -> 100 us  [body(): lax.all_to_all(chosen, 'z', split_axis=0, concat_axis=0, tiled=True)]
    all_to_all x7 -> x6, blocking collectives: 107 us -> 93.4 us  [body(): lax.all_to_all(parts, 'y', split_axis=0, concat_axis=0, tiled=True)]
    all_to_all x2 -> x1, waiting for transfers between devices: 22.7 us -> 10.2 us  [body(): lax.all_to_all(chosen, 'z', split_axis=0, concat_axis=0, tiled=True)]
    all_to_all x1 -> x2, waiting for transfers between devices: 14 us -> 18.2 us  [body(): lax.all_to_all(parts, 'y', split_axis=0, concat_axis=0, tiled=True)]
    unnamed x49 -> x53, local copies, waits for them, and re-layouts: 21.8 us -> 17.9 us
    all_to_all x2 -> x1, starting transfers between devices: 11.9 us -> 8.46 us  [body(): lax.all_to_all(chosen, 'z', split_axis=0, concat_axis=0, tiled=True)]
where the time goes in v5:
time: 558 us; the launch traced here: 556 us
  blocking collectives  403 us (72%)
  waiting for transfers between devices  45.9 us (8%)
  Pallas kernels  34.4 us (6%)
  starting transfers between devices  32 us (6%)
  local copies, waits for them, and re-layouts  22.2 us (4%)
  between operations  14.6 us (3%)
    all_gather x8, blocking collectives, body(): token_rows = lax.all_gather(arrived, 'y', axis=0, tiled=True)  117 us
    all_to_all x7, blocking collectives, body(): lax.all_to_all(chosen, 'z', split_axis=0, concat_axis=0, tiled=True)  100 us
    all_to_all x6, blocking collectives, body(): lax.all_to_all(parts, 'y', split_axis=0, concat_axis=0, tiled=True)  93.4 us
    all_to_all x7, blocking collectives, body(): lax.all_to_all(summed, 'z', split_axis=0, concat_axis=0, tiled=True)  91.7 us
    pallas_call x34, Pallas kernels, in_vmem(): pl.pallas_call(kernel, grid=(1,), out_shape=out_shape, in_specs=specs, ou...  34.4 us
    all_to_all x2, waiting for transfers between devices, body(): lax.all_to_all(parts, 'y', split_axis=0, concat_axis=0, tiled=True)  18.2 us
    unnamed x53, local copies, waits for them, and re-layouts  17.9 us
  transfers between devices with their start and end apart: 13, of which 11 were waited for; matrix products, arithmetic and copies ran while one was open for 1% of the time, Pallas kernels for 2%

profile of v5, /device:TPU:8, one launch (start us, length us, event | category | flops | bytes accessed | tf_op | source)
XLA Modules:
  0.0 556.3 jit_solution(16635693149414891498)
XLA Ops:
  21.4 10.2 %all-to-all-done = bf16[8,8,1792]{2,1,0:T(8,128)(2,1)S(1)} async-done(((bf16[8,8,1792]{2,1,0:T(8,128)(2,1)}), bf16[8,8,1792]{2,1,0:T(8,128)(2,1)S(1)}, u32[]{:S(2)}, u32[]{:S(2)}) %all-to-all-start) | async-done | bytes 229408 | tf_op jit(solution)/shard_map/all_to_all | solution.py:281
  31.5 14.9 %all_gather.33.refs_0_ = bf16[256,1792]{1,0:T(8,128)(2,1)S(1)} all-gather(bf16[64,1792]{1,0:T(8,128)(2,1)S(1)} %bitcast.174), channel_id=1, replica_groups=mesh['section'=8,'z'=8,'y'=4] {'y'}, dimensions={0}, use_global_device_ids=true | all-gather | bytes 1146880 | tf_op jit(solution)/shard_map/all_gather | solution.py:286
  54.6 16.7 %all_to_all.268 = bf16[4,32,3584]{2,1,0:T(8,128)(2,1)S(1)} all-to-all(bf16[4,32,3584]{2,1,0:T(8,128)(2,1)S(1)} %bitcast.136), channel_id=1, replica_groups=mesh['section'=8,'z'=8,'y'=4] {'y'}, dimensions={0} | all-to-all | bytes 1835008 | tf_op jit(solution)/shard_map/all_to_all | solution.py:306
  71.5 15.2 %all_to_all.269 = bf16[8,8,1792]{2,1,0:T(8,128)(2,1)S(1)} all-to-all(bf16[8,8,1792]{2,1,0:T(8,128)(2,1)S(1)} %bitcast.163), channel_id=1, replica_groups=mesh['section'=8,'z'=8,'y'=4] {'z'}, dimensions={0} | all-to-all | bytes 458752 | tf_op jit(solution)/shard_map/all_to_all | solution.py:321
  90.2 12.9 %all_to_all.270 = bf16[8,8,1792]{2,1,0:T(8,128)(2,1)S(1)} all-to-all(bf16[8,8,1792]{2,1,0:T(8,128)(2,1)S(1)} %bitcast.156), channel_id=1, replica_groups=mesh['section'=8,'z'=8,'y'=4] {'z'}, dimensions={0} | all-to-all | bytes 458752 | tf_op jit(solution)/shard_map/all_to_all | solution.py:281
  103.1 14.0 %all_gather.34.refs_0_ = bf16[256,1792]{1,0:T(8,128)(2,1)S(1)} all-gather(bf16[64,1792]{1,0:T(8,128)(2,1)S(1)} %bitcast.175), channel_id=1, replica_groups=mesh['section'=8,'z'=8,'y'=4] {'y'}, dimensions={0}, use_global_device_ids=true | all-gather | bytes 1146880 | tf_op jit(solution)/shard_map/all_gather | solution.py:286
  119.1 17.6 %all_to_all.271 = bf16[4,32,3584]{2,1,0:T(8,128)(2,1)S(1)} all-to-all(bf16[4,32,3584]{2,1,0:T(8,128)(2,1)S(1)} %bitcast.135), channel_id=1, replica_groups=mesh['section'=8,'z'=8,'y'=4] {'y'}, dimensions={0} | all-to-all | bytes 1835008 | tf_op jit(solution)/shard_map/all_to_all | solution.py:306
  137.0 13.4 %all_to_all.272 = bf16[8,8,1792]{2,1,0:T(8,128)(2,1)S(1)} all-to-all(bf16[8,8,1792]{2,1,0:T(8,128)(2,1)S(1)} %bitcast.164), channel_id=1, replica_groups=mesh['section'=8,'z'=8,'y'=4] {'z'}, dimensions={0} | all-to-all | bytes 458752 | tf_op jit(solution)/shard_map/all_to_all | solution.py:321
  153.9 14.1 %all_to_all.273 = bf16[8,8,1792]{2,1,0:T(8,128)(2,1)S(1)} all-to-all(bf16[8,8,1792]{2,1,0:T(8,128)(2,1)S(1)} %bitcast.157), channel_id=1, replica_groups=mesh['section'=8,'z'=8,'y'=4] {'z'}, dimensions={0} | all-to-all | bytes 458752 | tf_op jit(solution)/shard_map/all_to_all | solution.py:281
  168.0 13.9 %all_gather.36.refs_0_ = bf16[256,1792]{1,0:T(8,128)(2,1)S(1)} all-gather(bf16[64,1792]{1,0:T(8,128)(2,1)S(1)} %bitcast.176), channel_id=1, replica_groups=mesh['section'=8,'z'=8,'y'=4] {'y'}, dimensions={0}, use_global_device_ids=true | all-gather | bytes 1146880 | tf_op jit(solution)/shard_map/all_gather | solution.py:286
  187.9 15.9 %all_to_all.274 = bf16[4,32,3584]{2,1,0:T(8,128)(2,1)S(1)} all-to-all(bf16[4,32,3584]{2,1,0:T(8,128)(2,1)S(1)} %bitcast.137), channel_id=1, replica_groups=mesh['section'=8,'z'=8,'y'=4] {'y'}, dimensions={0} | all-to-all | bytes 1835008 | tf_op jit(solution)/shard_map/all_to_all | solution.py:306
  204.2 12.5 %all_to_all.275 = bf16[8,8,1792]{2,1,0:T(8,128)(2,1)S(1)} all-to-all(bf16[8,8,1792]{2,1,0:T(8,128)(2,1)S(1)} %bitcast.165), channel_id=1, replica_groups=mesh['section'=8,'z'=8,'y'=4] {'z'}, dimensions={0} | all-to-all | bytes 458752 | tf_op jit(solution)/shard_map/all_to_all | solution.py:321
  220.2 15.0 %all_to_all.276 = bf16[8,8,1792]{2,1,0:T(8,128)(2,1)S(1)} all-to-all(bf16[8,8,1792]{2,1,0:T(8,128)(2,1)S(1)} %bitcast.158), channel_id=1, replica_groups=mesh['section'=8,'z'=8,'y'=4] {'z'}, dimensions={0} | all-to-all | bytes 458752 | tf_op jit(solution)/shard_map/all_to_all | solution.py:281
  235.1 13.8 %all_gather.37.refs_0_ = bf16[256,1792]{1,0:T(8,128)(2,1)S(1)} all-gather(bf16[64,1792]{1,0:T(8,128)(2,1)S(1)} %bitcast.177), channel_id=1, replica_groups=mesh['section'=8,'z'=8,'y'=4] {'y'}, dimensions={0}, use_global_device_ids=true | all-gather | bytes 1146880 | tf_op jit(solution)/shard_map/all_gather | solution.py:286
  250.9 14.4 %all_to_all.277 = bf16[4,32,3584]{2,1,0:T(8,128)(2,1)S(1)} all-to-all(bf16[4,32,3584]{2,1,0:T(8,128)(2,1)S(1)} %bitcast.138), channel_id=1, replica_groups=mesh['section'=8,'z'=8,'y'=4] {'y'}, dimensions={0} | all-to-all | bytes 1835008 | tf_op jit(solution)/shard_map/all_to_all | solution.py:306
  265.6 12.5 %all_to_all.278 = bf16[8,8,1792]{2,1,0:T(8,128)(2,1)S(1)} all-to-all(bf16[8,8,1792]{2,1,0:T(8,128)(2,1)S(1)} %bitcast.166), channel_id=1, replica_groups=mesh['section'=8,'z'=8,'y'=4] {'z'}, dimensions={0} | all-to-all | bytes 458752 | tf_op jit(solution)/shard_map/all_to_all | solution.py:321
  281.6 14.5 %all_to_all.279 = bf16[8,8,1792]{2,1,0:T(8,128)(2,1)S(1)} all-to-all(bf16[8,8,1792]{2,1,0:T(8,128)(2,1)S(1)} %bitcast.159), channel_id=1, replica_groups=mesh['section'=8,'z'=8,'y'=4] {'z'}, dimensions={0} | all-to-all | bytes 458752 | tf_op jit(solution)/shard_map/all_to_all | solution.py:281
  296.1 13.6 %all_gather.38.refs_0_ = bf16[256,1792]{1,0:T(8,128)(2,1)S(1)} all-gather(bf16[64,1792]{1,0:T(8,128)(2,1)S(1)} %bitcast.178), channel_id=1, replica_groups=mesh['section'=8,'z'=8,'y'=4] {'y'}, dimensions={0}, use_global_device_ids=true | all-gather | bytes 1146880 | tf_op jit(solution)/shard_map/all_gather | solution.py:286
  311.7 14.4 %all_to_all.280 = bf16[4,32,3584]{2,1,0:T(8,128)(2,1)S(1)} all-to-all(bf16[4,32,3584]{2,1,0:T(8,128)(2,1)S(1)} %bitcast.139), channel_id=1, replica_groups=mesh['section'=8,'z'=8,'y'=4] {'y'}, dimensions={0} | all-to-all | bytes 1835008 | tf_op jit(solution)/shard_map/all_to_all | solution.py:306
  326.4 12.5 %all_to_all.281 = bf16[8,8,1792]{2,1,0:T(8,128)(2,1)S(1)} all-to-all(bf16[8,8,1792]{2,1,0:T(8,128)(2,1)S(1)} %bitcast.167), channel_id=1, replica_groups=mesh['section'=8,'z'=8,'y'=4] {'z'}, dimensions={0} | all-to-all | bytes 458752 | tf_op jit(solution)/shard_map/all_to_all | solution.py:321
  342.4 14.7 %all_to_all.282 = bf16[8,8,1792]{2,1,0:T(8,128)(2,1)S(1)} all-to-all(bf16[8,8,1792]{2,1,0:T(8,128)(2,1)S(1)} %bitcast.160), channel_id=1, replica_groups=mesh['section'=8,'z'=8,'y'=4] {'z'}, dimensions={0} | all-to-all | bytes 458752 | tf_op jit(solution)/shard_map/all_to_all | solution.py:281
  357.1 13.6 %all_gather.39.refs_0_ = bf16[256,1792]{1,0:T(8,128)(2,1)S(1)} all-gather(bf16[64,1792]{1,0:T(8,128)(2,1)S(1)} %bitcast.179), channel_id=1, replica_groups=mesh['section'=8,'z'=8,'y'=4] {'y'}, dimensions={0}, use_global_device_ids=true | all-gather | bytes 1146880 | tf_op jit(solution)/shard_map/all_gather | solution.py:286
  372.7 14.4 %all_to_all.283 = bf16[4,32,3584]{2,1,0:T(8,128)(2,1)S(1)} all-to-all(bf16[4,32,3584]{2,1,0:T(8,128)(2,1)S(1)} %bitcast.140), channel_id=1, replica_groups=mesh['section'=8,'z'=8,'y'=4] {'y'}, dimensions={0} | all-to-all | bytes 1835008 | tf_op jit(solution)/shard_map/all_to_all | solution.py:306
  387.4 12.5 %all_to_all.284 = bf16[8,8,1792]{2,1,0:T(8,128)(2,1)S(1)} all-to-all(bf16[8,8,1792]{2,1,0:T(8,128)(2,1)S(1)} %bitcast.168), channel_id=1, replica_groups=mesh['section'=8,'z'=8,'y'=4] {'z'}, dimensions={0} | all-to-all | bytes 458752 | tf_op jit(solution)/shard_map/all_to_all | solution.py:321
  403.4 14.6 %all_to_all.285 = bf16[8,8,1792]{2,1,0:T(8,128)(2,1)S(1)} all-to-all(bf16[8,8,1792]{2,1,0:T(8,128)(2,1)S(1)} %bitcast.161), channel_id=1, replica_groups=mesh['section'=8,'z'=8,'y'=4] {'z'}, dimensions={0} | all-to-all | bytes 458752 | tf_op jit(solution)/shard_map/all_to_all | solution.py:281
  418.0 13.9 %all_gather.40.refs_0_ = bf16[256,1792]{1,0:T(8,128)(2,1)S(1)} all-gather(bf16[64,1792]{1,0:T(8,128)(2,1)S(1)} %bitcast.180), channel_id=1, replica_groups=mesh['section'=8,'z'=8,'y'=4] {'y'}, dimensions={0}, use_global_device_ids=true | all-gather | bytes 1146880 | tf_op jit(solution)/shard_map/all_gather | solution.py:286
  445.8 8.8 %all-to-all-done.19 = bf16[4,32,3584]{2,1,0:T(8,128)(2,1)S(1)} async-done(((bf16[4,32,3584]{2,1,0:T(8,128)(2,1)}), bf16[4,32,3584]{2,1,0:T(8,128)(2,1)S(1)}, u32[]{:S(2)}, u32[]{:S(2)}) %all-to-all-start.19) | async-done | bytes 917536 | tf_op jit(solution)/shard_map/all_to_all | solution.py:306
  455.0 13.0 %all_to_all.286 = bf16[8,8,1792]{2,1,0:T(8,128)(2,1)S(1)} all-to-all(bf16[8,8,1792]{2,1,0:T(8,128)(2,1)S(1)} %bitcast.169), channel_id=1, replica_groups=mesh['section'=8,'z'=8,'y'=4] {'z'}, dimensions={0} | all-to-all | bytes 458752 | tf_op jit(solution)/shard_map/all_to_all | solution.py:321
  474.8 14.4 %all_to_all.287 = bf16[8,8,1792]{2,1,0:T(8,128)(2,1)S(1)} all-to-all(bf16[8,8,1792]{2,1,0:T(8,128)(2,1)S(1)} %bitcast.162), channel_id=1, replica_groups=mesh['section'=8,'z'=8,'y'=4] {'z'}, dimensions={0} | all-to-all | bytes 458752 | tf_op jit(solution)/shard_map/all_to_all | solution.py:281
  489.2 19.4 %all_gather.41.refs_0_ = bf16[288,1792]{1,0:T(8,128)(2,1)S(1)} all-gather(bf16[72,1792]{1,0:T(8,128)(2,1)S(1)} %pad_maximum_fusion), channel_id=1, replica_groups=mesh['section'=8,'z'=8,'y'=4] {'y'}, dimensions={0}, use_global_device_ids=true | all-gather | bytes 1290240 | tf_op jit(solution)/shard_map/all_gather | solution.py:286
  520.2 9.4 %all-to-all-done.22 = bf16[4,32,3584]{2,1,0:T(8,128)(2,1)S(1)} async-done(((bf16[4,32,3584]{2,1,0:T(8,128)(2,1)}), bf16[4,32,3584]{2,1,0:T(8,128)(2,1)S(1)}, u32[]{:S(2)}, u32[]{:S(2)}) %all-to-all-start.22) | async-done | bytes 917536 | tf_op jit(solution)/shard_map/all_to_all | solution.py:306
  537.3 10.0 %all-to-all-done.23 = bf16[8,16,1792]{2,1,0:T(8,128)(2,1)S(1)} async-done(((bf16[8,16,1792]{2,1,0:T(8,128)(2,1)}), bf16[8,16,1792]{2,1,0:T(8,128)(2,1)S(1)}, u32[]{:S(2)}, u32[]{:S(2)}) %all-to-all-start.23) | async-done | bytes 458784 | tf_op jit(solution)/shard_map/all_to_all | solution.py:321
  (173 shorter events, 100.8 us)
Async XLA Ops:
  7.2 112.0 %all-gather.5.cloned.1.call-start = ((), (), s32[]{:S(2)}) async-start(), calls=%async_computation.24 | async-start | bytes 4730880 | tf_op jit(solution)/shard_map/all_gather | solution.py:188
  11.8 19.7 %all-to-all-start = ((bf16[8,8,1792]{2,1,0:T(8,128)(2,1)}), bf16[8,8,1792]{2,1,0:T(8,128)(2,1)S(1)}, u32[]{:S(2)}, u32[]{:S(2)}) async-start(bf16[8,8,1792]{2,1,0:T(8,128)(2,1)} %bitcast.10), calls=%async_computation | async-start | bytes 458752 | tf_op jit(solution)/shard_map/all_to_all | solution.py:281
  46.4 2.0 copy-start.1
  48.5 2.0 copy-start.5
  52.6 64.6 %copy-start.6 = (bf16[1,3584,512]{2,1,0:T(8,128)(2,1)S(1)}, bf16[1,3584,512]{2,1,0:T(8,128)(2,1)}, u32[]{:S(2)}) copy-start(bf16[1,3584,512]{2,1,0:T(8,128)(2,1)} %param.26) | copy-start | bytes 11010052
  52.6 64.6 %copy-start.10 = (bf16[1,512,3584]{2,1,0:T(8,128)(2,1)S(1)}, bf16[1,512,3584]{2,1,0:T(8,128)(2,1)}, u32[]{:S(2)}) copy-start(bf16[1,512,3584]{2,1,0:T(8,128)(2,1)} %param.27) | copy-start | bytes 11010052
  54.5 35.2 %copy-start.19 = (bf16[8,8,3584]{2,1,0:T(8,128)(2,1)S(1)}, bf16[8,8,3584]{2,1,0:T(8,128)(2,1)}, u32[]{:S(2)}) copy-start(bf16[8,8,3584]{2,1,0:T(8,128)(2,1)} %param.20) | copy-start | bytes 1376260
  54.6 35.2 %copy-start.16 = (f32[1,3584]{1,0:T(1,128)S(1)}, f32[1,3584]{1,0:T(1,128)}, u32[]{:S(2)}) copy-start(f32[1,3584]{1,0:T(1,128)} %gain.15) | copy-start | bytes 43012
  71.2 45.9 %copy-start.2 = (bf16[1,3584,512]{2,1,0:T(8,128)(2,1)S(1)}, bf16[1,3584,512]{2,1,0:T(8,128)(2,1)}, u32[]{:S(2)}) copy-start(bf16[1,3584,512]{2,1,0:T(8,128)(2,1)} %param.25) | copy-start | bytes 11010052
  87.5 2.2 collective-permute-start
  136.7 45.2 %copy-start.3 = (bf16[1,3584,512]{2,1,0:T(8,128)(2,1)S(1)}, bf16[1,3584,512]{2,1,0:T(8,128)(2,1)}, u32[]{:S(2)}) copy-start(bf16[1,3584,512]{2,1,0:T(8,128)(2,1)} %param.25) | copy-start | bytes 11010052
  151.2 2.2 collective-permute-start.1
  181.9 2.0 copy-start.7
  217.5 2.2 collective-permute-start.2
  278.9 2.2 collective-permute-start.3
  339.7 2.2 collective-permute-start.4
  400.7 2.2 collective-permute-start.5
  431.9 3.2 copy-start.17
  431.9 3.2 copy-start.18
  435.1 2.3 copy-start.13
  439.3 15.4 %all-to-all-start.19 = ((bf16[4,32,3584]{2,1,0:T(8,128)(2,1)}), bf16[4,32,3584]{2,1,0:T(8,128)(2,1)S(1)}, u32[]{:S(2)}, u32[]{:S(2)}) async-start(bf16[4,32,3584]{2,1,0:T(8,128)(2,1)} %bitcast.54), calls=%async_computation.19 | async-start | bytes 1835008 | tf_op jit(solution)/shard_map/all_to_all | solution.py:306
  445.1 84.5 %all-gather.7.cloned.1.call-start = ((), (), s32[]{:S(2)}) async-start(), calls=%async_computation.25 | async-start | bytes 2365440 | tf_op jit(solution)/shard_map/all_gather | solution.py:301
  468.7 2.2 collective-permute-start.6
  470.8 37.8 %copy-start.8 = (bf16[1,3584,512]{2,1,0:T(8,128)(2,1)S(1)}, bf16[1,3584,512]{2,1,0:T(8,128)(2,1)}, u32[]{:S(2)}) copy-start(bf16[1,3584,512]{2,1,0:T(8,128)(2,1)} %param.26) | copy-start | bytes 11010052
  470.9 2.5 copy-start.14
  473.3 35.4 %copy-start.4 = (bf16[1,3584,512]{2,1,0:T(8,128)(2,1)S(1)}, bf16[1,3584,512]{2,1,0:T(8,128)(2,1)}, u32[]{:S(2)}) copy-start(bf16[1,3584,512]{2,1,0:T(8,128)(2,1)} %param.25) | copy-start | bytes 11010052
  508.7 2.1 copy-start.12
  510.8 8.3 %copy-start.22 = (s32[4,1,1]{0,2,1:T(1,128)S(1)}, s32[4,1,1]{0,2,1:T(1,128)}, u32[]{:S(2)}) copy-start(s32[4,1,1]{0,2,1:T(1,128)} %constant.66.clone) | copy-start | bytes 52
  510.8 8.3 %copy-start.21 = (s32[8]{0:T(128)S(1)}, s32[8]{0:T(128)}, u32[]{:S(2)}) copy-start(s32[8]{0:T(128)} %constant.65.clone) | copy-start | bytes 100
  510.8 8.7 %copy-start.20 = (s32[1,8,64]{2,1,0:T(8,128)S(1)}, s32[1,8,64]{2,1,0:T(8,128)}, u32[]{:S(2)}) copy-start(s32[1,8,64]{2,1,0:T(8,128)} %param.30) | copy-start | bytes 6148
  513.9 15.6 %all-to-all-start.22 = ((bf16[4,32,3584]{2,1,0:T(8,128)(2,1)}), bf16[4,32,3584]{2,1,0:T(8,128)(2,1)S(1)}, u32[]{:S(2)}, u32[]{:S(2)}) async-start(bf16[4,32,3584]{2,1,0:T(8,128)(2,1)} %bitcast.60), calls=%async_computation.22 | async-start | bytes 1835008 | tf_op jit(solution)/shard_map/all_to_all | solution.py:306
  530.7 16.6 %all-to-all-start.23 = ((bf16[8,16,1792]{2,1,0:T(8,128)(2,1)}), bf16[8,16,1792]{2,1,0:T(8,128)(2,1)S(1)}, u32[]{:S(2)}, u32[]{:S(2)}) async-start(bf16[8,16,1792]{2,1,0:T(8,128)(2,1)} %fusion.3), calls=%async_computation.23 | async-start | bytes 917504 | tf_op jit(solution)/shard_map/all_to_all | solution.py:321
  (4 other events, 5.6 us)
Sparse Core Ops, SparseCore 0:
  10.6 87.2 all-gather.4
  449.1 72.7 all-gather.6

commit v6 on v5

--- a/solution.py
+++ b/solution.py
@@ -1,3 +1,5 @@
+import functools
+
 import jax
 import jax.numpy as jnp
 import numpy as np
@@ -57,7 +59,7 @@
         grid=(1,),
         out_shape=out_shape,
         in_specs=specs,
-        out_specs=pl.BlockSpec(memory_space=pltpu.VMEM),
+        out_specs=jax.tree.map(lambda _: pl.BlockSpec(memory_space=pltpu.VMEM), out_shape),
         compiler_params=pltpu.CompilerParams(vmem_limit_bytes=limit_mib * 1024 * 1024),
         cost_estimate=pl.CostEstimate(flops=flops, bytes_accessed=moved, transcendentals=0),
     )(*operands, *tables)
@@ -82,16 +84,37 @@
     return jnp.where(hit, 1.0, 0.0), jnp.where(hit, weight, 0.0)
 
 
-def choose_kernel(tokens, gain, routes, out):
+def table_kernel(folded, routes, hits_out, weights_out):
+    for tick in range(routes.shape[0]):
+        for k, offset in enumerate((0, 4)):
+            hits, weights = slot_hits(routes[tick], folded, offset)
+            cols = slice(k * folded, (k + 1) * folded)
+            hits_out[tick, :, cols] = hits
+            weights_out[tick, :, cols] = weights
+
+
+def choose_kernel(made, tokens, gain, table, out):
     folded, half = out.shape
     normed = rms_scale(tokens[...], gain[...]).astype(jnp.bfloat16).astype(jnp.float32)
     picked = 0.0
-    for offset, part in ((0, normed[:, :half]), (4, normed[:, half:])):
-        hits, _ = slot_hits(routes[0], folded, offset)
+    for k, offset in enumerate((0, 4)):
+        if made:
+            hits = table[0, :, k * folded : (k + 1) * folded]
+        else:
+            hits, _ = slot_hits(table[0], folded, offset)
         picked = picked + lax.dot_general(
-            hits, part, (((0,), (0,)), ((), ())), preferred_element_type=jnp.float32
+            hits,
+            normed[:, k * half : (k + 1) * half],
+            (((0,), (0,)), ((), ())),
+            preferred_element_type=jnp.float32,
         )
     out[...] = picked.astype(jnp.bfloat16)
+
+
+def copies_kernel(rows, out):
+    height = rows.shape[0]
+    for k in range(out.shape[0] // height):
+        out[k * height : (k + 1) * height, :] = rows[...]
 
 
 def latent_kernel(rows, attn_gain, kv_gain, w_latent, cosine, sine, out):
@@ -144,14 +167,20 @@
     out[...] = spread.astype(jnp.bfloat16)
 
 
-def combine_kernel(tokens, returned, routes, out):
+def combine_kernel(tokens, returned, table, out):
     folded, half = returned.shape
-    rows = returned[...].astype(jnp.float32)
-    for offset, cols in ((0, slice(0, half)), (4, slice(half, 2 * half))):
-        _, weights = slot_hits(routes[0], folded, offset)
-        moe_sum = jnp.dot(
-            weights, rows, precision=lax.Precision.HIGHEST, preferred_element_type=jnp.float32
-        )
+    span_dev = tokens.shape[0]
+    for k in range(2):
+        cols = slice(k * half, (k + 1) * half)
+        rest = table[0, :, k * folded : (k + 1) * folded]
+        terms = []
+        for _ in range(3):
+            term = rest.astype(jnp.bfloat16)
+            rest = rest - term.astype(jnp.float32)
+            terms.append(term.astype(jnp.float32))
+        terms = jnp.concatenate(terms, axis=0).astype(jnp.bfloat16)
+        sums = matmul(terms, returned[...])
+        moe_sum = sums[:span_dev] + sums[span_dev : 2 * span_dev] + sums[2 * span_dev :]
         out[:, cols] = (tokens[:, cols].astype(jnp.float32) + moe_sum).astype(jnp.bfloat16)
 
 
@@ -266,24 +295,36 @@
             late_rows = side_by_side(project(EARLY, n_sections, gains, latent_full, turns))
             tokens, late_rows = lax.optimization_barrier((tokens, late_rows))
         chosen = in_vmem(
-            choose_kernel,
+            functools.partial(choose_kernel, tick > 0),
             jax.ShapeDtypeStruct((2 * slots, half), jnp.bfloat16),
             (tokens, moe_gain),
             8,
             tick=tick,
-            tables=(routes,),
+            tables=(hits if tick else routes,),
         )
         if tick == 0:
-            chosen, offsets = lax.optimization_barrier((chosen, offsets))
+            held = lax.optimization_barrier((chosen, offsets, routes))
+            chosen, offsets, routes = held
+            table = jax.ShapeDtypeStruct((n_sections, span_dev, 4 * slots), jnp.float32)
+            make = functools.partial(table_kernel, 2 * slots)
+            hits, weighs = in_vmem(make, [table] * 2, (routes,), 8)
             positions = by_tick(offsets)[:, None] + member * span_dev
             positions = positions + jnp.arange(span_dev, dtype=jnp.int32)[None, :]
             turns = rotation(kv_width - LAT, positions.reshape(-1))
         arrived = lax.all_to_all(chosen, "z", split_axis=0, concat_axis=0, tiled=True)
         if last_tick:
+            late_rows = jnp.pad(late_rows, ((0, 8), (0, 0)))
             arrived = jnp.concatenate([arrived, late_rows], axis=0)
         if tick == 0:
-            arrived, turns = lax.optimization_barrier((arrived, turns))
-        token_rows = lax.all_gather(arrived, "y", axis=0, tiled=True)
+            held = lax.optimization_barrier((arrived, turns, hits, weighs))
+            arrived, turns, hits, weighs = held
+        copies = in_vmem(
+            copies_kernel,
+            jax.ShapeDtypeStruct((n_columns * arrived.shape[0], half), jnp.bfloat16),
+            (arrived,),
+            8,
+        )
+        token_rows = lax.all_to_all(copies, "y", split_axis=0, concat_axis=0, tiled=True)
         parts = in_vmem(
             lambda *refs: expert_kernel(n_columns, *refs),
             jax.ShapeDtypeStruct((n_columns * slots, model_width), jnp.bfloat16),
@@ -313,7 +354,7 @@
             12,
         )
         if last_tick:
-            late_rows = token_rows.reshape(n_columns, -1, half)[:, 2 * slots :]
+            late_rows = token_rows.reshape(n_columns, -1, half)[:, 2 * slots : 2 * slots + 8]
             late_rows = apart(late_rows, n_sections - EARLY)
             late = pack_late(late_rows, block_order, EARLY, n_sections)
             summed = jnp.concatenate([summed.reshape(n_planes, -1, half), late], axis=1)
@@ -329,7 +370,7 @@
             (tokens, returned),
             8,
             tick=tick,
-            tables=(routes,),
+            tables=(weighs,),
         )
         if not last_tick:
             layer_in = shifted(layer_out, "section", 1)

time: 558 us -> 587 us (1.052)
  blocking collectives: 403 us -> 435 us
    all_to_all x0 -> x8, blocking collectives: none -> 142 us  [body(): lax.all_to_all(copies, 'y', split_axis=0, concat_axis=0, tiled=True)]
    all_gather x8 -> x0, blocking collectives: 117 us -> none  [body(): token_rows = lax.all_gather(arrived, 'y', axis=0, tiled=True)]
    all_to_all x6, blocking collectives: 93.4 us -> 102 us  [body(): lax.all_to_all(parts, 'y', split_axis=0, concat_axis=0, tiled=True)]
    pallas_call x34 -> x43, Pallas kernels: 34.4 us -> 30.1 us  [in_vmem(): pl.pallas_call(kernel, grid=(1,), out_shape=out_shape, in_specs=specs, ou...]
where the time goes in v6:
time: 587 us; the launch traced here: 586 us
  blocking collectives  435 us (74%)
  waiting for transfers between devices  50.4 us (9%)
  starting transfers between devices  32.7 us (6%)
  Pallas kernels  30.1 us (5%)
  local copies, waits for them, and re-layouts  17.9 us (3%)
  between operations  14.7 us (3%)
    all_to_all x8, blocking collectives, body(): lax.all_to_all(copies, 'y', split_axis=0, concat_axis=0, tiled=True)  142 us
    all_to_all x6, blocking collectives, body(): lax.all_to_all(parts, 'y', split_axis=0, concat_axis=0, tiled=True)  102 us
    all_to_all x7, blocking collectives, body(): lax.all_to_all(chosen, 'z', split_axis=0, concat_axis=0, tiled=True)  99.7 us
    all_to_all x7, blocking collectives, body(): lax.all_to_all(summed, 'z', split_axis=0, concat_axis=0, tiled=True)  91.7 us
    pallas_call x43, Pallas kernels, in_vmem(): pl.pallas_call(kernel, grid=(1,), out_shape=out_shape, in_specs=specs, ou...  30.1 us
    all_to_all x2, waiting for transfers between devices, body(): lax.all_to_all(parts, 'y', split_axis=0, concat_axis=0, tiled=True)  21.3 us
    unnamed x53, local copies, waits for them, and re-layouts  13.7 us
  transfers between devices with their start and end apart: 13, of which 11 were waited for; matrix products, arithmetic and copies ran while one was open for 1% of the time, Pallas kernels for 2%

profile of v6, /device:TPU:8, one launch (start us, length us, event | category | flops | bytes accessed | tf_op | source)
XLA Modules:
  0.0 585.6 jit_solution(182468122104850437)
XLA Ops:
  21.6 9.9 %all-to-all-done = bf16[8,8,1792]{2,1,0:T(8,128)(2,1)S(1)} async-done(((bf16[8,8,1792]{2,1,0:T(8,128)(2,1)}), bf16[8,8,1792]{2,1,0:T(8,128)(2,1)S(1)}, u32[]{:S(2)}, u32[]{:S(2)}) %all-to-all-start) | async-done | bytes 229408 | tf_op jit(solution)/shard_map/all_to_all | solution.py:314
  31.6 16.0 %all_to_all.350 = bf16[4,64,1792]{2,1,0:T(8,128)(2,1)S(1)} all-to-all(bf16[4,64,1792]{2,1,0:T(8,128)(2,1)S(1)} %bitcast.167), channel_id=1, replica_groups=mesh['section'=8,'z'=8,'y'=4] {'y'}, dimensions={0} | all-to-all | bytes 1835008 | tf_op jit(solution)/shard_map/all_to_all | solution.py:327
  55.7 21.6 %all_to_all.351 = bf16[4,32,3584]{2,1,0:T(8,128)(2,1)S(1)} all-to-all(bf16[4,32,3584]{2,1,0:T(8,128)(2,1)S(1)} %bitcast.154), channel_id=1, replica_groups=mesh['section'=8,'z'=8,'y'=4] {'y'}, dimensions={0} | all-to-all | bytes 1835008 | tf_op jit(solution)/shard_map/all_to_all | solution.py:347
  77.6 14.7 %all_to_all.352 = bf16[8,8,1792]{2,1,0:T(8,128)(2,1)S(1)} all-to-all(bf16[8,8,1792]{2,1,0:T(8,128)(2,1)S(1)} %bitcast.195), channel_id=1, replica_groups=mesh['section'=8,'z'=8,'y'=4] {'z'}, dimensions={0} | all-to-all | bytes 458752 | tf_op jit(solution)/shard_map/all_to_all | solution.py:362
  95.1 13.1 %all_to_all.353 = bf16[8,8,1792]{2,1,0:T(8,128)(2,1)S(1)} all-to-all(bf16[8,8,1792]{2,1,0:T(8,128)(2,1)S(1)} %bitcast.188), channel_id=1, replica_groups=mesh['section'=8,'z'=8,'y'=4] {'z'}, dimensions={0} | all-to-all | bytes 458752 | tf_op jit(solution)/shard_map/all_to_all | solution.py:314
  108.3 17.3 %all_to_all.354 = bf16[4,64,1792]{2,1,0:T(8,128)(2,1)S(1)} all-to-all(bf16[4,64,1792]{2,1,0:T(8,128)(2,1)S(1)} %bitcast.169), channel_id=1, replica_groups=mesh['section'=8,'z'=8,'y'=4] {'y'}, dimensions={0} | all-to-all | bytes 1835008 | tf_op jit(solution)/shard_map/all_to_all | solution.py:327
  127.6 17.3 %all_to_all.355 = bf16[4,32,3584]{2,1,0:T(8,128)(2,1)S(1)} all-to-all(bf16[4,32,3584]{2,1,0:T(8,128)(2,1)S(1)} %bitcast.152), channel_id=1, replica_groups=mesh['section'=8,'z'=8,'y'=4] {'y'}, dimensions={0} | all-to-all | bytes 1835008 | tf_op jit(solution)/shard_map/all_to_all | solution.py:347
  145.2 13.7 %all_to_all.356 = bf16[8,8,1792]{2,1,0:T(8,128)(2,1)S(1)} all-to-all(bf16[8,8,1792]{2,1,0:T(8,128)(2,1)S(1)} %bitcast.197), channel_id=1, replica_groups=mesh['section'=8,'z'=8,'y'=4] {'z'}, dimensions={0} | all-to-all | bytes 458752 | tf_op jit(solution)/shard_map/all_to_all | solution.py:362
  161.7 14.5 %all_to_all.357 = bf16[8,8,1792]{2,1,0:T(8,128)(2,1)S(1)} all-to-all(bf16[8,8,1792]{2,1,0:T(8,128)(2,1)S(1)} %bitcast.189), channel_id=1, replica_groups=mesh['section'=8,'z'=8,'y'=4] {'z'}, dimensions={0} | all-to-all | bytes 458752 | tf_op jit(solution)/shard_map/all_to_all | solution.py:314
  176.2 16.6 %all_to_all.358 = bf16[4,64,1792]{2,1,0:T(8,128)(2,1)S(1)} all-to-all(bf16[4,64,1792]{2,1,0:T(8,128)(2,1)S(1)} %bitcast.171), channel_id=1, replica_groups=mesh['section'=8,'z'=8,'y'=4] {'y'}, dimensions={0} | all-to-all | bytes 1835008 | tf_op jit(solution)/shard_map/all_to_all | solution.py:327
  196.8 15.8 %all_to_all.359 = bf16[4,32,3584]{2,1,0:T(8,128)(2,1)S(1)} all-to-all(bf16[4,32,3584]{2,1,0:T(8,128)(2,1)S(1)} %bitcast.157), channel_id=1, replica_groups=mesh['section'=8,'z'=8,'y'=4] {'y'}, dimensions={0} | all-to-all | bytes 1835008 | tf_op jit(solution)/shard_map/all_to_all | solution.py:347
  212.9 12.5 %all_to_all.360 = bf16[8,8,1792]{2,1,0:T(8,128)(2,1)S(1)} all-to-all(bf16[8,8,1792]{2,1,0:T(8,128)(2,1)S(1)} %bitcast.199), channel_id=1, replica_groups=mesh['section'=8,'z'=8,'y'=4] {'z'}, dimensions={0} | all-to-all | bytes 458752 | tf_op jit(solution)/shard_map/all_to_all | solution.py:362
  228.2 14.4 %all_to_all.361 = bf16[8,8,1792]{2,1,0:T(8,128)(2,1)S(1)} all-to-all(bf16[8,8,1792]{2,1,0:T(8,128)(2,1)S(1)} %bitcast.190), channel_id=1, replica_groups=mesh['section'=8,'z'=8,'y'=4] {'z'}, dimensions={0} | all-to-all | bytes 458752 | tf_op jit(solution)/shard_map/all_to_all | solution.py:314
  242.7 16.6 %all_to_all.362 = bf16[4,64,1792]{2,1,0:T(8,128)(2,1)S(1)} all-to-all(bf16[4,64,1792]{2,1,0:T(8,128)(2,1)S(1)} %bitcast.173), channel_id=1, replica_groups=mesh['section'=8,'z'=8,'y'=4] {'y'}, dimensions={0} | all-to-all | bytes 1835008 | tf_op jit(solution)/shard_map/all_to_all | solution.py:327
  261.3 15.8 %all_to_all.363 = bf16[4,32,3584]{2,1,0:T(8,128)(2,1)S(1)} all-to-all(bf16[4,32,3584]{2,1,0:T(8,128)(2,1)S(1)} %bitcast.159), channel_id=1, replica_groups=mesh['section'=8,'z'=8,'y'=4] {'y'}, dimensions={0} | all-to-all | bytes 1835008 | tf_op jit(solution)/shard_map/all_to_all | solution.py:347
  277.3 12.5 %all_to_all.364 = bf16[8,8,1792]{2,1,0:T(8,128)(2,1)S(1)} all-to-all(bf16[8,8,1792]{2,1,0:T(8,128)(2,1)S(1)} %bitcast.201), channel_id=1, replica_groups=mesh['section'=8,'z'=8,'y'=4] {'z'}, dimensions={0} | all-to-all | bytes 458752 | tf_op jit(solution)/shard_map/all_to_all | solution.py:362
  292.7 14.4 %all_to_all.365 = bf16[8,8,1792]{2,1,0:T(8,128)(2,1)S(1)} all-to-all(bf16[8,8,1792]{2,1,0:T(8,128)(2,1)S(1)} %bitcast.191), channel_id=1, replica_groups=mesh['section'=8,'z'=8,'y'=4] {'z'}, dimensions={0} | all-to-all | bytes 458752 | tf_op jit(solution)/shard_map/all_to_all | solution.py:314
  307.1 16.6 %all_to_all.366 = bf16[4,64,1792]{2,1,0:T(8,128)(2,1)S(1)} all-to-all(bf16[4,64,1792]{2,1,0:T(8,128)(2,1)S(1)} %bitcast.175), channel_id=1, replica_groups=mesh['section'=8,'z'=8,'y'=4] {'y'}, dimensions={0} | all-to-all | bytes 1835008 | tf_op jit(solution)/shard_map/all_to_all | solution.py:327
  325.7 15.8 %all_to_all.367 = bf16[4,32,3584]{2,1,0:T(8,128)(2,1)S(1)} all-to-all(bf16[4,32,3584]{2,1,0:T(8,128)(2,1)S(1)} %bitcast.161), channel_id=1, replica_groups=mesh['section'=8,'z'=8,'y'=4] {'y'}, dimensions={0} | all-to-all | bytes 1835008 | tf_op jit(solution)/shard_map/all_to_all | solution.py:347
  341.7 12.5 %all_to_all.368 = bf16[8,8,1792]{2,1,0:T(8,128)(2,1)S(1)} all-to-all(bf16[8,8,1792]{2,1,0:T(8,128)(2,1)S(1)} %bitcast.203), channel_id=1, replica_groups=mesh['section'=8,'z'=8,'y'=4] {'z'}, dimensions={0} | all-to-all | bytes 458752 | tf_op jit(solution)/shard_map/all_to_all | solution.py:362
  357.1 14.4 %all_to_all.369 = bf16[8,8,1792]{2,1,0:T(8,128)(2,1)S(1)} all-to-all(bf16[8,8,1792]{2,1,0:T(8,128)(2,1)S(1)} %bitcast.192), channel_id=1, replica_groups=mesh['section'=8,'z'=8,'y'=4] {'z'}, dimensions={0} | all-to-all | bytes 458752 | tf_op jit(solution)/shard_map/all_to_all | solution.py:314
  371.5 16.6 %all_to_all.370 = bf16[4,64,1792]{2,1,0:T(8,128)(2,1)S(1)} all-to-all(bf16[4,64,1792]{2,1,0:T(8,128)(2,1)S(1)} %bitcast.177), channel_id=1, replica_groups=mesh['section'=8,'z'=8,'y'=4] {'y'}, dimensions={0} | all-to-all | bytes 1835008 | tf_op jit(solution)/shard_map/all_to_all | solution.py:327
  390.1 15.8 %all_to_all.371 = bf16[4,32,3584]{2,1,0:T(8,128)(2,1)S(1)} all-to-all(bf16[4,32,3584]{2,1,0:T(8,128)(2,1)S(1)} %bitcast.163), channel_id=1, replica_groups=mesh['section'=8,'z'=8,'y'=4] {'y'}, dimensions={0} | all-to-all | bytes 1835008 | tf_op jit(solution)/shard_map/all_to_all | solution.py:347
  406.2 12.5 %all_to_all.372 = bf16[8,8,1792]{2,1,0:T(8,128)(2,1)S(1)} all-to-all(bf16[8,8,1792]{2,1,0:T(8,128)(2,1)S(1)} %bitcast.205), channel_id=1, replica_groups=mesh['section'=8,'z'=8,'y'=4] {'z'}, dimensions={0} | all-to-all | bytes 458752 | tf_op jit(solution)/shard_map/all_to_all | solution.py:362
  421.5 14.4 %all_to_all.373 = bf16[8,8,1792]{2,1,0:T(8,128)(2,1)S(1)} all-to-all(bf16[8,8,1792]{2,1,0:T(8,128)(2,1)S(1)} %bitcast.193), channel_id=1, replica_groups=mesh['section'=8,'z'=8,'y'=4] {'z'}, dimensions={0} | all-to-all | bytes 458752 | tf_op jit(solution)/shard_map/all_to_all | solution.py:314
  435.9 16.6 %all_to_all.374 = bf16[4,64,1792]{2,1,0:T(8,128)(2,1)S(1)} all-to-all(bf16[4,64,1792]{2,1,0:T(8,128)(2,1)S(1)} %bitcast.179), channel_id=1, replica_groups=mesh['section'=8,'z'=8,'y'=4] {'y'}, dimensions={0} | all-to-all | bytes 1835008 | tf_op jit(solution)/shard_map/all_to_all | solution.py:327
  465.6 11.2 %all-to-all-done.26 = bf16[4,32,3584]{2,1,0:T(8,128)(2,1)S(1)} async-done(((bf16[4,32,3584]{2,1,0:T(8,128)(2,1)}), bf16[4,32,3584]{2,1,0:T(8,128)(2,1)S(1)}, u32[]{:S(2)}, u32[]{:S(2)}) %all-to-all-start.26) | async-done | bytes 917536 | tf_op jit(solution)/shard_map/all_to_all | solution.py:347
  477.0 13.3 %all_to_all.375 = bf16[8,8,1792]{2,1,0:T(8,128)(2,1)S(1)} all-to-all(bf16[8,8,1792]{2,1,0:T(8,128)(2,1)S(1)} %bitcast.207), channel_id=1, replica_groups=mesh['section'=8,'z'=8,'y'=4] {'z'}, dimensions={0} | all-to-all | bytes 458752 | tf_op jit(solution)/shard_map/all_to_all | solution.py:362
  496.4 14.6 %all_to_all.376 = bf16[8,8,1792]{2,1,0:T(8,128)(2,1)S(1)} all-to-all(bf16[8,8,1792]{2,1,0:T(8,128)(2,1)S(1)} %bitcast.187), channel_id=1, replica_groups=mesh['section'=8,'z'=8,'y'=4] {'z'}, dimensions={0} | all-to-all | bytes 458752 | tf_op jit(solution)/shard_map/all_to_all | solution.py:314
  511.2 25.4 %all_to_all.377 = bf16[4,80,1792]{2,1,0:T(8,128)(2,1)S(1)} all-to-all(bf16[4,80,1792]{2,1,0:T(8,128)(2,1)S(1)} %bitcast.151), channel_id=1, replica_groups=mesh['section'=8,'z'=8,'y'=4] {'y'}, dimensions={0} | all-to-all | bytes 2293760 | tf_op jit(solution)/shard_map/all_to_all | solution.py:327
  545.8 10.2 %all-to-all-done.30 = bf16[4,32,3584]{2,1,0:T(8,128)(2,1)S(1)} async-done(((bf16[4,32,3584]{2,1,0:T(8,128)(2,1)}), bf16[4,32,3584]{2,1,0:T(8,128)(2,1)S(1)}, u32[]{:S(2)}, u32[]{:S(2)}) %all-to-all-start.30) | async-done | bytes 917536 | tf_op jit(solution)/shard_map/all_to_all | solution.py:347
  565.5 11.7 %all-to-all-done.31 = bf16[8,16,1792]{2,1,0:T(8,128)(2,1)S(1)} async-done(((bf16[8,16,1792]{2,1,0:T(8,128)(2,1)}), bf16[8,16,1792]{2,1,0:T(8,128)(2,1)S(1)}, u32[]{:S(2)}, u32[]{:S(2)}) %all-to-all-start.31) | async-done | bytes 458784 | tf_op jit(solution)/shard_map/all_to_all | solution.py:362
  (182 shorter events, 92.9 us)
Async XLA Ops:
  7.2 120.4 %all-gather.5.cloned.1.call-start = ((), (), s32[]{:S(2)}) async-start(), calls=%async_computation.32 | async-start | bytes 4730880 | tf_op jit(solution)/shard_map/all_gather | solution.py:217
  11.8 19.7 %all-to-all-start = ((bf16[8,8,1792]{2,1,0:T(8,128)(2,1)}), bf16[8,8,1792]{2,1,0:T(8,128)(2,1)S(1)}, u32[]{:S(2)}, u32[]{:S(2)}) async-start(bf16[8,8,1792]{2,1,0:T(8,128)(2,1)} %bitcast.10), calls=%async_computation | async-start | bytes 458752 | tf_op jit(solution)/shard_map/all_to_all | solution.py:314
  47.6 2.0 copy-start.1
  49.6 2.0 copy-start.5
  53.7 41.0 %copy-start.19 = (bf16[8,8,3584]{2,1,0:T(8,128)(2,1)S(1)}, bf16[8,8,3584]{2,1,0:T(8,128)(2,1)}, u32[]{:S(2)}) copy-start(bf16[8,8,3584]{2,1,0:T(8,128)(2,1)} %param.20) | copy-start | bytes 1376260
  53.7 71.9 %copy-start.10 = (bf16[1,512,3584]{2,1,0:T(8,128)(2,1)S(1)}, bf16[1,512,3584]{2,1,0:T(8,128)(2,1)}, u32[]{:S(2)}) copy-start(bf16[1,512,3584]{2,1,0:T(8,128)(2,1)} %param.27) | copy-start | bytes 11010052
  55.6 39.1 %copy-start.16 = (f32[1,3584]{1,0:T(1,128)S(1)}, f32[1,3584]{1,0:T(1,128)}, u32[]{:S(2)}) copy-start(f32[1,3584]{1,0:T(1,128)} %gain.15) | copy-start | bytes 43012
  55.7 70.0 %copy-start.6 = (bf16[1,3584,512]{2,1,0:T(8,128)(2,1)S(1)}, bf16[1,3584,512]{2,1,0:T(8,128)(2,1)}, u32[]{:S(2)}) copy-start(bf16[1,3584,512]{2,1,0:T(8,128)(2,1)} %param.26) | copy-start | bytes 11010052
  77.6 48.0 %copy-start.2 = (bf16[1,3584,512]{2,1,0:T(8,128)(2,1)S(1)}, bf16[1,3584,512]{2,1,0:T(8,128)(2,1)}, u32[]{:S(2)}) copy-start(bf16[1,3584,512]{2,1,0:T(8,128)(2,1)} %param.25) | copy-start | bytes 11010052
  92.5 2.2 collective-permute-start
  127.6 65.2 %copy-start.7 = (bf16[1,3584,512]{2,1,0:T(8,128)(2,1)S(1)}, bf16[1,3584,512]{2,1,0:T(8,128)(2,1)}, u32[]{:S(2)}) copy-start(bf16[1,3584,512]{2,1,0:T(8,128)(2,1)} %param.26) | copy-start | bytes 11010052
  145.2 47.6 %copy-start.3 = (bf16[1,3584,512]{2,1,0:T(8,128)(2,1)S(1)}, bf16[1,3584,512]{2,1,0:T(8,128)(2,1)}, u32[]{:S(2)}) copy-start(bf16[1,3584,512]{2,1,0:T(8,128)(2,1)} %param.25) | copy-start | bytes 11010052
  159.1 2.2 collective-permute-start.1
  225.7 2.2 collective-permute-start.2
  290.1 2.2 collective-permute-start.3
  354.5 2.2 collective-permute-start.4
  418.9 2.2 collective-permute-start.5
  452.5 3.2 copy-start.17
  452.5 3.2 copy-start.18
  455.8 2.3 copy-start.13
  459.9 16.8 %all-to-all-start.26 = ((bf16[4,32,3584]{2,1,0:T(8,128)(2,1)}), bf16[4,32,3584]{2,1,0:T(8,128)(2,1)S(1)}, u32[]{:S(2)}, u32[]{:S(2)}) async-start(bf16[4,32,3584]{2,1,0:T(8,128)(2,1)} %bitcast.68), calls=%async_computation.26 | async-start | bytes 1835008 | tf_op jit(solution)/shard_map/all_to_all | solution.py:347
  464.8 91.1 %all-gather.7.cloned.1.call-start = ((), (), s32[]{:S(2)}) async-start(), calls=%async_computation.33 | async-start | bytes 2365440 | tf_op jit(solution)/shard_map/all_gather | solution.py:342
  476.7 59.8 %copy-start.12 = (bf16[1,512,3584]{2,1,0:T(8,128)(2,1)S(1)}, bf16[1,512,3584]{2,1,0:T(8,128)(2,1)}, u32[]{:S(2)}) copy-start(bf16[1,512,3584]{2,1,0:T(8,128)(2,1)} %param.27) | copy-start | bytes 11010052
  490.6 2.2 collective-permute-start.6
  492.8 2.3 copy-start.14
  495.1 41.5 %copy-start.8 = (bf16[1,3584,512]{2,1,0:T(8,128)(2,1)S(1)}, bf16[1,3584,512]{2,1,0:T(8,128)(2,1)}, u32[]{:S(2)}) copy-start(bf16[1,3584,512]{2,1,0:T(8,128)(2,1)} %param.26) | copy-start | bytes 11010052
  496.4 40.1 %copy-start.4 = (bf16[1,3584,512]{2,1,0:T(8,128)(2,1)S(1)}, bf16[1,3584,512]{2,1,0:T(8,128)(2,1)}, u32[]{:S(2)}) copy-start(bf16[1,3584,512]{2,1,0:T(8,128)(2,1)} %param.25) | copy-start | bytes 11010052
  536.5 8.1 %copy-start.22 = (s32[4,1,1]{0,2,1:T(1,128)S(1)}, s32[4,1,1]{0,2,1:T(1,128)}, u32[]{:S(2)}) copy-start(s32[4,1,1]{0,2,1:T(1,128)} %constant.66.clone) | copy-start | bytes 52
  536.6 8.1 %copy-start.21 = (s32[8]{0:T(128)S(1)}, s32[8]{0:T(128)}, u32[]{:S(2)}) copy-start(s32[8]{0:T(128)} %constant.65.clone) | copy-start | bytes 100
  536.6 8.4 %copy-start.20 = (s32[1,8,64]{2,1,0:T(8,128)S(1)}, s32[1,8,64]{2,1,0:T(8,128)}, u32[]{:S(2)}) copy-start(s32[1,8,64]{2,1,0:T(8,128)} %param.30) | copy-start | bytes 6148
  539.7 16.2 %all-to-all-start.30 = ((bf16[4,32,3584]{2,1,0:T(8,128)(2,1)}), bf16[4,32,3584]{2,1,0:T(8,128)(2,1)S(1)}, u32[]{:S(2)}, u32[]{:S(2)}) async-start(bf16[4,32,3584]{2,1,0:T(8,128)(2,1)} %bitcast.76), calls=%async_computation.30 | async-start | bytes 1835008 | tf_op jit(solution)/shard_map/all_to_all | solution.py:347
  557.0 20.1 %all-to-all-start.31 = ((bf16[8,16,1792]{2,1,0:T(8,128)(2,1)}), bf16[8,16,1792]{2,1,0:T(8,128)(2,1)S(1)}, u32[]{:S(2)}, u32[]{:S(2)}) async-start(bf16[8,16,1792]{2,1,0:T(8,128)(2,1)} %fusion.4), calls=%async_computation.31 | async-start | bytes 917504 | tf_op jit(solution)/shard_map/all_to_all | solution.py:362
  (4 other events, 5.6 us)
Sparse Core Ops, SparseCore 0:
  10.6 89.0 all-gather.4
  468.8 75.5 all-gather.6

commit v7 on v6

--- a/solution.py
+++ b/solution.py
@@ -111,12 +111,6 @@
     out[...] = picked.astype(jnp.bfloat16)
 
 
-def copies_kernel(rows, out):
-    height = rows.shape[0]
-    for k in range(out.shape[0] // height):
-        out[k * height : (k + 1) * height, :] = rows[...]
-
-
 def latent_kernel(rows, attn_gain, kv_gain, w_latent, cosine, sine, out):
     normed = rms_scale(rows[...], attn_gain[...]).astype(jnp.bfloat16)
     latent = matmul(normed, w_latent[...])
@@ -153,17 +147,28 @@
         out[:, cols] = matmul(hidden, w_down[:, cols]).astype(jnp.bfloat16)
 
 
-def total_kernel(parts, quarters, out):
-    folded, half = out.shape
-    slots = folded // 2
+def total_kernel(columns, quarters, *rest):
+    out = rest[-1]
+    height, half = out.shape
+    slots = quarters.shape[0] // columns
+    group = height // (slots // 4)
     total = quarters[:slots, :].astype(jnp.float32)
-    for k in range(1, parts):
+    for k in range(1, columns):
         total = total + quarters[k * slots : (k + 1) * slots, :].astype(jnp.float32)
     total = total.astype(jnp.bfloat16)
-    place = lambda row: (row // 8) * 4 + row % 4
-    first = one_hot(folded, slots, place, lambda row: row % 8 < 4)
-    second = one_hot(folded, slots, place, lambda row: row % 8 >= 4)
+    place = lambda row: (row // group) * 4 + row % 4
+    first = one_hot(height, slots, place, lambda row: row % group < 4)
+    second = one_hot(height, slots, place, lambda row: (row % group >= 4) & (row % group < 8))
     spread = matmul(first, total[:, :half]) + matmul(second, total[:, half:])
+    if len(rest) > 1:
+        gathered, pick = rest[0], rest[1]
+        stride = gathered.shape[0] // columns
+        source = lambda row: (row // 8) * stride + stride - 8 + row % 8
+        kv_rows = matmul(one_hot(8 * columns, gathered.shape[0], source), gathered[...])
+        picked = matmul(pick[...], kv_rows.astype(jnp.bfloat16)).astype(jnp.bfloat16)
+        place = lambda row: (row // group) * 8 + row % 8
+        third = one_hot(height, picked.shape[0], place, lambda row: row % group >= 8)
+        spread = spread + matmul(third, picked)
     out[...] = spread.astype(jnp.bfloat16)
 
 
@@ -237,62 +242,39 @@
         block = jnp.repeat(order, KVBLK, axis=-1)
         return block * KVBLK + np.arange(block.shape[-1], dtype=np.int32) % KVBLK
 
-    def deliver_whole(gathered, block_order, first, last):
-        count = last - first
-        gathered = gathered.reshape(n_members, count, span_dev, kv_width)
+    def early_picks(block_order, count):
         order = lax.dynamic_slice_in_dim(
-            block_order[first:last], member * per_owner, per_owner, 1
+            block_order[:count], member * per_owner, per_owner, 1
         )
         every = np.arange(n_members * span_dev, dtype=np.int32)
         pick = (owned_rows(order)[..., None] == every).astype(jnp.bfloat16)
-        pick = pick.reshape(count, span_dev, n_members, span_dev)
+        return pick.reshape(count, span_dev, n_members, span_dev)
+
+    def deliver_early(gathered, pick):
+        gathered = gathered.reshape(n_members, pick.shape[0], span_dev, kv_width)
         return jnp.einsum(
             "tdmr,mtrk->tdk", pick, gathered, preferred_element_type=jnp.float32
         ).astype(jnp.bfloat16)
 
-    def side_by_side(rows):
-        wide = [rows[..., i : i + 8, :] for i in range(0, rows.shape[-2], 8)]
-        wide = jnp.concatenate(wide, axis=-1)
-        spare = model_width // 2 - wide.shape[-1]
-        return jnp.pad(wide, [(0, 0)] * (wide.ndim - 1) + [(0, spare)])
-
-    def apart(wide, count):
-        pieces = [wide[..., i * kv_width : (i + 1) * kv_width] for i in range(count)]
-        return jnp.concatenate(pieces, axis=-2)
-
-    def pack_late(column_rows, block_order, first, last):
-        count = last - first
-        order = block_order[first:last].reshape(count, n_planes, n_columns, per_owner)
-        order = lax.dynamic_index_in_dim(order, column, 2, keepdims=False)
-        wanted = jnp.transpose(owned_rows(order), (1, 0, 2))
-        col = np.arange(n_columns, dtype=np.int32)[:, None, None]
-        tick = np.arange(count, dtype=np.int32)[None, :, None]
-        row = np.arange(span_dev, dtype=np.int32)[None, None, :]
-        held = (plane * n_columns + col) * span_dev + row + 0 * tick
-        same = tick + 0 * held == np.arange(count, dtype=np.int32)[:, None, None, None]
-        hit = (wanted[..., None, None, None] == held) & same[:, None]
-        hit = hit.reshape(n_planes * count * span_dev, -1).astype(jnp.bfloat16)
-        source = column_rows.reshape(-1, kv_width)
-        packed = matmul(hit, source).astype(jnp.bfloat16)
-        return side_by_side(packed.reshape(n_planes, count * span_dev, kv_width))
-
-    def unpack_late(arrived, first, last):
-        count = last - first
-        rows = jnp.sum(arrived.astype(jnp.float32), axis=0).astype(jnp.bfloat16)
-        return apart(rows, count).reshape(count, span_dev, kv_width)
+    def late_picks(block_order):
+        order = block_order[-1].reshape(n_planes, n_columns, per_owner)
+        order = lax.dynamic_index_in_dim(order, column, 1, keepdims=False)
+        held = plane * n_columns * span_dev + np.arange(n_columns * span_dev, dtype=np.int32)
+        pick = (owned_rows(order)[..., None] == held).astype(jnp.bfloat16)
+        return pick.reshape(n_planes * span_dev, n_columns * span_dev)
 
     half = model_width // 2
     slots = experts * capacity
     tick_rows = []
-    layer_in = jnp.zeros((span_dev, model_width), jnp.bfloat16)
     gains = (attn_gain, kv_gain)
     flops = 2 * 3 * n_columns * slots * model_width * local_gate.shape[1]
     for tick in range(n_sections):
         last_tick = tick + 1 == n_sections
-        tokens = jnp.where(section_id == 0, spans[tick], layer_in)
+        tokens = jnp.where(is_first, spans[tick], layer_in) if tick else spans[0]
         tick_rows.append(tokens)
         if last_tick:
-            late_rows = side_by_side(project(EARLY, n_sections, gains, latent_full, turns))
+            late_rows = project(EARLY, n_sections, gains, latent_full, turns)
+            late_rows = jnp.pad(late_rows, ((0, 0), (0, half - kv_width)))
             tokens, late_rows = lax.optimization_barrier((tokens, late_rows))
         chosen = in_vmem(
             functools.partial(choose_kernel, tick > 0),
@@ -303,8 +285,11 @@
             tables=(hits if tick else routes,),
         )
         if tick == 0:
-            held = lax.optimization_barrier((chosen, offsets, routes))
-            chosen, offsets, routes = held
+            held = (chosen, offsets, routes, owner_map, section_id == 0)
+            held = lax.optimization_barrier(held)
+            chosen, offsets, routes, owner_map, is_first = held
+            block_order = by_tick(owner_map[0])
+            picks = early_picks(block_order, EARLY), late_picks(block_order)
             table = jax.ShapeDtypeStruct((n_sections, span_dev, 4 * slots), jnp.float32)
             make = functools.partial(table_kernel, 2 * slots)
             hits, weighs = in_vmem(make, [table] * 2, (routes,), 8)
@@ -313,18 +298,11 @@
             turns = rotation(kv_width - LAT, positions.reshape(-1))
         arrived = lax.all_to_all(chosen, "z", split_axis=0, concat_axis=0, tiled=True)
         if last_tick:
-            late_rows = jnp.pad(late_rows, ((0, 8), (0, 0)))
             arrived = jnp.concatenate([arrived, late_rows], axis=0)
         if tick == 0:
-            held = lax.optimization_barrier((arrived, turns, hits, weighs))
-            arrived, turns, hits, weighs = held
-        copies = in_vmem(
-            copies_kernel,
-            jax.ShapeDtypeStruct((n_columns * arrived.shape[0], half), jnp.bfloat16),
-            (arrived,),
-            8,
-        )
-        token_rows = lax.all_to_all(copies, "y", split_axis=0, concat_axis=0, tiled=True)
+            held = lax.optimization_barrier((arrived, turns, hits, weighs, picks))
+            arrived, turns, hits, weighs, picks = held
+        token_rows = lax.all_gather(arrived, "y", axis=0, tiled=True)
         parts = in_vmem(
             lambda *refs: expert_kernel(n_columns, *refs),
             jax.ShapeDtypeStruct((n_columns * slots, model_width), jnp.bfloat16),
@@ -340,29 +318,20 @@
             early_rows = project(0, EARLY, gains, latent_full, turns)
             parts, early_rows = lax.optimization_barrier((parts, early_rows))
             early = lax.all_gather(early_rows, ("z", "y"), axis=0)
-        if last_tick:
-            held = (parts, token_rows, owner_map)
-            parts, token_rows, owner_map = lax.optimization_barrier(held)
-            block_order = by_tick(owner_map[0])
         quarters = lax.all_to_all(parts, "y", split_axis=0, concat_axis=0, tiled=True)
         if last_tick:
             quarters, early = lax.optimization_barrier((quarters, early))
         summed = in_vmem(
-            lambda *refs: total_kernel(n_columns, *refs),
-            jax.ShapeDtypeStruct((2 * slots, half), jnp.bfloat16),
-            (quarters,),
+            functools.partial(total_kernel, n_columns),
+            jax.ShapeDtypeStruct(((4 if last_tick else 2) * slots, half), jnp.bfloat16),
+            (quarters, token_rows, picks[1]) if last_tick else (quarters,),
             12,
         )
-        if last_tick:
-            late_rows = token_rows.reshape(n_columns, -1, half)[:, 2 * slots : 2 * slots + 8]
-            late_rows = apart(late_rows, n_sections - EARLY)
-            late = pack_late(late_rows, block_order, EARLY, n_sections)
-            summed = jnp.concatenate([summed.reshape(n_planes, -1, half), late], axis=1)
-            summed = summed.reshape(-1, half)
         returned = lax.all_to_all(summed, "z", split_axis=0, concat_axis=0, tiled=True)
         if last_tick:
             returned = returned.reshape(n_planes, -1, half)
-            late = unpack_late(returned[:, -8:], EARLY, n_sections)
+            late = jnp.sum(returned[:, -8:, :kv_width].astype(jnp.float32), axis=0)
+            late = late.astype(jnp.bfloat16)[None]
             returned = returned[:, :-8].reshape(-1, half)
         layer_out = in_vmem(
             combine_kernel,
@@ -374,7 +343,7 @@
         )
         if not last_tick:
             layer_in = shifted(layer_out, "section", 1)
-    early = deliver_whole(early, block_order, 0, EARLY)
+    early = deliver_early(early, picks[0])
     delivered = [early, late]
     blank = jnp.zeros((n_spans, span_dev, kv_width), jnp.bfloat16)
     kv_ticks = jnp.concatenate(delivered + [blank], axis=0)

time: 587 us -> 549 us (0.935)
  waiting for transfers between devices: 50.4 us -> 25.1 us
  starting transfers between devices: 32.7 us -> 21.8 us
    all_to_all x8 -> x0, blocking collectives: 142 us -> none  [body(): lax.all_to_all(copies, 'y', split_axis=0, concat_axis=0, tiled=True)]
    all_gather x0 -> x8, blocking collectives: none -> 114 us  [body(): token_rows = lax.all_gather(arrived, 'y', axis=0, tiled=True)]
    all_to_all x6 -> x8, blocking collectives: 102 us -> 126 us  [body(): lax.all_to_all(parts, 'y', split_axis=0, concat_axis=0, tiled=True)]
    all_to_all x2 -> x0, waiting for transfers between devices: 21.3 us -> none  [body(): lax.all_to_all(parts, 'y', split_axis=0, concat_axis=0, tiled=True)]
    all_to_all x2 -> x0, starting transfers between devices: 9.86 us -> none  [body(): lax.all_to_all(parts, 'y', split_axis=0, concat_axis=0, tiled=True)]
    unnamed x53 -> x47, local copies, waits for them, and re-layouts: 13.7 us -> 15.8 us
    pallas_call x43 -> x35, Pallas kernels: 30.1 us -> 29 us  [in_vmem(): pl.pallas_call(kernel, grid=(1,), out_shape=out_shape, in_specs=specs, ou...]
  transfers between devices with their start and end apart: 13 -> 11, of which waited for: 11 -> 9; matrix products, arithmetic and copies ran while one was open for 1% -> 2% of each run, Pallas kernels for 2% -> 2%
where the time goes in v7:
time: 549 us; the launch traced here: 547 us
  blocking collectives  431 us (79%)
  Pallas kernels  29 us (5%)
  waiting for transfers between devices  25.1 us (5%)
  local copies, waits for them, and re-layouts  22 us (4%)
  starting transfers between devices  21.8 us (4%)
  between operations  14.7 us (3%)
    all_to_all x8, blocking collectives, body(): lax.all_to_all(parts, 'y', split_axis=0, concat_axis=0, tiled=True)  126 us
    all_gather x8, blocking collectives, body(): token_rows = lax.all_gather(arrived, 'y', axis=0, tiled=True)  114 us
    all_to_all x7, blocking collectives, body(): lax.all_to_all(chosen, 'z', split_axis=0, concat_axis=0, tiled=True)  99.7 us
    all_to_all x7, blocking collectives, body(): lax.all_to_all(summed, 'z', split_axis=0, concat_axis=0, tiled=True)  92.1 us
    pallas_call x35, Pallas kernels, in_vmem(): pl.pallas_call(kernel, grid=(1,), out_shape=out_shape, in_specs=specs, ou...  29 us
    unnamed x47, local copies, waits for them, and re-layouts  15.8 us
    all_to_all x1, waiting for transfers between devices, body(): lax.all_to_all(summed, 'z', split_axis=0, concat_axis=0, tiled=True)  11.7 us
  transfers between devices with their start and end apart: 11, of which 9 were waited for; matrix products, arithmetic and copies ran while one was open for 2% of the time, Pallas kernels for 2%

profile of v7, /device:TPU:8, one launch (start us, length us, event | category | flops | bytes accessed | tf_op | source)
XLA Modules:
  0.0 547.3 jit_solution(5612704882800585612)
XLA Ops:
  11.8 8.5 %all-to-all-start = ((bf16[8,8,1792]{2,1,0:T(8,128)(2,1)}), bf16[8,8,1792]{2,1,0:T(8,128)(2,1)S(1)}, u32[]{:S(2)}, u32[]{:S(2)}) async-start(bf16[8,8,1792]{2,1,0:T(8,128)(2,1)} %bitcast.10), calls=%async_computation | async-start | bytes 458752 | tf_op jit(solution)/shard_map/all_to_all | solution.py:299
  31.5 14.5 %all_gather.33.refs_0_ = bf16[256,1792]{1,0:T(8,128)(2,1)S(1)} all-gather(bf16[64,1792]{1,0:T(8,128)(2,1)S(1)} %bitcast.160), channel_id=1, replica_groups=mesh['section'=8,'z'=8,'y'=4] {'y'}, dimensions={0}, use_global_device_ids=true | all-gather | bytes 1146880 | tf_op jit(solution)/shard_map/all_gather | solution.py:305
  54.1 16.8 %all_to_all.271 = bf16[4,32,3584]{2,1,0:T(8,128)(2,1)S(1)} all-to-all(bf16[4,32,3584]{2,1,0:T(8,128)(2,1)S(1)} %bitcast.122), channel_id=1, replica_groups=mesh['section'=8,'z'=8,'y'=4] {'y'}, dimensions={0} | all-to-all | bytes 1835008 | tf_op jit(solution)/shard_map/all_to_all | solution.py:321
  71.1 15.2 %all_to_all.272 = bf16[8,8,1792]{2,1,0:T(8,128)(2,1)S(1)} all-to-all(bf16[8,8,1792]{2,1,0:T(8,128)(2,1)S(1)} %bitcast.150), channel_id=1, replica_groups=mesh['section'=8,'z'=8,'y'=4] {'z'}, dimensions={0} | all-to-all | bytes 458752 | tf_op jit(solution)/shard_map/all_to_all | solution.py:330
  89.2 13.3 %all_to_all.273 = bf16[8,8,1792]{2,1,0:T(8,128)(2,1)S(1)} all-to-all(bf16[8,8,1792]{2,1,0:T(8,128)(2,1)S(1)} %bitcast.144), channel_id=1, replica_groups=mesh['section'=8,'z'=8,'y'=4] {'z'}, dimensions={0} | all-to-all | bytes 458752 | tf_op jit(solution)/shard_map/all_to_all | solution.py:299
  102.5 13.6 %all_gather.34.refs_0_ = bf16[256,1792]{1,0:T(8,128)(2,1)S(1)} all-gather(bf16[64,1792]{1,0:T(8,128)(2,1)S(1)} %bitcast.161), channel_id=1, replica_groups=mesh['section'=8,'z'=8,'y'=4] {'y'}, dimensions={0}, use_global_device_ids=true | all-gather | bytes 1146880 | tf_op jit(solution)/shard_map/all_gather | solution.py:305
  118.1 16.9 %all_to_all.274 = bf16[4,32,3584]{2,1,0:T(8,128)(2,1)S(1)} all-to-all(bf16[4,32,3584]{2,1,0:T(8,128)(2,1)S(1)} %bitcast.121), channel_id=1, replica_groups=mesh['section'=8,'z'=8,'y'=4] {'y'}, dimensions={0} | all-to-all | bytes 1835008 | tf_op jit(solution)/shard_map/all_to_all | solution.py:321
  135.3 13.3 %all_to_all.275 = bf16[8,8,1792]{2,1,0:T(8,128)(2,1)S(1)} all-to-all(bf16[8,8,1792]{2,1,0:T(8,128)(2,1)S(1)} %bitcast.151), channel_id=1, replica_groups=mesh['section'=8,'z'=8,'y'=4] {'z'}, dimensions={0} | all-to-all | bytes 458752 | tf_op jit(solution)/shard_map/all_to_all | solution.py:330
  151.4 12.9 %all_to_all.276 = bf16[8,8,1792]{2,1,0:T(8,128)(2,1)S(1)} all-to-all(bf16[8,8,1792]{2,1,0:T(8,128)(2,1)S(1)} %bitcast.145), channel_id=1, replica_groups=mesh['section'=8,'z'=8,'y'=4] {'z'}, dimensions={0} | all-to-all | bytes 458752 | tf_op jit(solution)/shard_map/all_to_all | solution.py:299
  164.3 13.9 %all_gather.36.refs_0_ = bf16[256,1792]{1,0:T(8,128)(2,1)S(1)} all-gather(bf16[64,1792]{1,0:T(8,128)(2,1)S(1)} %bitcast.162), channel_id=1, replica_groups=mesh['section'=8,'z'=8,'y'=4] {'y'}, dimensions={0}, use_global_device_ids=true | all-gather | bytes 1146880 | tf_op jit(solution)/shard_map/all_gather | solution.py:305
  184.2 17.3 %all_to_all.277 = bf16[4,32,3584]{2,1,0:T(8,128)(2,1)S(1)} all-to-all(bf16[4,32,3584]{2,1,0:T(8,128)(2,1)S(1)} %bitcast.123), channel_id=1, replica_groups=mesh['section'=8,'z'=8,'y'=4] {'y'}, dimensions={0} | all-to-all | bytes 1835008 | tf_op jit(solution)/shard_map/all_to_all | solution.py:321
  201.8 13.2 %all_to_all.278 = bf16[8,8,1792]{2,1,0:T(8,128)(2,1)S(1)} all-to-all(bf16[8,8,1792]{2,1,0:T(8,128)(2,1)S(1)} %bitcast.152), channel_id=1, replica_groups=mesh['section'=8,'z'=8,'y'=4] {'z'}, dimensions={0} | all-to-all | bytes 458752 | tf_op jit(solution)/shard_map/all_to_all | solution.py:330
  217.8 15.0 %all_to_all.279 = bf16[8,8,1792]{2,1,0:T(8,128)(2,1)S(1)} all-to-all(bf16[8,8,1792]{2,1,0:T(8,128)(2,1)S(1)} %bitcast.146), channel_id=1, replica_groups=mesh['section'=8,'z'=8,'y'=4] {'z'}, dimensions={0} | all-to-all | bytes 458752 | tf_op jit(solution)/shard_map/all_to_all | solution.py:299
  232.8 13.8 %all_gather.37.refs_0_ = bf16[256,1792]{1,0:T(8,128)(2,1)S(1)} all-gather(bf16[64,1792]{1,0:T(8,128)(2,1)S(1)} %bitcast.163), channel_id=1, replica_groups=mesh['section'=8,'z'=8,'y'=4] {'y'}, dimensions={0}, use_global_device_ids=true | all-gather | bytes 1146880 | tf_op jit(solution)/shard_map/all_gather | solution.py:305
  248.6 14.4 %all_to_all.280 = bf16[4,32,3584]{2,1,0:T(8,128)(2,1)S(1)} all-to-all(bf16[4,32,3584]{2,1,0:T(8,128)(2,1)S(1)} %bitcast.124), channel_id=1, replica_groups=mesh['section'=8,'z'=8,'y'=4] {'y'}, dimensions={0} | all-to-all | bytes 1835008 | tf_op jit(solution)/shard_map/all_to_all | solution.py:321
  263.3 12.5 %all_to_all.281 = bf16[8,8,1792]{2,1,0:T(8,128)(2,1)S(1)} all-to-all(bf16[8,8,1792]{2,1,0:T(8,128)(2,1)S(1)} %bitcast.153), channel_id=1, replica_groups=mesh['section'=8,'z'=8,'y'=4] {'z'}, dimensions={0} | all-to-all | bytes 458752 | tf_op jit(solution)/shard_map/all_to_all | solution.py:330
  278.6 14.6 %all_to_all.282 = bf16[8,8,1792]{2,1,0:T(8,128)(2,1)S(1)} all-to-all(bf16[8,8,1792]{2,1,0:T(8,128)(2,1)S(1)} %bitcast.147), channel_id=1, replica_groups=mesh['section'=8,'z'=8,'y'=4] {'z'}, dimensions={0} | all-to-all | bytes 458752 | tf_op jit(solution)/shard_map/all_to_all | solution.py:299
  293.2 13.6 %all_gather.38.refs_0_ = bf16[256,1792]{1,0:T(8,128)(2,1)S(1)} all-gather(bf16[64,1792]{1,0:T(8,128)(2,1)S(1)} %bitcast.164), channel_id=1, replica_groups=mesh['section'=8,'z'=8,'y'=4] {'y'}, dimensions={0}, use_global_device_ids=true | all-gather | bytes 1146880 | tf_op jit(solution)/shard_map/all_gather | solution.py:305
  308.9 14.4 %all_to_all.283 = bf16[4,32,3584]{2,1,0:T(8,128)(2,1)S(1)} all-to-all(bf16[4,32,3584]{2,1,0:T(8,128)(2,1)S(1)} %bitcast.125), channel_id=1, replica_groups=mesh['section'=8,'z'=8,'y'=4] {'y'}, dimensions={0} | all-to-all | bytes 1835008 | tf_op jit(solution)/shard_map/all_to_all | solution.py:321
  323.5 12.5 %all_to_all.284 = bf16[8,8,1792]{2,1,0:T(8,128)(2,1)S(1)} all-to-all(bf16[8,8,1792]{2,1,0:T(8,128)(2,1)S(1)} %bitcast.154), channel_id=1, replica_groups=mesh['section'=8,'z'=8,'y'=4] {'z'}, dimensions={0} | all-to-all | bytes 458752 | tf_op jit(solution)/shard_map/all_to_all | solution.py:330
  338.9 14.6 %all_to_all.285 = bf16[8,8,1792]{2,1,0:T(8,128)(2,1)S(1)} all-to-all(bf16[8,8,1792]{2,1,0:T(8,128)(2,1)S(1)} %bitcast.148), channel_id=1, replica_groups=mesh['section'=8,'z'=8,'y'=4] {'z'}, dimensions={0} | all-to-all | bytes 458752 | tf_op jit(solution)/shard_map/all_to_all | solution.py:299
  353.5 13.6 %all_gather.39.refs_0_ = bf16[256,1792]{1,0:T(8,128)(2,1)S(1)} all-gather(bf16[64,1792]{1,0:T(8,128)(2,1)S(1)} %bitcast.165), channel_id=1, replica_groups=mesh['section'=8,'z'=8,'y'=4] {'y'}, dimensions={0}, use_global_device_ids=true | all-gather | bytes 1146880 | tf_op jit(solution)/shard_map/all_gather | solution.py:305
  369.1 14.4 %all_to_all.286 = bf16[4,32,3584]{2,1,0:T(8,128)(2,1)S(1)} all-to-all(bf16[4,32,3584]{2,1,0:T(8,128)(2,1)S(1)} %bitcast.126), channel_id=1, replica_groups=mesh['section'=8,'z'=8,'y'=4] {'y'}, dimensions={0} | all-to-all | bytes 1835008 | tf_op jit(solution)/shard_map/all_to_all | solution.py:321
  383.8 12.5 %all_to_all.287 = bf16[8,8,1792]{2,1,0:T(8,128)(2,1)S(1)} all-to-all(bf16[8,8,1792]{2,1,0:T(8,128)(2,1)S(1)} %bitcast.155), channel_id=1, replica_groups=mesh['section'=8,'z'=8,'y'=4] {'z'}, dimensions={0} | all-to-all | bytes 458752 | tf_op jit(solution)/shard_map/all_to_all | solution.py:330
  399.1 14.7 %all_to_all.288 = bf16[8,8,1792]{2,1,0:T(8,128)(2,1)S(1)} all-to-all(bf16[8,8,1792]{2,1,0:T(8,128)(2,1)S(1)} %bitcast.149), channel_id=1, replica_groups=mesh['section'=8,'z'=8,'y'=4] {'z'}, dimensions={0} | all-to-all | bytes 458752 | tf_op jit(solution)/shard_map/all_to_all | solution.py:299
  413.8 13.6 %all_gather.40.refs_0_ = bf16[256,1792]{1,0:T(8,128)(2,1)S(1)} all-gather(bf16[64,1792]{1,0:T(8,128)(2,1)S(1)} %bitcast.166), channel_id=1, replica_groups=mesh['section'=8,'z'=8,'y'=4] {'y'}, dimensions={0}, use_global_device_ids=true | all-gather | bytes 1146880 | tf_op jit(solution)/shard_map/all_gather | solution.py:305
  433.9 15.2 %all_to_all.289 = bf16[4,32,3584]{2,1,0:T(8,128)(2,1)S(1)} all-to-all(bf16[4,32,3584]{2,1,0:T(8,128)(2,1)S(1)} %bitcast.120), channel_id=1, replica_groups=mesh['section'=8,'z'=8,'y'=4] {'y'}, dimensions={0} | all-to-all | bytes 1835008 | tf_op jit(solution)/shard_map/all_to_all | solution.py:321
  449.4 12.7 %all_to_all.290 = bf16[8,8,1792]{2,1,0:T(8,128)(2,1)S(1)} all-to-all(bf16[8,8,1792]{2,1,0:T(8,128)(2,1)S(1)} %bitcast.156), channel_id=1, replica_groups=mesh['section'=8,'z'=8,'y'=4] {'z'}, dimensions={0} | all-to-all | bytes 458752 | tf_op jit(solution)/shard_map/all_to_all | solution.py:330
  468.3 14.7 %all_to_all.291 = bf16[8,8,1792]{2,1,0:T(8,128)(2,1)S(1)} all-to-all(bf16[8,8,1792]{2,1,0:T(8,128)(2,1)S(1)} %bitcast.143), channel_id=1, replica_groups=mesh['section'=8,'z'=8,'y'=4] {'z'}, dimensions={0} | all-to-all | bytes 458752 | tf_op jit(solution)/shard_map/all_to_all | solution.py:299
  483.0 17.2 %all_gather.41.refs_0_.rest_0_ = bf16[288,1792]{1,0:T(8,128)(2,1)S(1)} all-gather(bf16[72,1792]{1,0:T(8,128)(2,1)S(1)} %pad_maximum_fusion), channel_id=1, replica_groups=mesh['section'=8,'z'=8,'y'=4] {'y'}, dimensions={0}, use_global_device_ids=true | all-gather | bytes 1290240 | tf_op jit(solution)/shard_map/all_gather | solution.py:305
  502.4 16.4 %all_to_all.292 = bf16[4,32,3584]{2,1,0:T(8,128)(2,1)S(1)} all-to-all(bf16[4,32,3584]{2,1,0:T(8,128)(2,1)S(1)} %bitcast.127), channel_id=1, replica_groups=mesh['section'=8,'z'=8,'y'=4] {'y'}, dimensions={0} | all-to-all | bytes 1835008 | tf_op jit(solution)/shard_map/all_to_all | solution.py:321
  527.2 11.7 %all-to-all-done.23 = bf16[8,16,1792]{2,1,0:T(8,128)(2,1)S(1)} async-done(((bf16[8,16,1792]{2,1,0:T(8,128)(2,1)}), bf16[8,16,1792]{2,1,0:T(8,128)(2,1)S(1)}, u32[]{:S(2)}, u32[]{:S(2)}) %all-to-all-start.23) | async-done | bytes 458784 | tf_op jit(solution)/shard_map/all_to_all | solution.py:330
  (161 shorter events, 81.4 us)
Async XLA Ops:
  7.2 0.8 copy-start
  7.2 110.9 %all-gather.5.cloned.1.call-start = ((), (), s32[]{:S(2)}) async-start(), calls=%async_computation.24 | async-start | bytes 4730880 | tf_op jit(solution)/shard_map/all_gather | solution.py:222
  9.9 0.7 copy-start.15
  11.8 19.7 %all-to-all-start = ((bf16[8,8,1792]{2,1,0:T(8,128)(2,1)}), bf16[8,8,1792]{2,1,0:T(8,128)(2,1)S(1)}, u32[]{:S(2)}, u32[]{:S(2)}) async-start(bf16[8,8,1792]{2,1,0:T(8,128)(2,1)} %bitcast.10), calls=%async_computation | async-start | bytes 458752 | tf_op jit(solution)/shard_map/all_to_all | solution.py:299
  20.3 498.5 %all-gather.7.cloned.1.call-start = ((), (), s32[]{:S(2)}) async-start(), calls=%async_computation.25 | async-start | bytes 2365440 | tf_op jit(solution)/shard_map/all_gather | solution.py:320
  46.0 2.1 copy-start.1
  48.0 2.0 copy-start.5
  50.0 2.0 copy-start.9
  52.1 64.0 %copy-start.6 = (bf16[1,3584,512]{2,1,0:T(8,128)(2,1)S(1)}, bf16[1,3584,512]{2,1,0:T(8,128)(2,1)}, u32[]{:S(2)}) copy-start(bf16[1,3584,512]{2,1,0:T(8,128)(2,1)} %param.22) | copy-start | bytes 11010052
  52.1 64.0 %copy-start.10 = (bf16[1,512,3584]{2,1,0:T(8,128)(2,1)S(1)}, bf16[1,512,3584]{2,1,0:T(8,128)(2,1)}, u32[]{:S(2)}) copy-start(bf16[1,512,3584]{2,1,0:T(8,128)(2,1)} %param.23) | copy-start | bytes 11010052
  54.1 34.7 %copy-start.19 = (bf16[8,8,3584]{2,1,0:T(8,128)(2,1)S(1)}, bf16[8,8,3584]{2,1,0:T(8,128)(2,1)}, u32[]{:S(2)}) copy-start(bf16[8,8,3584]{2,1,0:T(8,128)(2,1)} %param.16) | copy-start | bytes 1376260
  54.1 34.7 %copy-start.16 = (f32[1,3584]{1,0:T(1,128)S(1)}, f32[1,3584]{1,0:T(1,128)}, u32[]{:S(2)}) copy-start(f32[1,3584]{1,0:T(1,128)} %gain.15) | copy-start | bytes 43012
  70.8 45.2 %copy-start.2 = (bf16[1,3584,512]{2,1,0:T(8,128)(2,1)S(1)}, bf16[1,3584,512]{2,1,0:T(8,128)(2,1)}, u32[]{:S(2)}) copy-start(bf16[1,3584,512]{2,1,0:T(8,128)(2,1)} %param.21) | copy-start | bytes 11010052
  86.6 2.2 collective-permute-start
  135.0 43.2 %copy-start.3 = (bf16[1,3584,512]{2,1,0:T(8,128)(2,1)S(1)}, bf16[1,3584,512]{2,1,0:T(8,128)(2,1)}, u32[]{:S(2)}) copy-start(bf16[1,3584,512]{2,1,0:T(8,128)(2,1)} %param.21) | copy-start | bytes 11010052
  148.8 2.2 collective-permute-start.1
  178.2 2.0 copy-start.7
  180.2 2.0 copy-start.11
  215.2 2.2 collective-permute-start.2
  276.1 2.2 collective-permute-start.3
  336.3 2.2 collective-permute-start.4
  396.5 2.2 collective-permute-start.5
  427.4 2.3 copy-start.17
  427.4 2.3 copy-start.18
  429.7 2.3 copy-start.13
  433.9 66.3 %copy-start.12 = (bf16[1,512,3584]{2,1,0:T(8,128)(2,1)S(1)}, bf16[1,512,3584]{2,1,0:T(8,128)(2,1)}, u32[]{:S(2)}) copy-start(bf16[1,512,3584]{2,1,0:T(8,128)(2,1)} %param.23) | copy-start | bytes 11010052
  462.3 2.2 collective-permute-start.6
  464.5 35.7 %copy-start.8 = (bf16[1,3584,512]{2,1,0:T(8,128)(2,1)S(1)}, bf16[1,3584,512]{2,1,0:T(8,128)(2,1)}, u32[]{:S(2)}) copy-start(bf16[1,3584,512]{2,1,0:T(8,128)(2,1)} %param.22) | copy-start | bytes 11010052
  464.5 2.4 copy-start.14
  466.9 33.2 %copy-start.4 = (bf16[1,3584,512]{2,1,0:T(8,128)(2,1)S(1)}, bf16[1,3584,512]{2,1,0:T(8,128)(2,1)}, u32[]{:S(2)}) copy-start(bf16[1,3584,512]{2,1,0:T(8,128)(2,1)} %param.21) | copy-start | bytes 11010052
  520.4 18.5 %all-to-all-start.23 = ((bf16[8,16,1792]{2,1,0:T(8,128)(2,1)}), bf16[8,16,1792]{2,1,0:T(8,128)(2,1)S(1)}, u32[]{:S(2)}, u32[]{:S(2)}) async-start(bf16[8,16,1792]{2,1,0:T(8,128)(2,1)} %bitcast.66), calls=%async_computation.23 | async-start | bytes 917504 | tf_op jit(solution)/shard_map/all_to_all | solution.py:330
Sparse Core Ops, SparseCore 0:
  10.6 87.3 all-gather.4
  434.0 72.9 all-gather.6

commit v8 on v7

--- a/solution.py
+++ b/solution.py
@@ -31,9 +31,10 @@
 
 def rotation(width, positions):
     half_dim = width // 2
-    frequency = 10000.0 ** (-jnp.arange(half_dim, dtype=jnp.float32) / half_dim)
+    step = jnp.arange(width, dtype=jnp.float32) % half_dim
+    frequency = 10000.0 ** (-step / half_dim)
     angles = positions.astype(jnp.float32)[:, None] * frequency[None, :]
-    return jnp.tile(jnp.cos(angles), (1, 2)), jnp.tile(jnp.sin(angles), (1, 2))
+    return jnp.cos(angles), jnp.sin(angles)
 
 
 def one_hot(rows, cols, wanted, kept=None):

time: 549 us -> 547 us (level)
    unnamed x47 -> x49, local copies, waits for them, and re-layouts: 15.8 us -> 13.5 us
where the time goes in v8:
time: 547 us; the launch traced here: 545 us
  blocking collectives  431 us (79%)
  Pallas kernels  29 us (5%)
  waiting for transfers between devices  25.1 us (5%)
  starting transfers between devices  22.4 us (4%)
  local copies, waits for them, and re-layouts  19.6 us (4%)
  between operations  14.7 us (3%)
    all_to_all x8, blocking collectives, body(): lax.all_to_all(parts, 'y', split_axis=0, concat_axis=0, tiled=True)  126 us
    all_gather x8, blocking collectives, body(): token_rows = lax.all_gather(arrived, 'y', axis=0, tiled=True)  115 us
    all_to_all x7, blocking collectives, body(): lax.all_to_all(chosen, 'z', split_axis=0, concat_axis=0, tiled=True)  98.3 us
    all_to_all x7, blocking collectives, body(): lax.all_to_all(summed, 'z', split_axis=0, concat_axis=0, tiled=True)  91.8 us
    pallas_call x35, Pallas kernels, in_vmem(): pl.pallas_call(kernel, grid=(1,), out_shape=out_shape, in_specs=specs, ou...  29 us
    unnamed x49, local copies, waits for them, and re-layouts  13.5 us
    all_to_all x1, waiting for transfers between devices, body(): lax.all_to_all(summed, 'z', split_axis=0, concat_axis=0, tiled=True)  11.7 us
  transfers between devices with their start and end apart: 11, of which 9 were waited for; matrix products, arithmetic and copies ran while one was open for 2% of the time, Pallas kernels for 2%

profile of v8, /device:TPU:8, one launch (start us, length us, event | category | flops | bytes accessed | tf_op | source)
XLA Modules:
  0.0 545.3 jit_solution(6229162197793083660)
XLA Ops:
  11.8 8.5 %all-to-all-start = ((bf16[8,8,1792]{2,1,0:T(8,128)(2,1)}), bf16[8,8,1792]{2,1,0:T(8,128)(2,1)S(1)}, u32[]{:S(2)}, u32[]{:S(2)}) async-start(bf16[8,8,1792]{2,1,0:T(8,128)(2,1)} %bitcast.10), calls=%async_computation | async-start | bytes 458752 | tf_op jit(solution)/shard_map/all_to_all | solution.py:300
  31.5 14.4 %all_gather.33.refs_0_ = bf16[256,1792]{1,0:T(8,128)(2,1)S(1)} all-gather(bf16[64,1792]{1,0:T(8,128)(2,1)S(1)} %bitcast.160), channel_id=1, replica_groups=mesh['section'=8,'z'=8,'y'=4] {'y'}, dimensions={0}, use_global_device_ids=true | all-gather | bytes 1146880 | tf_op jit(solution)/shard_map/all_gather | solution.py:306
  54.1 16.4 %all_to_all.271 = bf16[4,32,3584]{2,1,0:T(8,128)(2,1)S(1)} all-to-all(bf16[4,32,3584]{2,1,0:T(8,128)(2,1)S(1)} %bitcast.122), channel_id=1, replica_groups=mesh['section'=8,'z'=8,'y'=4] {'y'}, dimensions={0} | all-to-all | bytes 1835008 | tf_op jit(solution)/shard_map/all_to_all | solution.py:322
  70.8 15.1 %all_to_all.272 = bf16[8,8,1792]{2,1,0:T(8,128)(2,1)S(1)} all-to-all(bf16[8,8,1792]{2,1,0:T(8,128)(2,1)S(1)} %bitcast.150), channel_id=1, replica_groups=mesh['section'=8,'z'=8,'y'=4] {'z'}, dimensions={0} | all-to-all | bytes 458752 | tf_op jit(solution)/shard_map/all_to_all | solution.py:331
  88.6 12.7 %all_to_all.273 = bf16[8,8,1792]{2,1,0:T(8,128)(2,1)S(1)} all-to-all(bf16[8,8,1792]{2,1,0:T(8,128)(2,1)S(1)} %bitcast.144), channel_id=1, replica_groups=mesh['section'=8,'z'=8,'y'=4] {'z'}, dimensions={0} | all-to-all | bytes 458752 | tf_op jit(solution)/shard_map/all_to_all | solution.py:300
  101.3 14.1 %all_gather.34.refs_0_ = bf16[256,1792]{1,0:T(8,128)(2,1)S(1)} all-gather(bf16[64,1792]{1,0:T(8,128)(2,1)S(1)} %bitcast.161), channel_id=1, replica_groups=mesh['section'=8,'z'=8,'y'=4] {'y'}, dimensions={0}, use_global_device_ids=true | all-gather | bytes 1146880 | tf_op jit(solution)/shard_map/all_gather | solution.py:306
  117.4 16.9 %all_to_all.274 = bf16[4,32,3584]{2,1,0:T(8,128)(2,1)S(1)} all-to-all(bf16[4,32,3584]{2,1,0:T(8,128)(2,1)S(1)} %bitcast.121), channel_id=1, replica_groups=mesh['section'=8,'z'=8,'y'=4] {'y'}, dimensions={0} | all-to-all | bytes 1835008 | tf_op jit(solution)/shard_map/all_to_all | solution.py:322
  134.6 13.5 %all_to_all.275 = bf16[8,8,1792]{2,1,0:T(8,128)(2,1)S(1)} all-to-all(bf16[8,8,1792]{2,1,0:T(8,128)(2,1)S(1)} %bitcast.151), channel_id=1, replica_groups=mesh['section'=8,'z'=8,'y'=4] {'z'}, dimensions={0} | all-to-all | bytes 458752 | tf_op jit(solution)/shard_map/all_to_all | solution.py:331
  150.9 13.4 %all_to_all.276 = bf16[8,8,1792]{2,1,0:T(8,128)(2,1)S(1)} all-to-all(bf16[8,8,1792]{2,1,0:T(8,128)(2,1)S(1)} %bitcast.145), channel_id=1, replica_groups=mesh['section'=8,'z'=8,'y'=4] {'z'}, dimensions={0} | all-to-all | bytes 458752 | tf_op jit(solution)/shard_map/all_to_all | solution.py:300
  164.4 14.1 %all_gather.36.refs_0_ = bf16[256,1792]{1,0:T(8,128)(2,1)S(1)} all-gather(bf16[64,1792]{1,0:T(8,128)(2,1)S(1)} %bitcast.162), channel_id=1, replica_groups=mesh['section'=8,'z'=8,'y'=4] {'y'}, dimensions={0}, use_global_device_ids=true | all-gather | bytes 1146880 | tf_op jit(solution)/shard_map/all_gather | solution.py:306
  184.6 16.9 %all_to_all.277 = bf16[4,32,3584]{2,1,0:T(8,128)(2,1)S(1)} all-to-all(bf16[4,32,3584]{2,1,0:T(8,128)(2,1)S(1)} %bitcast.123), channel_id=1, replica_groups=mesh['section'=8,'z'=8,'y'=4] {'y'}, dimensions={0} | all-to-all | bytes 1835008 | tf_op jit(solution)/shard_map/all_to_all | solution.py:322
  201.8 12.8 %all_to_all.278 = bf16[8,8,1792]{2,1,0:T(8,128)(2,1)S(1)} all-to-all(bf16[8,8,1792]{2,1,0:T(8,128)(2,1)S(1)} %bitcast.152), channel_id=1, replica_groups=mesh['section'=8,'z'=8,'y'=4] {'z'}, dimensions={0} | all-to-all | bytes 458752 | tf_op jit(solution)/shard_map/all_to_all | solution.py:331
  217.3 14.0 %all_to_all.279 = bf16[8,8,1792]{2,1,0:T(8,128)(2,1)S(1)} all-to-all(bf16[8,8,1792]{2,1,0:T(8,128)(2,1)S(1)} %bitcast.146), channel_id=1, replica_groups=mesh['section'=8,'z'=8,'y'=4] {'z'}, dimensions={0} | all-to-all | bytes 458752 | tf_op jit(solution)/shard_map/all_to_all | solution.py:300
  231.3 14.2 %all_gather.37.refs_0_ = bf16[256,1792]{1,0:T(8,128)(2,1)S(1)} all-gather(bf16[64,1792]{1,0:T(8,128)(2,1)S(1)} %bitcast.163), channel_id=1, replica_groups=mesh['section'=8,'z'=8,'y'=4] {'y'}, dimensions={0}, use_global_device_ids=true | all-gather | bytes 1146880 | tf_op jit(solution)/shard_map/all_gather | solution.py:306
  247.5 16.2 %all_to_all.280 = bf16[4,32,3584]{2,1,0:T(8,128)(2,1)S(1)} all-to-all(bf16[4,32,3584]{2,1,0:T(8,128)(2,1)S(1)} %bitcast.124), channel_id=1, replica_groups=mesh['section'=8,'z'=8,'y'=4] {'y'}, dimensions={0} | all-to-all | bytes 1835008 | tf_op jit(solution)/shard_map/all_to_all | solution.py:322
  264.0 12.5 %all_to_all.281 = bf16[8,8,1792]{2,1,0:T(8,128)(2,1)S(1)} all-to-all(bf16[8,8,1792]{2,1,0:T(8,128)(2,1)S(1)} %bitcast.153), channel_id=1, replica_groups=mesh['section'=8,'z'=8,'y'=4] {'z'}, dimensions={0} | all-to-all | bytes 458752 | tf_op jit(solution)/shard_map/all_to_all | solution.py:331
  279.3 14.4 %all_to_all.282 = bf16[8,8,1792]{2,1,0:T(8,128)(2,1)S(1)} all-to-all(bf16[8,8,1792]{2,1,0:T(8,128)(2,1)S(1)} %bitcast.147), channel_id=1, replica_groups=mesh['section'=8,'z'=8,'y'=4] {'z'}, dimensions={0} | all-to-all | bytes 458752 | tf_op jit(solution)/shard_map/all_to_all | solution.py:300
  293.7 13.6 %all_gather.38.refs_0_ = bf16[256,1792]{1,0:T(8,128)(2,1)S(1)} all-gather(bf16[64,1792]{1,0:T(8,128)(2,1)S(1)} %bitcast.164), channel_id=1, replica_groups=mesh['section'=8,'z'=8,'y'=4] {'y'}, dimensions={0}, use_global_device_ids=true | all-gather | bytes 1146880 | tf_op jit(solution)/shard_map/all_gather | solution.py:306
  309.2 14.4 %all_to_all.283 = bf16[4,32,3584]{2,1,0:T(8,128)(2,1)S(1)} all-to-all(bf16[4,32,3584]{2,1,0:T(8,128)(2,1)S(1)} %bitcast.125), channel_id=1, replica_groups=mesh['section'=8,'z'=8,'y'=4] {'y'}, dimensions={0} | all-to-all | bytes 1835008 | tf_op jit(solution)/shard_map/all_to_all | solution.py:322
  323.9 12.5 %all_to_all.284 = bf16[8,8,1792]{2,1,0:T(8,128)(2,1)S(1)} all-to-all(bf16[8,8,1792]{2,1,0:T(8,128)(2,1)S(1)} %bitcast.154), channel_id=1, replica_groups=mesh['section'=8,'z'=8,'y'=4] {'z'}, dimensions={0} | all-to-all | bytes 458752 | tf_op jit(solution)/shard_map/all_to_all | solution.py:331
  339.3 14.4 %all_to_all.285 = bf16[8,8,1792]{2,1,0:T(8,128)(2,1)S(1)} all-to-all(bf16[8,8,1792]{2,1,0:T(8,128)(2,1)S(1)} %bitcast.148), channel_id=1, replica_groups=mesh['section'=8,'z'=8,'y'=4] {'z'}, dimensions={0} | all-to-all | bytes 458752 | tf_op jit(solution)/shard_map/all_to_all | solution.py:300
  353.7 13.6 %all_gather.39.refs_0_ = bf16[256,1792]{1,0:T(8,128)(2,1)S(1)} all-gather(bf16[64,1792]{1,0:T(8,128)(2,1)S(1)} %bitcast.165), channel_id=1, replica_groups=mesh['section'=8,'z'=8,'y'=4] {'y'}, dimensions={0}, use_global_device_ids=true | all-gather | bytes 1146880 | tf_op jit(solution)/shard_map/all_gather | solution.py:306
  369.2 14.4 %all_to_all.286 = bf16[4,32,3584]{2,1,0:T(8,128)(2,1)S(1)} all-to-all(bf16[4,32,3584]{2,1,0:T(8,128)(2,1)S(1)} %bitcast.126), channel_id=1, replica_groups=mesh['section'=8,'z'=8,'y'=4] {'y'}, dimensions={0} | all-to-all | bytes 1835008 | tf_op jit(solution)/shard_map/all_to_all | solution.py:322
  383.9 12.5 %all_to_all.287 = bf16[8,8,1792]{2,1,0:T(8,128)(2,1)S(1)} all-to-all(bf16[8,8,1792]{2,1,0:T(8,128)(2,1)S(1)} %bitcast.155), channel_id=1, replica_groups=mesh['section'=8,'z'=8,'y'=4] {'z'}, dimensions={0} | all-to-all | bytes 458752 | tf_op jit(solution)/shard_map/all_to_all | solution.py:331
  399.3 14.5 %all_to_all.288 = bf16[8,8,1792]{2,1,0:T(8,128)(2,1)S(1)} all-to-all(bf16[8,8,1792]{2,1,0:T(8,128)(2,1)S(1)} %bitcast.149), channel_id=1, replica_groups=mesh['section'=8,'z'=8,'y'=4] {'z'}, dimensions={0} | all-to-all | bytes 458752 | tf_op jit(solution)/shard_map/all_to_all | solution.py:300
  413.8 13.8 %all_gather.40.refs_0_ = bf16[256,1792]{1,0:T(8,128)(2,1)S(1)} all-gather(bf16[64,1792]{1,0:T(8,128)(2,1)S(1)} %bitcast.166), channel_id=1, replica_groups=mesh['section'=8,'z'=8,'y'=4] {'y'}, dimensions={0}, use_global_device_ids=true | all-gather | bytes 1146880 | tf_op jit(solution)/shard_map/all_gather | solution.py:306
  431.6 15.2 %all_to_all.289 = bf16[4,32,3584]{2,1,0:T(8,128)(2,1)S(1)} all-to-all(bf16[4,32,3584]{2,1,0:T(8,128)(2,1)S(1)} %bitcast.120), channel_id=1, replica_groups=mesh['section'=8,'z'=8,'y'=4] {'y'}, dimensions={0} | all-to-all | bytes 1835008 | tf_op jit(solution)/shard_map/all_to_all | solution.py:322
  447.0 12.9 %all_to_all.290 = bf16[8,8,1792]{2,1,0:T(8,128)(2,1)S(1)} all-to-all(bf16[8,8,1792]{2,1,0:T(8,128)(2,1)S(1)} %bitcast.156), channel_id=1, replica_groups=mesh['section'=8,'z'=8,'y'=4] {'z'}, dimensions={0} | all-to-all | bytes 458752 | tf_op jit(solution)/shard_map/all_to_all | solution.py:331
  466.1 14.9 %all_to_all.291 = bf16[8,8,1792]{2,1,0:T(8,128)(2,1)S(1)} all-to-all(bf16[8,8,1792]{2,1,0:T(8,128)(2,1)S(1)} %bitcast.143), channel_id=1, replica_groups=mesh['section'=8,'z'=8,'y'=4] {'z'}, dimensions={0} | all-to-all | bytes 458752 | tf_op jit(solution)/shard_map/all_to_all | solution.py:300
  481.1 16.8 %all_gather.41.refs_0_.rest_0_ = bf16[288,1792]{1,0:T(8,128)(2,1)S(1)} all-gather(bf16[72,1792]{1,0:T(8,128)(2,1)S(1)} %pad_maximum_fusion), channel_id=1, replica_groups=mesh['section'=8,'z'=8,'y'=4] {'y'}, dimensions={0}, use_global_device_ids=true | all-gather | bytes 1290240 | tf_op jit(solution)/shard_map/all_gather | solution.py:306
  500.1 16.0 %all_to_all.292 = bf16[4,32,3584]{2,1,0:T(8,128)(2,1)S(1)} all-to-all(bf16[4,32,3584]{2,1,0:T(8,128)(2,1)S(1)} %bitcast.127), channel_id=1, replica_groups=mesh['section'=8,'z'=8,'y'=4] {'y'}, dimensions={0} | all-to-all | bytes 1835008 | tf_op jit(solution)/shard_map/all_to_all | solution.py:322
  525.1 11.7 %all-to-all-done.23 = bf16[8,16,1792]{2,1,0:T(8,128)(2,1)S(1)} async-done(((bf16[8,16,1792]{2,1,0:T(8,128)(2,1)}), bf16[8,16,1792]{2,1,0:T(8,128)(2,1)S(1)}, u32[]{:S(2)}, u32[]{:S(2)}) %all-to-all-start.23) | async-done | bytes 458784 | tf_op jit(solution)/shard_map/all_to_all | solution.py:331
  (160 shorter events, 79.4 us)
Async XLA Ops:
  7.2 0.8 copy-start
  7.2 110.2 %all-gather.5.cloned.1.call-start = ((), (), s32[]{:S(2)}) async-start(), calls=%async_computation.24 | async-start | bytes 4730880 | tf_op jit(solution)/shard_map/all_gather | solution.py:223
  9.9 0.7 copy-start.14
  11.8 19.7 %all-to-all-start = ((bf16[8,8,1792]{2,1,0:T(8,128)(2,1)}), bf16[8,8,1792]{2,1,0:T(8,128)(2,1)S(1)}, u32[]{:S(2)}, u32[]{:S(2)}) async-start(bf16[8,8,1792]{2,1,0:T(8,128)(2,1)} %bitcast.10), calls=%async_computation | async-start | bytes 458752 | tf_op jit(solution)/shard_map/all_to_all | solution.py:300
  20.3 495.8 %all-gather.7.cloned.1.call-start = ((), (), s32[]{:S(2)}) async-start(), calls=%async_computation.25 | async-start | bytes 2365440 | tf_op jit(solution)/shard_map/all_gather | solution.py:321
  45.9 2.1 copy-start.1
  48.0 2.0 copy-start.5
  50.0 2.0 copy-start.9
  52.1 63.3 %copy-start.6 = (bf16[1,3584,512]{2,1,0:T(8,128)(2,1)S(1)}, bf16[1,3584,512]{2,1,0:T(8,128)(2,1)}, u32[]{:S(2)}) copy-start(bf16[1,3584,512]{2,1,0:T(8,128)(2,1)} %param.22) | copy-start | bytes 11010052
  52.1 63.3 %copy-start.10 = (bf16[1,512,3584]{2,1,0:T(8,128)(2,1)S(1)}, bf16[1,512,3584]{2,1,0:T(8,128)(2,1)}, u32[]{:S(2)}) copy-start(bf16[1,512,3584]{2,1,0:T(8,128)(2,1)} %param.23) | copy-start | bytes 11010052
  54.0 34.2 %copy-start.18 = (bf16[8,8,3584]{2,1,0:T(8,128)(2,1)S(1)}, bf16[8,8,3584]{2,1,0:T(8,128)(2,1)}, u32[]{:S(2)}) copy-start(bf16[8,8,3584]{2,1,0:T(8,128)(2,1)} %param.16) | copy-start | bytes 1376260
  54.1 34.2 %copy-start.15 = (f32[1,3584]{1,0:T(1,128)S(1)}, f32[1,3584]{1,0:T(1,128)}, u32[]{:S(2)}) copy-start(f32[1,3584]{1,0:T(1,128)} %gain.15) | copy-start | bytes 43012
  70.5 44.9 %copy-start.2 = (bf16[1,3584,512]{2,1,0:T(8,128)(2,1)S(1)}, bf16[1,3584,512]{2,1,0:T(8,128)(2,1)}, u32[]{:S(2)}) copy-start(bf16[1,3584,512]{2,1,0:T(8,128)(2,1)} %param.21) | copy-start | bytes 11010052
  86.0 2.2 collective-permute-start
  134.3 44.2 %copy-start.3 = (bf16[1,3584,512]{2,1,0:T(8,128)(2,1)S(1)}, bf16[1,3584,512]{2,1,0:T(8,128)(2,1)}, u32[]{:S(2)}) copy-start(bf16[1,3584,512]{2,1,0:T(8,128)(2,1)} %param.21) | copy-start | bytes 11010052
  148.4 2.2 collective-permute-start.1
  178.5 2.0 copy-start.7
  180.6 2.0 copy-start.11
  214.8 2.2 collective-permute-start.2
  276.7 2.2 collective-permute-start.3
  336.7 2.2 collective-permute-start.4
  396.7 2.2 collective-permute-start.5
  413.8 15.9 %slice-start = ((s8[4587520]{0:T(1024)(128)(4,1)}), s8[4194304]{0:T(1024)(128)(4,1)S(1)}, s32[]{:S(2)}) async-start(s8[4587520]{0:T(1024)(128)(4,1)} %bitcast.116), calls=%async_computation.26 | async-start | bytes 8388608
  427.5 2.1 slice-start.1
  427.5 2.1 copy-start.16
  427.5 2.1 copy-start.17
  431.6 66.3 %copy-start.12 = (bf16[1,512,3584]{2,1,0:T(8,128)(2,1)S(1)}, bf16[1,512,3584]{2,1,0:T(8,128)(2,1)}, u32[]{:S(2)}) copy-start(bf16[1,512,3584]{2,1,0:T(8,128)(2,1)} %param.23) | copy-start | bytes 11010052
  460.1 2.2 collective-permute-start.6
  462.3 35.6 %copy-start.8 = (bf16[1,3584,512]{2,1,0:T(8,128)(2,1)S(1)}, bf16[1,3584,512]{2,1,0:T(8,128)(2,1)}, u32[]{:S(2)}) copy-start(bf16[1,3584,512]{2,1,0:T(8,128)(2,1)} %param.22) | copy-start | bytes 11010052
  462.3 2.5 copy-start.13
  464.8 33.1 %copy-start.4 = (bf16[1,3584,512]{2,1,0:T(8,128)(2,1)S(1)}, bf16[1,3584,512]{2,1,0:T(8,128)(2,1)}, u32[]{:S(2)}) copy-start(bf16[1,3584,512]{2,1,0:T(8,128)(2,1)} %param.21) | copy-start | bytes 11010052
  517.7 19.1 %all-to-all-start.23 = ((bf16[8,16,1792]{2,1,0:T(8,128)(2,1)}), bf16[8,16,1792]{2,1,0:T(8,128)(2,1)S(1)}, u32[]{:S(2)}, u32[]{:S(2)}) async-start(bf16[8,16,1792]{2,1,0:T(8,128)(2,1)} %bitcast.64), calls=%async_computation.23 | async-start | bytes 917504 | tf_op jit(solution)/shard_map/all_to_all | solution.py:331
Sparse Core Ops, SparseCore 0:
  10.6 89.7 all-gather.4
  431.7 72.7 all-gather.6

commit v9 on v8

--- a/solution.py
+++ b/solution.py
@@ -76,7 +76,8 @@
     for k in range(TOPK):
         same = routes[:, k : k + 1] == expert
         picked = jnp.where(same, 1.0, picked)
-        weight = jnp.where(same, routes[:, TOPK + k : TOPK + k + 1], weight)
+        last = routes.shape[1] - TOPK + k
+        weight = jnp.where(same, routes[:, last : last + 1], weight)
     row = lax.broadcasted_iota(jnp.int32, (rows, rows), 0)
     col = lax.broadcasted_iota(jnp.int32, (rows, rows), 1)
     earlier = jnp.where(col < row, 1.0, 0.0)
@@ -94,9 +95,17 @@
             weights_out[tick, :, cols] = weights
 
 
-def choose_kernel(made, tokens, gain, table, out):
+def first_choose_kernel(gain, tokens, ids, out):
+    choose_rows(tokens[0], gain, ids, out, False)
+
+
+def choose_kernel(tokens, gain, table, out):
+    choose_rows(tokens[...], gain, table, out, True)
+
+
+def choose_rows(tokens, gain, table, out, made):
     folded, half = out.shape
-    normed = rms_scale(tokens[...], gain[...]).astype(jnp.bfloat16).astype(jnp.float32)
+    normed = rms_scale(tokens, gain[...]).astype(jnp.bfloat16).astype(jnp.float32)
     picked = 0.0
     for k, offset in enumerate((0, 4)):
         if made:
@@ -165,11 +174,13 @@
         gathered, pick = rest[0], rest[1]
         stride = gathered.shape[0] // columns
         source = lambda row: (row // 8) * stride + stride - 8 + row % 8
-        kv_rows = matmul(one_hot(8 * columns, gathered.shape[0], source), gathered[...])
+        width = 640
+        kv_rows = matmul(one_hot(8 * columns, gathered.shape[0], source), gathered[:, :width])
         picked = matmul(pick[...], kv_rows.astype(jnp.bfloat16)).astype(jnp.bfloat16)
         place = lambda row: (row // group) * 8 + row % 8
         third = one_hot(height, picked.shape[0], place, lambda row: row % group >= 8)
-        spread = spread + matmul(third, picked)
+        kv_part = spread[:, :width] + matmul(third, picked)
+        spread = jnp.concatenate([kv_part, spread[:, width:]], axis=1)
     out[...] = spread.astype(jnp.bfloat16)
 
 
@@ -227,7 +238,7 @@
         return lax.dynamic_slice_in_dim(padded, n_spans - section_id, n_sections, 0)
 
     own_ids = by_tick(lax.dynamic_slice_in_dim(expert_ids[0], member * span_dev, span_dev, 1))
-    routes = jnp.concatenate([own_ids.astype(jnp.float32), by_tick(gate_vals[0])], axis=2)
+    own_ids = own_ids.astype(jnp.float32)
 
     def project(first, last, gains, weights, turns):
         rows = jnp.concatenate(tick_rows[first:last], axis=0)
@@ -248,14 +259,16 @@
             block_order[:count], member * per_owner, per_owner, 1
         )
         every = np.arange(n_members * span_dev, dtype=np.int32)
-        pick = (owned_rows(order)[..., None] == every).astype(jnp.bfloat16)
-        return pick.reshape(count, span_dev, n_members, span_dev)
+        pick = (owned_rows(order)[..., None] == every).reshape(
+            count * span_dev, n_members, 1, span_dev
+        )
+        tick = np.arange(count, dtype=np.int32)
+        same = np.repeat(tick, span_dev)[:, None, None, None] == tick[None, None, :, None]
+        return (pick & same).astype(jnp.bfloat16).reshape(count * span_dev, -1)
 
     def deliver_early(gathered, pick):
-        gathered = gathered.reshape(n_members, pick.shape[0], span_dev, kv_width)
-        return jnp.einsum(
-            "tdmr,mtrk->tdk", pick, gathered, preferred_element_type=jnp.float32
-        ).astype(jnp.bfloat16)
+        picked = matmul(pick, gathered.reshape(-1, kv_width)).astype(jnp.bfloat16)
+        return picked.reshape(-1, span_dev, kv_width)
 
     def late_picks(block_order):
         order = block_order[-1].reshape(n_planes, n_columns, per_owner)
@@ -278,17 +291,18 @@
             late_rows = jnp.pad(late_rows, ((0, 0), (0, half - kv_width)))
             tokens, late_rows = lax.optimization_barrier((tokens, late_rows))
         chosen = in_vmem(
-            functools.partial(choose_kernel, tick > 0),
+            choose_kernel if tick else first_choose_kernel,
             jax.ShapeDtypeStruct((2 * slots, half), jnp.bfloat16),
-            (tokens, moe_gain),
+            (tokens, moe_gain) if tick else (moe_gain,),
             8,
             tick=tick,
-            tables=(hits if tick else routes,),
+            tables=(hits,) if tick else (spans, own_ids),
         )
         if tick == 0:
-            held = (chosen, offsets, routes, owner_map, section_id == 0)
+            held = (chosen, offsets, own_ids, gate_vals, owner_map, section_id == 0)
             held = lax.optimization_barrier(held)
-            chosen, offsets, routes, owner_map, is_first = held
+            chosen, offsets, own_ids, gate_vals, owner_map, is_first = held
+            routes = jnp.concatenate([own_ids, by_tick(gate_vals[0])], axis=2)
             block_order = by_tick(owner_map[0])
             picks = early_picks(block_order, EARLY), late_picks(block_order)
             table = jax.ShapeDtypeStruct((n_sections, span_dev, 4 * slots), jnp.float32)
@@ -301,8 +315,9 @@
         if last_tick:
             arrived = jnp.concatenate([arrived, late_rows], axis=0)
         if tick == 0:
-            held = lax.optimization_barrier((arrived, turns, hits, weighs, picks))
-            arrived, turns, hits, weighs, picks = held
+            held = (arrived, turns, hits, weighs, picks, tokens)
+            held = lax.optimization_barrier(held)
+            arrived, turns, hits, weighs, picks, tokens = held
         token_rows = lax.all_gather(arrived, "y", axis=0, tiled=True)
         parts = in_vmem(
             lambda *refs: expert_kernel(n_columns, *refs),

time: 547 us -> 545 us (level)
    unnamed x49 -> x51, local copies, waits for them, and re-layouts: 13.5 us -> 14.6 us
where the time goes in v9:
time: 545 us; the launch traced here: 544 us
  blocking collectives  431 us (79%)
  Pallas kernels  28.9 us (5%)
  starting transfers between devices  22.4 us (4%)
  waiting for transfers between devices  22.2 us (4%)
  local copies, waits for them, and re-layouts  19.4 us (4%)
  between operations  14.7 us (3%)
    all_to_all x8, blocking collectives, body(): lax.all_to_all(parts, 'y', split_axis=0, concat_axis=0, tiled=True)  124 us
    all_gather x8, blocking collectives, body(): token_rows = lax.all_gather(arrived, 'y', axis=0, tiled=True)  115 us
    all_to_all x7, blocking collectives, body(): lax.all_to_all(chosen, 'z', split_axis=0, concat_axis=0, tiled=True)  100 us
    all_to_all x7, blocking collectives, body(): lax.all_to_all(summed, 'z', split_axis=0, concat_axis=0, tiled=True)  91.9 us
    pallas_call x35, Pallas kernels, in_vmem(): pl.pallas_call(kernel, grid=(1,), out_shape=out_shape, in_specs=specs, ou...  28.9 us
    unnamed x51, local copies, waits for them, and re-layouts  14.6 us
    all_to_all x1, waiting for transfers between devices, body(): lax.all_to_all(summed, 'z', split_axis=0, concat_axis=0, tiled=True)  11.3 us
  transfers between devices with their start and end apart: 11, of which 9 were waited for; matrix products, arithmetic and copies ran while one was open for 2% of the time, Pallas kernels for 2%

profile of v9, /device:TPU:8, one launch (start us, length us, event | category | flops | bytes accessed | tf_op | source)
XLA Modules:
  0.0 543.6 jit_solution(1832230231077875411)
XLA Ops:
  11.1 8.5 %all-to-all-start = ((bf16[8,8,1792]{2,1,0:T(8,128)(2,1)}), bf16[8,8,1792]{2,1,0:T(8,128)(2,1)S(1)}, u32[]{:S(2)}, u32[]{:S(2)}) async-start(bf16[8,8,1792]{2,1,0:T(8,128)(2,1)} %bitcast.8), calls=%async_computation | async-start | bytes 458752 | tf_op jit(solution)/shard_map/all_to_all | solution.py:314
  30.7 14.3 %all_gather.33.refs_0_ = bf16[256,1792]{1,0:T(8,128)(2,1)S(1)} all-gather(bf16[64,1792]{1,0:T(8,128)(2,1)S(1)} %bitcast.158), channel_id=1, replica_groups=mesh['section'=8,'z'=8,'y'=4] {'y'}, dimensions={0}, use_global_device_ids=true | all-gather | bytes 1146880 | tf_op jit(solution)/shard_map/all_gather | solution.py:321
  53.2 16.5 %all_to_all.271 = bf16[4,32,3584]{2,1,0:T(8,128)(2,1)S(1)} all-to-all(bf16[4,32,3584]{2,1,0:T(8,128)(2,1)S(1)} %bitcast.121), channel_id=1, replica_groups=mesh['section'=8,'z'=8,'y'=4] {'y'}, dimensions={0} | all-to-all | bytes 1835008 | tf_op jit(solution)/shard_map/all_to_all | solution.py:337
  70.1 14.8 %all_to_all.272 = bf16[8,8,1792]{2,1,0:T(8,128)(2,1)S(1)} all-to-all(bf16[8,8,1792]{2,1,0:T(8,128)(2,1)S(1)} %bitcast.149), channel_id=1, replica_groups=mesh['section'=8,'z'=8,'y'=4] {'z'}, dimensions={0} | all-to-all | bytes 458752 | tf_op jit(solution)/shard_map/all_to_all | solution.py:346
  87.7 14.0 %all_to_all.273 = bf16[8,8,1792]{2,1,0:T(8,128)(2,1)S(1)} all-to-all(bf16[8,8,1792]{2,1,0:T(8,128)(2,1)S(1)} %bitcast.143), channel_id=1, replica_groups=mesh['section'=8,'z'=8,'y'=4] {'z'}, dimensions={0} | all-to-all | bytes 458752 | tf_op jit(solution)/shard_map/all_to_all | solution.py:314
  101.6 14.6 %all_gather.34.refs_0_ = bf16[256,1792]{1,0:T(8,128)(2,1)S(1)} all-gather(bf16[64,1792]{1,0:T(8,128)(2,1)S(1)} %bitcast.159), channel_id=1, replica_groups=mesh['section'=8,'z'=8,'y'=4] {'y'}, dimensions={0}, use_global_device_ids=true | all-gather | bytes 1146880 | tf_op jit(solution)/shard_map/all_gather | solution.py:321
  118.2 16.3 %all_to_all.274 = bf16[4,32,3584]{2,1,0:T(8,128)(2,1)S(1)} all-to-all(bf16[4,32,3584]{2,1,0:T(8,128)(2,1)S(1)} %bitcast.120), channel_id=1, replica_groups=mesh['section'=8,'z'=8,'y'=4] {'y'}, dimensions={0} | all-to-all | bytes 1835008 | tf_op jit(solution)/shard_map/all_to_all | solution.py:337
  134.8 13.9 %all_to_all.275 = bf16[8,8,1792]{2,1,0:T(8,128)(2,1)S(1)} all-to-all(bf16[8,8,1792]{2,1,0:T(8,128)(2,1)S(1)} %bitcast.150), channel_id=1, replica_groups=mesh['section'=8,'z'=8,'y'=4] {'z'}, dimensions={0} | all-to-all | bytes 458752 | tf_op jit(solution)/shard_map/all_to_all | solution.py:346
  151.5 14.7 %all_to_all.276 = bf16[8,8,1792]{2,1,0:T(8,128)(2,1)S(1)} all-to-all(bf16[8,8,1792]{2,1,0:T(8,128)(2,1)S(1)} %bitcast.144), channel_id=1, replica_groups=mesh['section'=8,'z'=8,'y'=4] {'z'}, dimensions={0} | all-to-all | bytes 458752 | tf_op jit(solution)/shard_map/all_to_all | solution.py:314
  166.2 13.6 %all_gather.36.refs_0_ = bf16[256,1792]{1,0:T(8,128)(2,1)S(1)} all-gather(bf16[64,1792]{1,0:T(8,128)(2,1)S(1)} %bitcast.160), channel_id=1, replica_groups=mesh['section'=8,'z'=8,'y'=4] {'y'}, dimensions={0}, use_global_device_ids=true | all-gather | bytes 1146880 | tf_op jit(solution)/shard_map/all_gather | solution.py:321
  185.9 14.4 %all_to_all.277 = bf16[4,32,3584]{2,1,0:T(8,128)(2,1)S(1)} all-to-all(bf16[4,32,3584]{2,1,0:T(8,128)(2,1)S(1)} %bitcast.122), channel_id=1, replica_groups=mesh['section'=8,'z'=8,'y'=4] {'y'}, dimensions={0} | all-to-all | bytes 1835008 | tf_op jit(solution)/shard_map/all_to_all | solution.py:337
  200.6 12.5 %all_to_all.278 = bf16[8,8,1792]{2,1,0:T(8,128)(2,1)S(1)} all-to-all(bf16[8,8,1792]{2,1,0:T(8,128)(2,1)S(1)} %bitcast.151), channel_id=1, replica_groups=mesh['section'=8,'z'=8,'y'=4] {'z'}, dimensions={0} | all-to-all | bytes 458752 | tf_op jit(solution)/shard_map/all_to_all | solution.py:346
  215.9 13.2 %all_to_all.279 = bf16[8,8,1792]{2,1,0:T(8,128)(2,1)S(1)} all-to-all(bf16[8,8,1792]{2,1,0:T(8,128)(2,1)S(1)} %bitcast.145), channel_id=1, replica_groups=mesh['section'=8,'z'=8,'y'=4] {'z'}, dimensions={0} | all-to-all | bytes 458752 | tf_op jit(solution)/shard_map/all_to_all | solution.py:314
  229.2 14.4 %all_gather.37.refs_0_ = bf16[256,1792]{1,0:T(8,128)(2,1)S(1)} all-gather(bf16[64,1792]{1,0:T(8,128)(2,1)S(1)} %bitcast.161), channel_id=1, replica_groups=mesh['section'=8,'z'=8,'y'=4] {'y'}, dimensions={0}, use_global_device_ids=true | all-gather | bytes 1146880 | tf_op jit(solution)/shard_map/all_gather | solution.py:321
  245.5 17.2 %all_to_all.280 = bf16[4,32,3584]{2,1,0:T(8,128)(2,1)S(1)} all-to-all(bf16[4,32,3584]{2,1,0:T(8,128)(2,1)S(1)} %bitcast.123), channel_id=1, replica_groups=mesh['section'=8,'z'=8,'y'=4] {'y'}, dimensions={0} | all-to-all | bytes 1835008 | tf_op jit(solution)/shard_map/all_to_all | solution.py:337
  263.0 12.8 %all_to_all.281 = bf16[8,8,1792]{2,1,0:T(8,128)(2,1)S(1)} all-to-all(bf16[8,8,1792]{2,1,0:T(8,128)(2,1)S(1)} %bitcast.152), channel_id=1, replica_groups=mesh['section'=8,'z'=8,'y'=4] {'z'}, dimensions={0} | all-to-all | bytes 458752 | tf_op jit(solution)/shard_map/all_to_all | solution.py:346
  278.6 14.4 %all_to_all.282 = bf16[8,8,1792]{2,1,0:T(8,128)(2,1)S(1)} all-to-all(bf16[8,8,1792]{2,1,0:T(8,128)(2,1)S(1)} %bitcast.146), channel_id=1, replica_groups=mesh['section'=8,'z'=8,'y'=4] {'z'}, dimensions={0} | all-to-all | bytes 458752 | tf_op jit(solution)/shard_map/all_to_all | solution.py:314
  292.9 13.6 %all_gather.38.refs_0_ = bf16[256,1792]{1,0:T(8,128)(2,1)S(1)} all-gather(bf16[64,1792]{1,0:T(8,128)(2,1)S(1)} %bitcast.162), channel_id=1, replica_groups=mesh['section'=8,'z'=8,'y'=4] {'y'}, dimensions={0}, use_global_device_ids=true | all-gather | bytes 1146880 | tf_op jit(solution)/shard_map/all_gather | solution.py:321
  308.5 14.5 %all_to_all.283 = bf16[4,32,3584]{2,1,0:T(8,128)(2,1)S(1)} all-to-all(bf16[4,32,3584]{2,1,0:T(8,128)(2,1)S(1)} %bitcast.124), channel_id=1, replica_groups=mesh['section'=8,'z'=8,'y'=4] {'y'}, dimensions={0} | all-to-all | bytes 1835008 | tf_op jit(solution)/shard_map/all_to_all | solution.py:337
  323.2 12.5 %all_to_all.284 = bf16[8,8,1792]{2,1,0:T(8,128)(2,1)S(1)} all-to-all(bf16[8,8,1792]{2,1,0:T(8,128)(2,1)S(1)} %bitcast.153), channel_id=1, replica_groups=mesh['section'=8,'z'=8,'y'=4] {'z'}, dimensions={0} | all-to-all | bytes 458752 | tf_op jit(solution)/shard_map/all_to_all | solution.py:346
  338.6 14.4 %all_to_all.285 = bf16[8,8,1792]{2,1,0:T(8,128)(2,1)S(1)} all-to-all(bf16[8,8,1792]{2,1,0:T(8,128)(2,1)S(1)} %bitcast.147), channel_id=1, replica_groups=mesh['section'=8,'z'=8,'y'=4] {'z'}, dimensions={0} | all-to-all | bytes 458752 | tf_op jit(solution)/shard_map/all_to_all | solution.py:314
  352.9 13.6 %all_gather.39.refs_0_ = bf16[256,1792]{1,0:T(8,128)(2,1)S(1)} all-gather(bf16[64,1792]{1,0:T(8,128)(2,1)S(1)} %bitcast.163), channel_id=1, replica_groups=mesh['section'=8,'z'=8,'y'=4] {'y'}, dimensions={0}, use_global_device_ids=true | all-gather | bytes 1146880 | tf_op jit(solution)/shard_map/all_gather | solution.py:321
  368.5 14.4 %all_to_all.286 = bf16[4,32,3584]{2,1,0:T(8,128)(2,1)S(1)} all-to-all(bf16[4,32,3584]{2,1,0:T(8,128)(2,1)S(1)} %bitcast.125), channel_id=1, replica_groups=mesh['section'=8,'z'=8,'y'=4] {'y'}, dimensions={0} | all-to-all | bytes 1835008 | tf_op jit(solution)/shard_map/all_to_all | solution.py:337
  383.2 12.5 %all_to_all.287 = bf16[8,8,1792]{2,1,0:T(8,128)(2,1)S(1)} all-to-all(bf16[8,8,1792]{2,1,0:T(8,128)(2,1)S(1)} %bitcast.154), channel_id=1, replica_groups=mesh['section'=8,'z'=8,'y'=4] {'z'}, dimensions={0} | all-to-all | bytes 458752 | tf_op jit(solution)/shard_map/all_to_all | solution.py:346
  398.6 14.7 %all_to_all.288 = bf16[8,8,1792]{2,1,0:T(8,128)(2,1)S(1)} all-to-all(bf16[8,8,1792]{2,1,0:T(8,128)(2,1)S(1)} %bitcast.148), channel_id=1, replica_groups=mesh['section'=8,'z'=8,'y'=4] {'z'}, dimensions={0} | all-to-all | bytes 458752 | tf_op jit(solution)/shard_map/all_to_all | solution.py:314
  413.2 13.7 %all_gather.40.refs_0_ = bf16[256,1792]{1,0:T(8,128)(2,1)S(1)} all-gather(bf16[64,1792]{1,0:T(8,128)(2,1)S(1)} %bitcast.164), channel_id=1, replica_groups=mesh['section'=8,'z'=8,'y'=4] {'y'}, dimensions={0}, use_global_device_ids=true | all-gather | bytes 1146880 | tf_op jit(solution)/shard_map/all_gather | solution.py:321
  431.0 15.3 %all_to_all.289 = bf16[4,32,3584]{2,1,0:T(8,128)(2,1)S(1)} all-to-all(bf16[4,32,3584]{2,1,0:T(8,128)(2,1)S(1)} %bitcast.119), channel_id=1, replica_groups=mesh['section'=8,'z'=8,'y'=4] {'y'}, dimensions={0} | all-to-all | bytes 1835008 | tf_op jit(solution)/shard_map/all_to_all | solution.py:337
  446.7 12.8 %all_to_all.290 = bf16[8,8,1792]{2,1,0:T(8,128)(2,1)S(1)} all-to-all(bf16[8,8,1792]{2,1,0:T(8,128)(2,1)S(1)} %bitcast.155), channel_id=1, replica_groups=mesh['section'=8,'z'=8,'y'=4] {'z'}, dimensions={0} | all-to-all | bytes 458752 | tf_op jit(solution)/shard_map/all_to_all | solution.py:346
  465.7 14.9 %all_to_all.291 = bf16[8,8,1792]{2,1,0:T(8,128)(2,1)S(1)} all-to-all(bf16[8,8,1792]{2,1,0:T(8,128)(2,1)S(1)} %bitcast.142), channel_id=1, replica_groups=mesh['section'=8,'z'=8,'y'=4] {'z'}, dimensions={0} | all-to-all | bytes 458752 | tf_op jit(solution)/shard_map/all_to_all | solution.py:314
  480.6 16.8 %all_gather.41.refs_0_.rest_0_ = bf16[288,1792]{1,0:T(8,128)(2,1)S(1)} all-gather(bf16[72,1792]{1,0:T(8,128)(2,1)S(1)} %pad_maximum_fusion), channel_id=1, replica_groups=mesh['section'=8,'z'=8,'y'=4] {'y'}, dimensions={0}, use_global_device_ids=true | all-gather | bytes 1290240 | tf_op jit(solution)/shard_map/all_gather | solution.py:321
  499.6 15.6 %all_to_all.292 = bf16[4,32,3584]{2,1,0:T(8,128)(2,1)S(1)} all-to-all(bf16[4,32,3584]{2,1,0:T(8,128)(2,1)S(1)} %bitcast.126), channel_id=1, replica_groups=mesh['section'=8,'z'=8,'y'=4] {'y'}, dimensions={0} | all-to-all | bytes 1835008 | tf_op jit(solution)/shard_map/all_to_all | solution.py:337
  523.8 11.3 %all-to-all-done.23 = bf16[8,16,1792]{2,1,0:T(8,128)(2,1)S(1)} async-done(((bf16[8,16,1792]{2,1,0:T(8,128)(2,1)}), bf16[8,16,1792]{2,1,0:T(8,128)(2,1)S(1)}, u32[]{:S(2)}, u32[]{:S(2)}) %all-to-all-start.23) | async-done | bytes 458784 | tf_op jit(solution)/shard_map/all_to_all | solution.py:346
  (163 shorter events, 78.3 us)
Async XLA Ops:
  7.2 0.8 copy-start
  7.2 111.0 %all-gather.5.cloned.1.call-start = ((), (), s32[]{:S(2)}) async-start(), calls=%async_computation.24 | async-start | bytes 4730880 | tf_op jit(solution)/shard_map/all_gather | solution.py:234
  8.2 1.0 copy-start.14
  11.1 19.6 %all-to-all-start = ((bf16[8,8,1792]{2,1,0:T(8,128)(2,1)}), bf16[8,8,1792]{2,1,0:T(8,128)(2,1)S(1)}, u32[]{:S(2)}, u32[]{:S(2)}) async-start(bf16[8,8,1792]{2,1,0:T(8,128)(2,1)} %bitcast.8), calls=%async_computation | async-start | bytes 458752 | tf_op jit(solution)/shard_map/all_to_all | solution.py:314
  19.6 495.6 %all-gather.7.cloned.1.call-start = ((), (), s32[]{:S(2)}) async-start(), calls=%async_computation.25 | async-start | bytes 2365440 | tf_op jit(solution)/shard_map/all_gather | solution.py:336
  45.1 2.1 copy-start.1
  47.1 2.0 copy-start.5
  49.2 2.1 copy-start.9
  51.2 36.0 %copy-start.15 = (bf16[8,8,3584]{2,1,0:T(8,128)(2,1)S(1)}, bf16[8,8,3584]{2,1,0:T(8,128)(2,1)}, u32[]{:S(2)}) copy-start(bf16[8,8,3584]{2,1,0:T(8,128)(2,1)} %tokens.1) | copy-start | bytes 1376260
  51.2 65.0 %copy-start.6 = (bf16[1,3584,512]{2,1,0:T(8,128)(2,1)S(1)}, bf16[1,3584,512]{2,1,0:T(8,128)(2,1)}, u32[]{:S(2)}) copy-start(bf16[1,3584,512]{2,1,0:T(8,128)(2,1)} %param.23) | copy-start | bytes 11010052
  51.2 65.0 %copy-start.10 = (bf16[1,512,3584]{2,1,0:T(8,128)(2,1)S(1)}, bf16[1,512,3584]{2,1,0:T(8,128)(2,1)}, u32[]{:S(2)}) copy-start(bf16[1,512,3584]{2,1,0:T(8,128)(2,1)} %param.24) | copy-start | bytes 11010052
  53.2 34.1 %copy-start.17 = (f32[1,3584]{1,0:T(1,128)S(1)}, f32[1,3584]{1,0:T(1,128)}, u32[]{:S(2)}) copy-start(f32[1,3584]{1,0:T(1,128)} %gain.15) | copy-start | bytes 43012
  53.2 63.0 %copy-start.2 = (bf16[1,3584,512]{2,1,0:T(8,128)(2,1)S(1)}, bf16[1,3584,512]{2,1,0:T(8,128)(2,1)}, u32[]{:S(2)}) copy-start(bf16[1,3584,512]{2,1,0:T(8,128)(2,1)} %param.22) | copy-start | bytes 11010052
  85.1 2.2 collective-permute-start
  118.2 61.6 %copy-start.3 = (bf16[1,3584,512]{2,1,0:T(8,128)(2,1)S(1)}, bf16[1,3584,512]{2,1,0:T(8,128)(2,1)}, u32[]{:S(2)}) copy-start(bf16[1,3584,512]{2,1,0:T(8,128)(2,1)} %param.22) | copy-start | bytes 11010052
  148.9 2.2 collective-permute-start.1
  179.8 2.0 copy-start.7
  181.9 2.0 copy-start.11
  213.4 2.2 collective-permute-start.2
  276.0 2.2 collective-permute-start.3
  336.0 2.2 collective-permute-start.4
  396.0 2.2 collective-permute-start.5
  413.2 15.9 %slice-start = ((s8[4587520]{0:T(1024)(128)(4,1)}), s8[4194304]{0:T(1024)(128)(4,1)S(1)}, s32[]{:S(2)}) async-start(s8[4587520]{0:T(1024)(128)(4,1)} %bitcast.115), calls=%async_computation.26 | async-start | bytes 8388608
  427.0 2.1 slice-start.1
  427.0 2.1 copy-start.18
  427.0 2.1 copy-start.19
  431.0 66.4 %copy-start.12 = (bf16[1,512,3584]{2,1,0:T(8,128)(2,1)S(1)}, bf16[1,512,3584]{2,1,0:T(8,128)(2,1)}, u32[]{:S(2)}) copy-start(bf16[1,512,3584]{2,1,0:T(8,128)(2,1)} %param.24) | copy-start | bytes 11010052
  459.7 2.2 collective-permute-start.6
  461.9 35.5 %copy-start.8 = (bf16[1,3584,512]{2,1,0:T(8,128)(2,1)S(1)}, bf16[1,3584,512]{2,1,0:T(8,128)(2,1)}, u32[]{:S(2)}) copy-start(bf16[1,3584,512]{2,1,0:T(8,128)(2,1)} %param.23) | copy-start | bytes 11010052
  461.9 2.5 copy-start.13
  464.3 33.1 %copy-start.4 = (bf16[1,3584,512]{2,1,0:T(8,128)(2,1)S(1)}, bf16[1,3584,512]{2,1,0:T(8,128)(2,1)}, u32[]{:S(2)}) copy-start(bf16[1,3584,512]{2,1,0:T(8,128)(2,1)} %param.22) | copy-start | bytes 11010052
  516.7 18.4 %all-to-all-start.23 = ((bf16[8,16,1792]{2,1,0:T(8,128)(2,1)}), bf16[8,16,1792]{2,1,0:T(8,128)(2,1)S(1)}, u32[]{:S(2)}, u32[]{:S(2)}) async-start(bf16[8,16,1792]{2,1,0:T(8,128)(2,1)} %bitcast.64), calls=%async_computation.23 | async-start | bytes 917504 | tf_op jit(solution)/shard_map/all_to_all | solution.py:346
  (1 other events, 0.7 us)
Sparse Core Ops, SparseCore 0:
  10.6 89.8 all-gather.4
  431.1 72.2 all-gather.6
